TPU v7x, 32 devices: a whole 2x2x4 slice. The times are simulated.
32 devices in a mesh: groups: 1, ctx: 16 (over z, y, x), head: 1, pair: 2 (over core).
Axes of the slice: x: 2, y: 2, z: 4, core: 2. Of those that a mesh axis runs over, the one named last changes fastest.
Arguments:
- queries: bfloat16 [8192, 3584], P(('groups', 'ctx', 'pair'), 'head'), may hold values from -80 to 80
- key_state_rows: bfloat16 [8192, 512], P(('groups', 'ctx', 'pair'), 'head'), may hold values from -8 to 8
- wanted: int32 [32, 31], P('groups'), may hold values from 0 to 127, as said below
- selected: int32 [128, 28, 16], P(('groups', 'ctx', 'pair'), 'head'), may hold values from 0 to 38, all different within a row
- w_query: bfloat16 [128, 128], replicated, may hold values from -0.5 to 0.5
- key_gate_weight: bfloat16 [384, 128], replicated, may hold values from -0.3125 to 0.3125
Outputs:
- distill_kl: float32 [128, 28], P(('groups', 'ctx', 'pair'), 'head')
Inputs may be any that keep to these rules, and one draw needn't show every extreme that they name: `wanted`: row i names 31 different storage blocks, none held by storage spans i and i xor 1; they lie in 30 different spans, one span named twice, so that at most 2 come from any one span. `selected`: each query block and head lists 16 different candidate places.
All inputs are finite; a program needn't handle non-finite values.
Results may differ from a plain program's by a relative error of at most 0.00078.
Values may be sent and summed in bfloat16 or wider, within the bound.
No kernel may reach another device: no remote copies, remote signals or barrier semaphores. Data moves between devices by JAX's collectives and lax.ppermute only.
A program may use at most 64 MiB of HBM per device.

v0:
```python
import math

import jax
import jax.numpy as jnp
from jax import lax
from jax.sharding import PartitionSpec as P

BLOCK_TOKENS = 64
CAP = 2


def swapped(shard, axis, distance):
    return lax.ppermute(shard, axis, [(i, i ^ 1 << distance) for i in range(lax.axis_size(axis))])


def teacher_share(q_rows, candidate_keys, member, n_query, n_cand, query_group_width):
    score_scale = 1.0 / math.sqrt(q_rows.shape[2])

    def per_head(head_idx):
        q_head = lax.dynamic_index_in_dim(q_rows, head_idx, 1, keepdims=False)
        k_head = lax.dynamic_index_in_dim(
            candidate_keys, head_idx // query_group_width, 1, keepdims=False
        )
        chosen = lax.dynamic_index_in_dim(member, head_idx, 1, keepdims=False)
        scores = (
            lax.dot_general(
                q_head, k_head, (((1,), (1,)), ((), ())), preferred_element_type=jnp.float32
            )
            * score_scale
        )
        scores = scores.reshape(n_query, BLOCK_TOKENS, n_cand, BLOCK_TOKENS)
        allowed = jnp.broadcast_to(chosen[:, None, :, None], scores.shape)
        row_max = jnp.max(jnp.where(allowed, scores, -jnp.inf), axis=(2, 3), keepdims=True)
        weights = jnp.where(allowed, jnp.exp(scores - row_max), 0.0)
        row_total = jnp.sum(weights, axis=(2, 3), keepdims=True)
        block_share = jnp.sum(weights / row_total, axis=3)
        return jnp.mean(block_share, axis=1)

    result = lax.map(per_head, jnp.arange(q_rows.shape[1], dtype=jnp.int32))
    return jnp.transpose(result, (1, 0, 2))


def pooling_keys(block_keys):
    key_max = jnp.max(block_keys, axis=1)
    key_min = jnp.min(block_keys, axis=1)
    key_mean = (jnp.sum(block_keys, axis=1, dtype=jnp.float32) / BLOCK_TOKENS).astype(jnp.bfloat16)
    return jnp.concatenate([key_max, key_min, key_mean], axis=-1)


def key_projector(pooled, key_gate_weight):
    flat = pooled.reshape(-1, pooled.shape[-1])
    gate = jnp.dot(flat, key_gate_weight, preferred_element_type=jnp.float32).astype(jnp.bfloat16)
    return gate.reshape(pooled.shape[0], pooled.shape[1], key_gate_weight.shape[1])


def divergence(logits, teacher, candidate_index):
    row_max = jnp.max(logits, axis=2, keepdims=True)
    row_total = jnp.sum(jnp.exp(logits - row_max), axis=2, keepdims=True)
    log_gate = logits - row_max - jnp.log(row_total)
    picked = jnp.take(log_gate, candidate_index, axis=2)
    positive = teacher > 0
    safe_share = jnp.where(positive, teacher, 1.0)
    return jnp.sum(jnp.where(positive, teacher * (jnp.log(safe_share) - picked), 0.0), axis=2)


def outgoing_blocks(wanted, local_blocks, self_index, span_count):
    holder = wanted // span_count
    spot_ids = wanted % span_count
    is_asked = holder == self_index
    asked_rank = jnp.cumsum(is_asked.astype(jnp.int32), axis=1) - 1
    slot_list = []
    for slot_idx in range(CAP):
        hit_mask = is_asked & (asked_rank == slot_idx)
        present = jnp.any(hit_mask, axis=1)
        which_block = jnp.sum(jnp.where(hit_mask, spot_ids, 0), axis=1)
        slot_list.append(jnp.where(present[:, None, None], local_blocks[which_block], 0))
    return jnp.stack(slot_list, axis=1)


def per_device(queries, key_state_rows, wanted, selected, w_query, key_gate_weight):
    self_index = lax.axis_size("pair") * lax.axis_index("ctx") + lax.axis_index("pair")
    span_rows, key_width = key_state_rows.shape
    head_width = w_query.shape[0]
    gate_dim = w_query.shape[1]
    span_count = span_rows // BLOCK_TOKENS
    q_heads = queries.shape[1] // head_width
    kv_heads = key_width // head_width
    query_group_width = q_heads // kv_heads
    local_ids = jnp.arange(span_count, dtype=jnp.int32)
    local_blocks = key_state_rows.reshape(span_count, BLOCK_TOKENS, key_width)
    twin_blocks = swapped(key_state_rows, "pair", 0).reshape(span_count, BLOCK_TOKENS, key_width)
    my_wants = lax.dynamic_index_in_dim(wanted, self_index, 0, keepdims=False)
    my_holder = my_wants // span_count
    outgoing = outgoing_blocks(wanted, local_blocks, self_index, span_count)
    incoming = lax.all_to_all(outgoing, ("ctx", "pair"), split_axis=0, concat_axis=0, tiled=True)
    req_range = jnp.arange(my_wants.shape[0], dtype=jnp.int32)
    earlier = (my_holder[None, :] == my_holder[:, None]) & (req_range[None, :] < req_range[:, None])
    my_rank = jnp.sum(earlier.astype(jnp.int32), axis=1)
    fetched = incoming[my_holder, my_rank]
    own_ids = self_index * span_count + local_ids
    twin_ids = jnp.bitwise_xor(self_index, 1) * span_count + local_ids
    candidate_index = jnp.concatenate([own_ids, twin_ids, my_wants])
    n_cand = candidate_index.shape[0]
    candidate_keys = jnp.concatenate([local_blocks, twin_blocks, fetched], axis=0).reshape(
        n_cand * BLOCK_TOKENS, kv_heads, head_width
    )
    cand_range = jnp.arange(n_cand, dtype=jnp.int32)
    member = jnp.any(selected[..., None] == cand_range, axis=2)
    member = member | (cand_range[None, None, :] == local_ids[:, None, None])
    q_rows = queries.reshape(span_rows, q_heads, head_width)
    teacher = teacher_share(q_rows, candidate_keys, member, span_count, n_cand, query_group_width)
    pooled = pooling_keys(local_blocks.reshape(span_count, BLOCK_TOKENS, kv_heads, head_width))
    key_gate_rows = key_projector(
        lax.all_gather(pooled, ("ctx", "pair"), axis=0, tiled=True), key_gate_weight
    )
    q_pool = (
        jnp.sum(
            q_rows.reshape(span_count, BLOCK_TOKENS, q_heads, head_width), axis=1, dtype=jnp.float32
        )
        / BLOCK_TOKENS
    ).astype(jnp.bfloat16)
    query_gate_rows = jnp.dot(
        q_pool.reshape(-1, head_width), w_query, preferred_element_type=jnp.float32
    ).astype(jnp.bfloat16)
    query_gate_rows = query_gate_rows.reshape(span_count, kv_heads, query_group_width, gate_dim)
    logits = jnp.einsum(
        "bkgd,jkd->bkgj", query_gate_rows, key_gate_rows, preferred_element_type=jnp.float32
    ) * (1.0 / math.sqrt(gate_dim))
    gathered_blocks = key_gate_rows.shape[0]
    logits = logits.reshape(span_count, q_heads, gathered_blocks)
    return divergence(logits, teacher, candidate_index)


def solution(mesh):
    return jax.shard_map(
        per_device,
        mesh=mesh,
        in_specs=(
            P(("groups", "ctx", "pair"), "head"),
            P(("groups", "ctx", "pair"), "head"),
            P("groups", None),
            P(("groups", "ctx", "pair"), "head", None),
            P(),
            P(),
        ),
        out_specs=P(("groups", "ctx", "pair"), "head"),
        check_vma=False,
    )
```

profile of v0, /device:TPU:17, one launch (start us, length us, event | category | flops | bytes accessed | tf_op | source)
XLA Modules:
  0.0 713.3 jit_solution(983013035070205913)
XLA Ops:
  9.9 6.3 all-to-all-start
  17.2 118.6 %all_gather.3 = bf16[128,4,384]{2,1,0:T(4,128)(2,1)S(1)} all-gather(bf16[4,4,384]{2,1,0:T(4,128)(2,1)S(1)} %pad_maximum_fusion.2), channel_id=1, replica_groups=mesh['groups'=1,'ctx'=16,'head'=1,'pair'=2] {'ctx','pair'}, dimensions={0}, use_global_device_ids=true | all-gather | bytes 405504 | tf_op jit(solution)/shard_map/all_gather | solution.py:114
  158.6 552.6 %while.12 = (s32[]{:T(128)}, f32[28,4,39]{1,2,0:T(8,128)}, s32[28]{0:T(128)S(1)}, pred[4,28,39]{2,1,0:T(8,128)(4,1)S(1)}, bf16[256,28,128]{0,2,1:T(8,128)(2,1)},...) while((s32[]{:T(128)}, f32[28,4,39]{1,2,0:T(8,128)}, ...), condition=%wide.region_11.12_spmd, body=%wide.region_7.11_spmd.sunk | while | flops 169967120 | bytes 16711591 | solution.py:39
  172.5 5.2 fusion.41
  192.2 5.2 fusion.41
  212.0 5.2 fusion.41
  231.7 5.2 fusion.41
  251.5 5.2 fusion.41
  271.2 5.2 fusion.41
  291.0 5.2 fusion.41
  310.7 5.2 fusion.41
  330.4 5.2 fusion.41
  369.9 5.2 fusion.41
  409.4 5.2 fusion.41
  429.1 5.2 fusion.41
  468.6 5.2 fusion.41
  488.3 5.2 fusion.41
  527.8 5.2 fusion.41
  547.5 5.2 fusion.41
  606.7 5.2 fusion.41
  626.5 5.2 fusion.41
  665.9 5.2 fusion.41
  685.7 5.2 fusion.41
  705.4 5.2 fusion.41
  (388 shorter events, 373.1 us)
Async XLA Ops:
  0.0 141.2 %copy-start = (bf16[384,128]{1,0:T(8,128)(2,1)S(1)}, bf16[384,128]{1,0:T(8,128)(2,1)}, u32[]{:S(2)}) copy-start(bf16[384,128]{1,0:T(8,128)(2,1)} %param.13) | copy-start | bytes 294916
  0.0 3.6 copy-start.1
  9.9 6.8 copy-start.3
  9.9 136.9 %all-to-all-start = ((bf16[32,2,64,512]{3,2,1,0:T(8,128)(2,1)}), bf16[32,2,64,512]{3,2,1,0:T(8,128)(2,1)}, u32[]{:S(2)}, u32[]{:S(2)}) async-start(bf16[32,2,64,512]{3,2,1,0:T(8,128)(2,1)} %pad_maximum_fusion), calls=%async_computation | async-start | bytes 8388608 | tf_op jit(solution)/shard_map/all_to_all | solution.py:95
  16.3 119.7 %copy-start.2 = (bf16[256,3584]{1,0:T(8,128)(2,1)S(1)}, bf16[256,3584]{1,0:T(8,128)(2,1)}, u32[]{:S(2)}) copy-start(bf16[256,3584]{1,0:T(8,128)(2,1)} %param.8) | copy-start | bytes 5505028
  16.3 134.8 %collective-permute-start = (bf16[256,512]{1,0:T(8,128)(2,1)S(1)}, bf16[256,512]{1,0:T(8,128)(2,1)S(1)}, u32[]{:S(2)}, u32[]{:S(2)}) collective-permute-start(bf16[256,512]{1,0:T(8,128)(2,1)S(1)} %copy-done.1), channel_id=1, source_target_pairs={{0,1},{1,0},{2,3},{3,2},{4,5},{5,4},{6,7},{7,6},{8,9},{9,8},{10,11... | collective-permute-start | bytes 786440 | tf_op jit(solution)/shard_map/ppermute | solution.py:13
  138.4 2.6 copy-start.4
where the time goes:
time: 717 us; the launch traced here: 713 us
  local copies, waits for them, and re-layouts  238 us (33%)
  other arithmetic  196 us (27%)
  blocking collectives  119 us (17%)
  loops' own time  106 us (15%)
  matrix products  47.9 us (7%)
    reduce_sum x28, other arithmetic, per_head(): return jnp.mean(block_share, axis=1)  145 us
    all_gather x1, blocking collectives, per_device(): lax.all_gather(pooled, ('ctx', 'pair'), axis=0, tiled=True)  119 us
    reshape x28, local copies, waits for them, and re-layouts, per_head(): scores = scores.reshape(n_query, BLOCK_TOKENS, n_cand, BLOCK_TOKENS)  107 us
    another operation x1, loops' own time, teacher_share(): result = lax.map(per_head, jnp.arange(q_rows.shape[1], dtype=jnp.int32))  106 us
    broadcast_in_dim x56, local copies, waits for them, and re-layouts, per_head(): allowed = jnp.broadcast_to(chosen[:, None, :, None], scores.shape)  82.8 us
    dot_general x28, matrix products, per_head(): lax.dot_general(q_head, k_head, (((1,), (1,)), ((), ())), preferred_eleme...  47.2 us
    reduce_sum x28, other arithmetic, per_head(): row_total = jnp.sum(weights, axis=(2, 3), keepdims=True)  20.7 us
    dynamic_slice x28, local copies, waits for them, and re-layouts, teacher_share(): result = lax.map(per_head, jnp.arange(q_rows.shape[1], dtype=jnp.int32))  17.8 us
  transfers between devices with their start and end apart: 2, of which 0 were waited for; matrix products, arithmetic and copies ran while one was open for 2% of the time, Pallas kernels for 0%

commit v1 on v0

v1 whole, which is shorter than its diff:
```python
import functools
import math

import jax
import jax.numpy as jnp
from jax import lax
from jax.experimental import pallas as pl
from jax.experimental.pallas import tpu as pltpu
from jax.sharding import PartitionSpec as P

BLOCK = 64
LANES = 128
SEL_ROWS = 16
NEG = -1e37


def gate_kernel(dims, *refs):
    n_piece, n_key, heads, n_sel, n_cand, blocks, head_size = dims
    sel_s, cand_s, dup_s = refs[:3]
    q_in = refs[3 : 3 + n_piece]
    k_in = refs[3 + n_piece : 3 + n_piece + n_key]
    wq_ref, wk_ref, out_ref = refs[3 + n_piece + n_key : 6 + n_piece + n_key]
    qbuf, kbuf, pool, qpool, teach, ms, ss, lv, sem_q, sem_k = refs[6 + n_piece + n_key :]
    span = q_in[0].shape[0]
    span_blocks = span // BLOCK
    n_slot = n_sel + 1
    rows = n_piece * heads * span_blocks
    exp_scale = math.log2(math.e) / math.sqrt(head_size)

    q_copies = [
        pltpu.make_async_copy(q_in[i], qbuf.at[pl.ds(i * span, span)], sem_q.at[i]) for i in range(n_piece)
    ]
    k_rows = k_in[0].shape[0]
    k_copies = [
        pltpu.make_async_copy(k_in[i], kbuf.at[pl.ds(i * k_rows, k_rows)], sem_k.at[i]) for i in range(n_key)
    ]
    for copy in k_copies + q_copies:
        copy.start()
    ms[...] = jnp.full(ms.shape, NEG, jnp.float32)
    ss[...] = jnp.zeros(ss.shape, jnp.float32)
    lv[...] = jnp.full(lv.shape, -1, jnp.int32)
    for copy in k_copies + q_copies:
        copy.wait()

    def pool_step(i, carry):
        first = pl.multiple_of(i * 8 * BLOCK, 8 * BLOCK)
        keys = kbuf[pl.ds(first, 8 * BLOCK), :].astype(jnp.float32).reshape(8, BLOCK, head_size)
        at = pl.ds(pl.multiple_of(i * 8, 8), 8)
        pool[at, 0:head_size] = jnp.max(keys, axis=1)
        pool[at, head_size : 2 * head_size] = jnp.min(keys, axis=1)
        pool[at, 2 * head_size :] = jnp.sum(keys, axis=1) * (1.0 / BLOCK)
        return carry

    lax.fori_loop(0, blocks // 8, pool_step, 0)

    lane = lax.broadcasted_iota(jnp.int32, (1, LANES), 1)
    low = lane < BLOCK
    zeros = jnp.zeros((BLOCK, head_size), jnp.bfloat16)

    def pair_step(ph, t, u):
        piece = ph // heads
        head = ph - piece * heads
        q_at = pl.ds(pl.multiple_of(piece * span + t * 2 * BLOCK, 2 * BLOCK), 2 * BLOCK)
        q = qbuf[q_at, pl.ds(pl.multiple_of(head * head_size, head_size), head_size)]
        q0, q1 = q[:BLOCK], q[BLOCK:]
        row = ph * span_blocks + 2 * t
        means = [jnp.sum(x.astype(jnp.float32), axis=0, keepdims=True) * (1.0 / BLOCK) for x in (q0, q1)]
        qpool[pl.ds(row, 1), :] = means[0]
        qpool[pl.ds(row + 1, 1), :] = means[1]
        rhs = jnp.concatenate(
            [jnp.concatenate([q0, zeros], axis=1), jnp.concatenate([zeros, q1], axis=1)], axis=0
        )
        tiles = []
        for slot in range(n_slot):
            halves = []
            for half in range(2):
                if slot < n_sel:
                    place = sel_s[(row + half) * n_sel + slot]
                else:
                    place = 2 * t + half
                at = cand_s[piece * n_cand + place]
                lv[u, half, slot : slot + 1, :] = jnp.full((1, LANES), at, jnp.int32)
                halves.append(kbuf[pl.ds(pl.multiple_of(at * BLOCK, BLOCK), BLOCK), :])
            tiles.append(jnp.concatenate(halves, axis=1))
        scores = lax.dot_general(
            jnp.concatenate(tiles, axis=0),
            rhs,
            (((1,), (1,)), ((), ())),
            preferred_element_type=jnp.float32,
        )
        for slot in range(n_slot):
            part = scores[slot * BLOCK : (slot + 1) * BLOCK]
            top = jnp.max(part, axis=0, keepdims=True)
            total = jnp.sum(jnp.exp2((part - top) * exp_scale), axis=0, keepdims=True)
            if slot == n_sel:
                keep = jnp.where(low, 1 - dup_s[row], 1 - dup_s[row + 1])
                total = total * keep.astype(jnp.float32)
            ms[u, slot : slot + 1, :] = top
            ss[u, slot : slot + 1, :] = total
        tops = ms[u]
        weight = jnp.exp2((tops - jnp.max(tops, axis=0, keepdims=True)) * exp_scale) * ss[u]
        share = weight / jnp.sum(weight, axis=0, keepdims=True)
        for half in range(2):
            mine = low if half == 0 else jnp.logical_not(low)
            mean = jnp.sum(jnp.where(mine, share, 0.0), axis=1, keepdims=True) * (1.0 / BLOCK)
            for c in range(blocks // LANES):
                hit = lv[u, half] == lane + c * LANES
                teach[c, pl.ds(row + half, 1), :] = jnp.sum(
                    jnp.where(hit, mean, 0.0), axis=0, keepdims=True
                )

    def head_step(ph, carry):
        for t in range(span_blocks // 2):
            pair_step(ph, t, t)
        return carry

    lax.fori_loop(0, n_piece * heads, head_step, 0)

    k_gate = jnp.dot(
        pool[...].astype(jnp.bfloat16), wk_ref[...], preferred_element_type=jnp.float32
    ).astype(jnp.bfloat16)
    q_gate = jnp.dot(
        qpool[...].astype(jnp.bfloat16), wq_ref[...], preferred_element_type=jnp.float32
    ).astype(jnp.bfloat16)
    logits = lax.dot_general(
        q_gate, k_gate, (((1,), (1,)), ((), ())), preferred_element_type=jnp.float32
    ) * (1.0 / math.sqrt(wq_ref.shape[1]))
    top = jnp.max(logits, axis=1, keepdims=True)
    log_gate = logits - top - jnp.log(jnp.sum(jnp.exp(logits - top), axis=1, keepdims=True))
    teacher = jnp.concatenate([teach[c] for c in range(blocks // LANES)], axis=1)
    positive = teacher > 0
    safe = jnp.where(positive, teacher, 1.0)
    out_ref[...] = jnp.sum(
        jnp.where(positive, teacher * (jnp.log(safe) - log_gate), 0.0), axis=1, keepdims=True
    )


def gate_call(sel, cand, dup, q_pieces, k_pieces, w_query, key_gate_weight, heads, n_sel, n_cand):
    head_size = w_query.shape[0]
    span = q_pieces[0].shape[0]
    k_rows = k_pieces[0].shape[0]
    blocks = len(k_pieces) * k_rows // BLOCK
    rows = len(q_pieces) * heads * (span // BLOCK)
    dims = (len(q_pieces), len(k_pieces), heads, n_sel, n_cand, blocks, head_size)
    unroll = span // BLOCK // 2
    slots = -(-(n_sel + 1) // 8) * 8
    smem = pl.BlockSpec(memory_space=pltpu.SMEM)
    hbm = pl.BlockSpec(memory_space=pl.ANY)
    vmem = pl.BlockSpec(memory_space=pltpu.VMEM)
    return pl.pallas_call(
        functools.partial(gate_kernel, dims),
        out_shape=jax.ShapeDtypeStruct((rows, 1), jnp.float32),
        in_specs=[smem] * 3 + [hbm] * (len(q_pieces) + len(k_pieces)) + [vmem] * 2,
        out_specs=vmem,
        scratch_shapes=[
            pltpu.VMEM((len(q_pieces) * span, heads * head_size), jnp.bfloat16),
            pltpu.VMEM((blocks * BLOCK, head_size), jnp.bfloat16),
            pltpu.VMEM((blocks, 3 * head_size), jnp.float32),
            pltpu.VMEM((rows, head_size), jnp.float32),
            pltpu.VMEM((blocks // LANES, rows, LANES), jnp.float32),
            pltpu.VMEM((unroll, slots, LANES), jnp.float32),
            pltpu.VMEM((unroll, slots, LANES), jnp.float32),
            pltpu.VMEM((unroll, 2, slots, LANES), jnp.int32),
            pltpu.SemaphoreType.DMA((len(q_pieces),)),
            pltpu.SemaphoreType.DMA((len(k_pieces),)),
        ],
        compiler_params=pltpu.CompilerParams(vmem_limit_bytes=40 * 1024 * 1024),
    )(sel, cand, dup, *q_pieces, *k_pieces, w_query, key_gate_weight)


def per_device(queries, key_state_rows, wanted, selected, w_query, key_gate_weight):
    n_ctx, n_pair = lax.axis_size("ctx"), lax.axis_size("pair")
    ctx, core = lax.axis_index("ctx"), lax.axis_index("pair")
    head_size = w_query.shape[0]
    span, key_width = key_state_rows.shape
    span_blocks = span // BLOCK
    q_heads = queries.shape[1] // head_size
    kv_heads = key_width // head_size
    heads = q_heads // kv_heads
    n_sel = selected.shape[2]
    plane = kv_heads if kv_heads in (1, 2, 4) and n_ctx % kv_heads == 0 and n_pair == 2 else 1
    layers = n_ctx // plane
    ring = plane > 1 and layers <= 4
    spot = ctx % plane
    layer = ctx // plane

    def place_of(block):
        if not ring:
            return block
        span_id = block // span_blocks
        other_ctx = span_id // n_pair
        step = (layer - other_ctx // plane) % layers
        which = (other_ctx % plane) ^ spot
        side = (span_id % n_pair) ^ core
        return ((side * layers + step) * plane + which) * span_blocks + block % span_blocks

    local_ids = jnp.arange(span_blocks, dtype=jnp.int32)
    candidates = []
    for p in range(plane if ring else 1):
        other_span = (ctx ^ p) * n_pair + core
        wants = lax.dynamic_index_in_dim(wanted, other_span, 0, keepdims=False)
        candidates.append(
            jnp.concatenate(
                [other_span * span_blocks + local_ids, (other_span ^ 1) * span_blocks + local_ids, wants]
            )
        )
    n_cand = candidates[0].shape[0]
    cand = place_of(jnp.stack(candidates)).astype(jnp.int32).reshape(-1)

    def lists(sel):
        sel = jnp.transpose(sel, (0, 2, 1, 3))
        dup = jnp.any(sel == local_ids[None, None, :, None], axis=3).astype(jnp.int32)
        return sel.reshape(-1), dup.reshape(-1)

    if not ring:
        gathered = lax.all_gather(key_state_rows, ("ctx", "pair"), axis=0, tiled=True)
        outs = []
        for g in range(kv_heads):
            sel, dup = lists(selected[None, :, g * heads : (g + 1) * heads])
            out = gate_call(
                sel, cand, dup,
                [queries[:, g * heads * head_size : (g + 1) * heads * head_size]],
                [gathered[:, g * head_size : (g + 1) * head_size]],
                w_query, key_gate_weight, heads, n_sel, n_cand,
            )
            outs.append(jnp.transpose(out.reshape(heads, span_blocks)))
        return jnp.concatenate(outs, axis=1)

    def flipped(x, p):
        return x if p == 0 else lax.ppermute(x, "ctx", [(i, i ^ p) for i in range(n_ctx)])

    def other_core(x):
        return lax.ppermute(x, "pair", [(0, 1), (1, 0)])

    keys = [
        flipped(lax.dynamic_slice_in_dim(key_state_rows, (spot ^ p) * head_size, head_size, 1), p)
        for p in range(plane)
    ]
    steps = [jnp.concatenate(keys, axis=0)]
    sel_rows = jnp.pad(
        selected.astype(jnp.bfloat16),
        ((0, SEL_ROWS - span_blocks), (0, 0), (0, head_size - n_sel)),
    ).reshape(SEL_ROWS, q_heads * head_size)
    sent = jnp.concatenate([queries, sel_rows], axis=0)
    width = heads * head_size
    pieces = [
        flipped(lax.dynamic_slice_in_dim(sent, (spot ^ p) * width, width, 1), p) for p in range(plane)
    ]
    for _ in range(layers - 1):
        steps.append(
            lax.ppermute(steps[-1], "ctx", [(i, (i + plane) % n_ctx) for i in range(n_ctx)])
        )
    k_pieces = steps + [other_core(x) for x in steps]
    sel = jnp.stack([x[span : span + span_blocks] for x in pieces])
    sel = sel.reshape(plane, span_blocks, heads, head_size)[..., :n_sel].astype(jnp.int32)
    sel, dup = lists(sel)
    q_pieces = [x[:span] for x in pieces]
    out = gate_call(sel, cand, dup, q_pieces, k_pieces, w_query, key_gate_weight, heads, n_sel, n_cand)
    out = out.reshape(plane, heads, span_blocks)
    back = jnp.stack([flipped(out[p], p) for p in range(plane)])
    order = jnp.arange(plane, dtype=jnp.int32) ^ spot
    back = jnp.transpose(back[order], (2, 0, 1))
    return back.reshape(span_blocks, q_heads)


def solution(mesh):
    return jax.shard_map(
        per_device,
        mesh=mesh,
        in_specs=(
            P(("groups", "ctx", "pair"), "head"),
            P(("groups", "ctx", "pair"), "head"),
            P("groups", None),
            P(("groups", "ctx", "pair"), "head", None),
            P(),
            P(),
        ),
        out_specs=P(("groups", "ctx", "pair"), "head"),
        check_vma=False,
    )
```

time: 717 us -> 97.5 us (0.14)
  the two profiles are of different devices: /device:TPU:17 before, /device:TPU:0 now
where the time goes in v1:
time: 97.5 us; the launch traced here: 96.9 us
  waiting for transfers between devices  46.3 us (47%)
  Pallas kernels  20.8 us (21%)
  starting transfers between devices  15.7 us (16%)
  local copies, waits for them, and re-layouts  13.2 us (14%)
    ppermute x3, waiting for transfers between devices, per_device(): lax.ppermute(steps[-1], 'ctx', [(i, (i + plane) % n_ctx) for i in range(n...  25.1 us
    ppermute x9, waiting for transfers between devices, flipped(): lax.ppermute(x, 'ctx', [(i, i ^ p) for i in range(n_ctx)])  21.2 us
    pallas_call x1, Pallas kernels, gate_call(): pl.pallas_call(functools.partial(gate_kernel, dims), out_shape=jax.ShapeD...  20.8 us
    ppermute x9, starting transfers between devices, flipped(): lax.ppermute(x, 'ctx', [(i, i ^ p) for i in range(n_ctx)])  13.2 us
    slice x4, local copies, waits for them, and re-layouts, per_device(): q_pieces = [x[:span] for x in pieces]  4.27 us
    slice x4, local copies, waits for them, and re-layouts, per_device(): sel = jnp.stack([x[span:span + span_blocks] for x in pieces])  2.88 us
  transfers between devices with their start and end apart: 16, of which 7 were waited for; matrix products, arithmetic and copies ran while one was open for 10% of the time, Pallas kernels for 0%

profile of v1, /device:TPU:0, one launch (start us, length us, event | category | flops | bytes accessed | tf_op | source)
XLA Modules:
  0.0 96.9 jit_solution(6122234795547368352)
XLA Ops:
  0.0 1.6 %constant_dynamic-update-slice_fusion = bf16[272,3584]{1,0:T(8,128)(2,1)S(1)} fusion(bf16[256,3584]{1,0:T(8,128)(2,1)} %param.6), kind=kLoop, calls=%fused_computation.15 | loop fusion | bytes 3670016
  1.9 1.0 %constant_dynamic-slice_fusion.10 = (bf16[272,896]{1,0:T(8,128)(2,1)S(1)}, bf16[272,896]{1,0:T(8,128)(2,1)}, bf16[272,896]{1,0:T(8,128)(2,1)S(1)}) fusion(bf16[272,3584]{1,0:T(8,128)(2,1)S(1)} %bitcast_dynamic-update-slice_fusion, s32[]{:T(128)S(6)} %select_n.96, s32[]{:T(128)S(6)} %select_n.98, s32[]{:T(128)S(6)} %select_n.97), kind=kLoop, calls=%fused_computation.26 | loop fusion | bytes 2924556 | tf_op jit(solution)/shard_map/dynamic_slice | solution.py:247
  2.9 3.9 %collective-permute-start.2 = (bf16[272,896]{1,0:T(8,128)(2,1)}, bf16[272,896]{1,0:T(8,128)(2,1)}, u32[]{:S(2)}, u32[]{:S(2)}) collective-permute-start(bf16[272,896]{1,0:T(8,128)(2,1)} %get-tuple-element.10), channel_id=1, source_target_pairs={{0,6},{2,4},{4,2},{6,0},{8,14},{10,12},{12,10},{14,8},{16,22},{18,... | collective-permute-start | bytes 1462280 | tf_op jit(solution)/shard_map/ppermute | solution.py:230
  7.4 1.6 %collective-permute-start.5 = (bf16[256,128]{1,0:T(8,128)(2,1)S(1)}, bf16[256,128]{1,0:T(8,128)(2,1)S(1)}, u32[]{:S(2)}, u32[]{:S(2)}) collective-permute-start(bf16[256,128]{1,0:T(8,128)(2,1)S(1)} %get-tuple-element.14), channel_id=1, source_target_pairs={{0,6},{2,4},{4,2},{6,0},{8,14},{10,12},{12,10},{14,8},{16,22},{18,... | collective-permute-start | bytes 196616 | tf_op jit(solution)/shard_map/ppermute | solution.py:230
  9.0 1.9 %collective-permute-start.3 = (bf16[256,128]{1,0:T(8,128)(2,1)S(1)}, bf16[256,128]{1,0:T(8,128)(2,1)S(1)}, u32[]{:S(2)}, u32[]{:S(2)}) collective-permute-start(bf16[256,128]{1,0:T(8,128)(2,1)S(1)} %get-tuple-element.13), channel_id=1, source_target_pairs={{0,2},{2,0},{4,6},{6,4},{8,10},{10,8},{12,14},{14,12},{16,18},{18,... | collective-permute-start | bytes 196616 | tf_op jit(solution)/shard_map/ppermute | solution.py:230
  11.0 9.3 %collective-permute-done.5 = bf16[256,128]{1,0:T(8,128)(2,1)S(1)} collective-permute-done((bf16[256,128]{1,0:T(8,128)(2,1)S(1)}, bf16[256,128]{1,0:T(8,128)(2,1)S(1)}, u32[]{:S(2)}, u32[]{:S(2)}) %collective-permute-start.5) | collective-permute-done | bytes 65568 | tf_op jit(solution)/shard_map/ppermute | solution.py:230
  20.3 1.7 %collective-permute-start = (bf16[272,896]{1,0:T(8,128)(2,1)S(1)}, bf16[272,896]{1,0:T(8,128)(2,1)}, u32[]{:S(2)}, u32[]{:S(2)}) collective-permute-start(bf16[272,896]{1,0:T(8,128)(2,1)S(1)} %get-tuple-element.9), channel_id=1, source_target_pairs={{0,2},{2,0},{4,6},{6,4},{8,10},{10,8},{12,14},{14,12},{16,18},{18,... | collective-permute-start | bytes 1462280 | tf_op jit(solution)/shard_map/ppermute | solution.py:230
  22.0 9.4 %collective-permute-done.4 = bf16[256,128]{1,0:T(8,128)(2,1)S(1)} collective-permute-done((bf16[256,128]{1,0:T(8,128)(2,1)S(1)}, bf16[256,128]{1,0:T(8,128)(2,1)S(1)}, u32[]{:S(2)}, u32[]{:S(2)}) %collective-permute-start.4) | collective-permute-done | bytes 65568 | tf_op jit(solution)/shard_map/ppermute | solution.py:230
  31.4 1.8 %collective-permute-start.6 = (bf16[1024,128]{1,0:T(8,128)(2,1)S(1)}, bf16[1024,128]{1,0:T(8,128)(2,1)S(1)}, u32[]{:S(2)}, u32[]{:S(2)}) collective-permute-start(bf16[1024,128]{1,0:T(8,128)(2,1)S(1)} %pad_maximum_fusion.refs_7_), channel_id=1, source_target_pairs={{0,8},{2,10},{4,12},{6,14},{8,16},{10,18},{12,20},{14,22},{16,24},... | collective-permute-start | bytes 786440 | tf_op jit(solution)/shard_map/ppermute | solution.py:251
  33.3 0.8 fusion.8
  34.2 7.7 %collective-permute-done.6.refs_8_ = bf16[1024,128]{1,0:T(8,128)(2,1)S(1)} collective-permute-done((bf16[1024,128]{1,0:T(8,128)(2,1)S(1)}, bf16[1024,128]{1,0:T(8,128)(2,1)S(1)}, u32[]{:S(2)}, u32[]{:S(2)}) %collective-permute-start.6) | collective-permute-done | bytes 262176 | tf_op jit(solution)/shard_map/ppermute | solution.py:251
  42.0 9.5 %collective-permute-done.7.refs_9_ = bf16[1024,128]{1,0:T(8,128)(2,1)S(1)} collective-permute-done((bf16[1024,128]{1,0:T(8,128)(2,1)S(1)}, bf16[1024,128]{1,0:T(8,128)(2,1)S(1)}, u32[]{:S(2)}, u32[]{:S(2)}) %collective-permute-start.7) | collective-permute-done | bytes 262176 | tf_op jit(solution)/shard_map/ppermute | solution.py:251
  52.3 7.9 %collective-permute-done.8.refs_10_ = bf16[1024,128]{1,0:T(8,128)(2,1)S(1)} collective-permute-done((bf16[1024,128]{1,0:T(8,128)(2,1)S(1)}, bf16[1024,128]{1,0:T(8,128)(2,1)S(1)}, u32[]{:S(2)}, u32[]{:S(2)}) %collective-permute-start.8) | collective-permute-done | bytes 262176 | tf_op jit(solution)/shard_map/ppermute | solution.py:251
  60.2 0.7 dynamic-slice
  60.9 1.1 %constant_dynamic-slice_fusion.11.refs_3_ = bf16[256,896]{1,0:T(8,128)(2,1)S(1)} fusion(bf16[272,3584]{1,0:T(8,128)(2,1)} %copy-done.2, s32[]{:T(128)S(6)} %select_n.95), kind=kLoop, calls=%fused_computation.27 | loop fusion | bytes 917508 | tf_op jit(solution)/shard_map/slice | solution.py:257
  62.0 0.7 slice.63
  65.0 1.1 %slice.64.refs_4_ = bf16[256,896]{1,0:T(8,128)(2,1)S(1)} slice(bf16[272,896]{1,0:T(8,128)(2,1)} %collective-permute-done), slice={[0:256], [0:896]} | slice | bytes 917504 | tf_op jit(solution)/shard_map/slice | solution.py:257
  66.1 1.1 %slice.65.refs_5_ = bf16[256,896]{1,0:T(8,128)(2,1)S(1)} slice(bf16[272,896]{1,0:T(8,128)(2,1)} %collective-permute-done.1), slice={[0:256], [0:896]} | slice | bytes 917504 | tf_op jit(solution)/shard_map/slice | solution.py:257
  67.1 1.1 %slice.66.refs_6_ = bf16[256,896]{1,0:T(8,128)(2,1)S(1)} slice(bf16[272,896]{1,0:T(8,128)(2,1)} %collective-permute-done.2), slice={[0:256], [0:896]} | slice | bytes 917504 | tf_op jit(solution)/shard_map/slice | solution.py:257
  68.2 20.8 %shard_map.64 = f32[112,1]{1,0:T(8,128)S(1)} custom-call(s32[1792]{0:T(1024)S(1)} %reshape.49.refs_0_, s32[156]{0:T(256)S(1)} %fusion.5.refs_1_, s32[112]{0:T(128)S(1)} %reshape.51.refs_2_, bf16[256,896]{1,0:T(8,128)(2,1)S(1)} %constant_dynamic-slice_fusion.11.refs_3_, bf16[256,896]{1,0:T(8,128)(2,1)S(1)} %slice.64.refs_4_, ...), custom_call_target="tpu_custom_call" | custom-call | tf_op jit(solution)/shard_map/pallas_call | solution.py:150
  89.4 2.5 %collective-permute-start.14 = (f32[7,4]{1,0:T(8,128)S(1)}, f32[7,4]{1,0:T(8,128)S(1)}, u32[]{:S(2)}, u32[]{:S(2)}) collective-permute-start(f32[7,4]{1,0:T(8,128)S(1)} %squeeze.27), channel_id=1, source_target_pairs={{0,4},{2,6},{4,0},{6,2},{8,12},{10,14},{12,8},{14,10},{16,20},{18,... | collective-permute-start | bytes 344 | tf_op jit(solution)/shard_map/ppermute | solution.py:230
  92.0 1.0 %collective-permute-start.13 = (f32[7,4]{1,0:T(8,128)S(1)}, f32[7,4]{1,0:T(8,128)S(1)}, u32[]{:S(2)}, u32[]{:S(2)}) collective-permute-start(f32[7,4]{1,0:T(8,128)S(1)} %squeeze.26), channel_id=1, source_target_pairs={{0,2},{2,0},{4,6},{6,4},{8,10},{10,8},{12,14},{14,12},{16,18},{18,... | collective-permute-start | bytes 344 | tf_op jit(solution)/shard_map/ppermute | solution.py:230
  93.1 0.8 collective-permute-done.15
  93.8 1.7 %collective-permute-done.13 = f32[7,4]{1,0:T(8,128)S(1)} collective-permute-done((f32[7,4]{1,0:T(8,128)S(1)}, f32[7,4]{1,0:T(8,128)S(1)}, u32[]{:S(2)}, u32[]{:S(2)}) %collective-permute-start.13) | collective-permute-done | bytes 144 | tf_op jit(solution)/shard_map/ppermute | solution.py:230
  (71 shorter events, 5.9 us)
Async XLA Ops:
  0.0 1.6 %copy-start.4 = (s32[4,28,16]{1,2,0:T(8,128)S(1)}, s32[4,28,16]{1,2,0:T(8,128)}, u32[]{:S(2)}) copy-start(s32[4,28,16]{1,2,0:T(8,128)} %param.9) | copy-start | bytes 21508
  1.6 5.7 %copy-start.3 = (bf16[256,512]{1,0:T(8,128)(2,1)S(1)}, bf16[256,512]{1,0:T(8,128)(2,1)}, u32[]{:S(2)}) copy-start(bf16[256,512]{1,0:T(8,128)(2,1)} %param.7) | copy-start | bytes 786436
  1.9 29.6 %copy-start.2 = (bf16[272,3584]{1,0:T(8,128)(2,1)}, bf16[272,3584]{1,0:T(8,128)(2,1)S(1)}, u32[]{:S(2)}) copy-start(bf16[272,3584]{1,0:T(8,128)(2,1)S(1)} %bitcast_dynamic-update-slice_fusion) | copy-start | bytes 5849092
  2.9 48.8 %collective-permute-start.2 = (bf16[272,896]{1,0:T(8,128)(2,1)}, bf16[272,896]{1,0:T(8,128)(2,1)}, u32[]{:S(2)}, u32[]{:S(2)}) collective-permute-start(bf16[272,896]{1,0:T(8,128)(2,1)} %get-tuple-element.10), channel_id=1, source_target_pairs={{0,6},{2,4},{4,2},{6,0},{8,14},{10,12},{12,10},{14,8},{16,22},{18,... | collective-permute-start | bytes 1462280 | tf_op jit(solution)/shard_map/ppermute | solution.py:230
  6.8 45.4 %collective-permute-start.1 = (bf16[272,896]{1,0:T(8,128)(2,1)S(1)}, bf16[272,896]{1,0:T(8,128)(2,1)}, u32[]{:S(2)}, u32[]{:S(2)}) collective-permute-start(bf16[272,896]{1,0:T(8,128)(2,1)S(1)} %get-tuple-element.11), channel_id=1, source_target_pairs={{0,4},{2,6},{4,0},{6,2},{8,12},{10,14},{12,8},{14,10},{16,20},{18,... | collective-permute-start | bytes 1462280 | tf_op jit(solution)/shard_map/ppermute | solution.py:230
  7.4 12.9 %collective-permute-start.5 = (bf16[256,128]{1,0:T(8,128)(2,1)S(1)}, bf16[256,128]{1,0:T(8,128)(2,1)S(1)}, u32[]{:S(2)}, u32[]{:S(2)}) collective-permute-start(bf16[256,128]{1,0:T(8,128)(2,1)S(1)} %get-tuple-element.14), channel_id=1, source_target_pairs={{0,6},{2,4},{4,2},{6,0},{8,14},{10,12},{12,10},{14,8},{16,22},{18,... | collective-permute-start | bytes 196616 | tf_op jit(solution)/shard_map/ppermute | solution.py:230
  8.9 22.5 %collective-permute-start.4 = (bf16[256,128]{1,0:T(8,128)(2,1)S(1)}, bf16[256,128]{1,0:T(8,128)(2,1)S(1)}, u32[]{:S(2)}, u32[]{:S(2)}) collective-permute-start(bf16[256,128]{1,0:T(8,128)(2,1)S(1)} %get-tuple-element.15), channel_id=1, source_target_pairs={{0,4},{2,6},{4,0},{6,2},{8,12},{10,14},{12,8},{14,10},{16,20},{18,... | collective-permute-start | bytes 196616 | tf_op jit(solution)/shard_map/ppermute | solution.py:230
  9.0 22.4 %collective-permute-start.3 = (bf16[256,128]{1,0:T(8,128)(2,1)S(1)}, bf16[256,128]{1,0:T(8,128)(2,1)S(1)}, u32[]{:S(2)}, u32[]{:S(2)}) collective-permute-start(bf16[256,128]{1,0:T(8,128)(2,1)S(1)} %get-tuple-element.13), channel_id=1, source_target_pairs={{0,2},{2,0},{4,6},{6,4},{8,10},{10,8},{12,14},{14,12},{16,18},{18,... | collective-permute-start | bytes 196616 | tf_op jit(solution)/shard_map/ppermute | solution.py:230
  20.3 43.2 %collective-permute-start = (bf16[272,896]{1,0:T(8,128)(2,1)S(1)}, bf16[272,896]{1,0:T(8,128)(2,1)}, u32[]{:S(2)}, u32[]{:S(2)}) collective-permute-start(bf16[272,896]{1,0:T(8,128)(2,1)S(1)} %get-tuple-element.9), channel_id=1, source_target_pairs={{0,2},{2,0},{4,6},{6,4},{8,10},{10,8},{12,14},{14,12},{16,18},{18,... | collective-permute-start | bytes 1462280 | tf_op jit(solution)/shard_map/ppermute | solution.py:230
  31.4 10.4 %collective-permute-start.6 = (bf16[1024,128]{1,0:T(8,128)(2,1)S(1)}, bf16[1024,128]{1,0:T(8,128)(2,1)S(1)}, u32[]{:S(2)}, u32[]{:S(2)}) collective-permute-start(bf16[1024,128]{1,0:T(8,128)(2,1)S(1)} %pad_maximum_fusion.refs_7_), channel_id=1, source_target_pairs={{0,8},{2,10},{4,12},{6,14},{8,16},{10,18},{12,20},{14,22},{16,24},... | collective-permute-start | bytes 786440 | tf_op jit(solution)/shard_map/ppermute | solution.py:251
  41.9 9.6 %collective-permute-start.7 = (bf16[1024,128]{1,0:T(8,128)(2,1)S(1)}, bf16[1024,128]{1,0:T(8,128)(2,1)S(1)}, u32[]{:S(2)}, u32[]{:S(2)}) collective-permute-start(bf16[1024,128]{1,0:T(8,128)(2,1)S(1)} %collective-permute-done.6.refs_8_), channel_id=1, source_target_pairs={{0,8},{2,10},{4,12},{6,14},{8,16},{10,18},{12,20},{14,22},{16,24},... | collective-permute-start | bytes 786440 | tf_op jit(solution)/shard_map/ppermute | solution.py:251
  51.5 8.7 %collective-permute-start.8 = (bf16[1024,128]{1,0:T(8,128)(2,1)S(1)}, bf16[1024,128]{1,0:T(8,128)(2,1)S(1)}, u32[]{:S(2)}, u32[]{:S(2)}) collective-permute-start(bf16[1024,128]{1,0:T(8,128)(2,1)S(1)} %collective-permute-done.7.refs_9_), channel_id=1, source_target_pairs={{0,8},{2,10},{4,12},{6,14},{8,16},{10,18},{12,20},{14,22},{16,24},... | collective-permute-start | bytes 786440 | tf_op jit(solution)/shard_map/ppermute | solution.py:251
  51.6 16.6 %collective-permute-start.9 = (bf16[1024,128]{1,0:T(8,128)(2,1)S(1)}, bf16[1024,128]{1,0:T(8,128)(2,1)S(1)}, u32[]{:S(2)}, u32[]{:S(2)}) collective-permute-start(bf16[1024,128]{1,0:T(8,128)(2,1)S(1)} %pad_maximum_fusion.refs_7_), channel_id=1, source_target_pairs={{0,1},{1,0},{2,3},{3,2},{4,5},{5,4},{6,7},{7,6},{8,9},{9,8},{10,11... | collective-permute-start | bytes 786440 | tf_op jit(solution)/shard_map/ppermute | solution.py:233
  51.7 16.5 %collective-permute-start.10 = (bf16[1024,128]{1,0:T(8,128)(2,1)S(1)}, bf16[1024,128]{1,0:T(8,128)(2,1)S(1)}, u32[]{:S(2)}, u32[]{:S(2)}) collective-permute-start(bf16[1024,128]{1,0:T(8,128)(2,1)S(1)} %collective-permute-done.6.refs_8_), channel_id=1, source_target_pairs={{0,1},{1,0},{2,3},{3,2},{4,5},{5,4},{6,7},{7,6},{8,9},{9,8},{10,11... | collective-permute-start | bytes 786440 | tf_op jit(solution)/shard_map/ppermute | solution.py:233
  52.2 16.0 %collective-permute-start.11 = (bf16[1024,128]{1,0:T(8,128)(2,1)S(1)}, bf16[1024,128]{1,0:T(8,128)(2,1)S(1)}, u32[]{:S(2)}, u32[]{:S(2)}) collective-permute-start(bf16[1024,128]{1,0:T(8,128)(2,1)S(1)} %collective-permute-done.7.refs_9_), channel_id=1, source_target_pairs={{0,1},{1,0},{2,3},{3,2},{4,5},{5,4},{6,7},{7,6},{8,9},{9,8},{10,11... | collective-permute-start | bytes 786440 | tf_op jit(solution)/shard_map/ppermute | solution.py:233
  60.2 8.1 %collective-permute-start.12 = (bf16[1024,128]{1,0:T(8,128)(2,1)S(1)}, bf16[1024,128]{1,0:T(8,128)(2,1)S(1)}, u32[]{:S(2)}, u32[]{:S(2)}) collective-permute-start(bf16[1024,128]{1,0:T(8,128)(2,1)S(1)} %collective-permute-done.8.refs_10_), channel_id=1, source_target_pairs={{0,1},{1,0},{2,3},{3,2},{4,5},{5,4},{6,7},{7,6},{8,9},{9,8},{10,11... | collective-permute-start | bytes 786440 | tf_op jit(solution)/shard_map/ppermute | solution.py:233
  60.9 7.3 %copy-start = (bf16[384,128]{1,0:T(8,128)(2,1)S(1)}, bf16[384,128]{1,0:T(8,128)(2,1)}, u32[]{:S(2)}) copy-start(bf16[384,128]{1,0:T(8,128)(2,1)} %refs_16_.1) | copy-start | bytes 294916
  60.9 7.3 %copy-start.1 = (bf16[128,128]{1,0:T(8,128)(2,1)S(1)}, bf16[128,128]{1,0:T(8,128)(2,1)}, u32[]{:S(2)}) copy-start(bf16[128,128]{1,0:T(8,128)(2,1)} %refs_15_.1) | copy-start | bytes 98308
  89.3 4.5 %collective-permute-start.15 = (f32[7,4]{1,0:T(8,128)S(1)}, f32[7,4]{1,0:T(8,128)S(1)}, u32[]{:S(2)}, u32[]{:S(2)}) collective-permute-start(f32[7,4]{1,0:T(8,128)S(1)} %squeeze.28), channel_id=1, source_target_pairs={{0,6},{2,4},{4,2},{6,0},{8,14},{10,12},{12,10},{14,8},{16,22},{18,... | collective-permute-start | bytes 344 | tf_op jit(solution)/shard_map/ppermute | solution.py:230
  89.4 4.4 %collective-permute-start.14 = (f32[7,4]{1,0:T(8,128)S(1)}, f32[7,4]{1,0:T(8,128)S(1)}, u32[]{:S(2)}, u32[]{:S(2)}) collective-permute-start(f32[7,4]{1,0:T(8,128)S(1)} %squeeze.27), channel_id=1, source_target_pairs={{0,4},{2,6},{4,0},{6,2},{8,12},{10,14},{12,8},{14,10},{16,20},{18,... | collective-permute-start | bytes 344 | tf_op jit(solution)/shard_map/ppermute | solution.py:230
  92.0 3.6 %collective-permute-start.13 = (f32[7,4]{1,0:T(8,128)S(1)}, f32[7,4]{1,0:T(8,128)S(1)}, u32[]{:S(2)}, u32[]{:S(2)}) collective-permute-start(f32[7,4]{1,0:T(8,128)S(1)} %squeeze.26), channel_id=1, source_target_pairs={{0,2},{2,0},{4,6},{6,4},{8,10},{10,8},{12,14},{14,12},{16,18},{18,... | collective-permute-start | bytes 344 | tf_op jit(solution)/shard_map/ppermute | solution.py:230

commit v2 on v1

--- a/solution.py
+++ b/solution.py
@@ -16,30 +16,47 @@
 
 def gate_kernel(dims, *refs):
     n_piece, n_key, heads, n_sel, n_cand, blocks, head_size = dims
-    sel_s, cand_s, dup_s = refs[:3]
-    q_in = refs[3 : 3 + n_piece]
-    k_in = refs[3 + n_piece : 3 + n_piece + n_key]
-    wq_ref, wk_ref, out_ref = refs[3 + n_piece + n_key : 6 + n_piece + n_key]
-    qbuf, kbuf, pool, qpool, teach, ms, ss, lv, sem_q, sem_k = refs[6 + n_piece + n_key :]
-    span = q_in[0].shape[0]
+    cand_s = refs[0]
+    q_in = refs[1 : 1 + n_piece]
+    k_in = refs[1 + n_piece : 1 + n_piece + n_key]
+    refs = refs[1 + n_piece + n_key :]
+    wq_ref, wk_ref = refs[:2]
+    out_refs = refs[2 : 2 + n_piece]
+    qbuf, kbuf, pool, qpool, teach, ms, ss, lv, sel_v, sel_s, sem_q, sem_k, sem_s = refs[2 + n_piece :]
+    stride = q_in[0].shape[0]
+    span = stride - SEL_ROWS
     span_blocks = span // BLOCK
     n_slot = n_sel + 1
     rows = n_piece * heads * span_blocks
     exp_scale = math.log2(math.e) / math.sqrt(head_size)
 
     q_copies = [
-        pltpu.make_async_copy(q_in[i], qbuf.at[pl.ds(i * span, span)], sem_q.at[i]) for i in range(n_piece)
+        pltpu.make_async_copy(q_in[i], qbuf.at[pl.ds(i * stride, stride)], sem_q.at[i]) for i in range(n_piece)
     ]
     k_rows = k_in[0].shape[0]
     k_copies = [
         pltpu.make_async_copy(k_in[i], kbuf.at[pl.ds(i * k_rows, k_rows)], sem_k.at[i]) for i in range(n_key)
     ]
-    for copy in k_copies + q_copies:
+    for copy in q_copies + k_copies:
         copy.start()
     ms[...] = jnp.full(ms.shape, NEG, jnp.float32)
     ss[...] = jnp.zeros(ss.shape, jnp.float32)
     lv[...] = jnp.full(lv.shape, -1, jnp.int32)
-    for copy in k_copies + q_copies:
+    for copy in q_copies:
+        copy.wait()
+
+    lane = lax.broadcasted_iota(jnp.int32, (1, LANES), 1)
+    sub = lax.broadcasted_iota(jnp.int32, (SEL_ROWS, 1), 0)
+    for i in range(n_piece):
+        for h in range(heads):
+            at = slice(h * head_size, h * head_size + LANES)
+            mine = qbuf[i * stride + span : (i + 1) * stride, at].astype(jnp.int32)
+            own = jnp.where((mine == sub) & (lane < n_sel), 1, 0)
+            own = jnp.max(own, axis=1, keepdims=True)
+            sel_v[i, :, h * LANES : (h + 1) * LANES] = jnp.where(lane == n_sel, own, mine)
+    sel_copy = pltpu.make_async_copy(sel_v, sel_s, sem_s)
+    sel_copy.start()
+    for copy in k_copies:
         copy.wait()
 
     def pool_step(i, carry):
@@ -52,15 +69,15 @@
         return carry
 
     lax.fori_loop(0, blocks // 8, pool_step, 0)
-
-    lane = lax.broadcasted_iota(jnp.int32, (1, LANES), 1)
+    sel_copy.wait()
+
     low = lane < BLOCK
     zeros = jnp.zeros((BLOCK, head_size), jnp.bfloat16)
 
     def pair_step(ph, t, u):
         piece = ph // heads
         head = ph - piece * heads
-        q_at = pl.ds(pl.multiple_of(piece * span + t * 2 * BLOCK, 2 * BLOCK), 2 * BLOCK)
+        q_at = pl.ds(pl.multiple_of(piece * stride + t * 2 * BLOCK, SEL_ROWS), 2 * BLOCK)
         q = qbuf[q_at, pl.ds(pl.multiple_of(head * head_size, head_size), head_size)]
         q0, q1 = q[:BLOCK], q[BLOCK:]
         row = ph * span_blocks + 2 * t
@@ -75,7 +92,7 @@
             halves = []
             for half in range(2):
                 if slot < n_sel:
-                    place = sel_s[(row + half) * n_sel + slot]
+                    place = sel_s[piece, 2 * t + half, head * LANES + slot]
                 else:
                     place = 2 * t + half
                 at = cand_s[piece * n_cand + place]
@@ -93,8 +110,8 @@
             top = jnp.max(part, axis=0, keepdims=True)
             total = jnp.sum(jnp.exp2((part - top) * exp_scale), axis=0, keepdims=True)
             if slot == n_sel:
-                keep = jnp.where(low, 1 - dup_s[row], 1 - dup_s[row + 1])
-                total = total * keep.astype(jnp.float32)
+                drop = [sel_s[piece, 2 * t + half, head * LANES + n_sel] for half in range(2)]
+                total = total * (1 - jnp.where(low, drop[0], drop[1])).astype(jnp.float32)
             ms[u, slot : slot + 1, :] = top
             ss[u, slot : slot + 1, :] = total
         tops = ms[u]
@@ -130,30 +147,39 @@
     teacher = jnp.concatenate([teach[c] for c in range(blocks // LANES)], axis=1)
     positive = teacher > 0
     safe = jnp.where(positive, teacher, 1.0)
-    out_ref[...] = jnp.sum(
-        jnp.where(positive, teacher * (jnp.log(safe) - log_gate), 0.0), axis=1, keepdims=True
-    )
-
-
-def gate_call(sel, cand, dup, q_pieces, k_pieces, w_query, key_gate_weight, heads, n_sel, n_cand):
+    kl = jnp.sum(jnp.where(positive, teacher * (jnp.log(safe) - log_gate), 0.0), axis=1, keepdims=True)
+    r = lax.broadcasted_iota(jnp.int32, (rows, 1), 0)
+    spread = jnp.where(r // span_blocks % heads == lane, kl, 0.0)
+    r = lax.broadcasted_iota(jnp.int32, (1, rows), 1)
+    b = lax.broadcasted_iota(jnp.int32, (8, 1), 0)
+    for i in range(n_piece):
+        pick = (r % span_blocks == b) & (r // (span_blocks * heads) == i) & (b < span_blocks)
+        tile = jnp.dot(
+            pick.astype(jnp.float32), spread, preferred_element_type=jnp.float32, precision=lax.Precision.HIGHEST
+        )
+        out_refs[i][...] = tile
+
+
+def gate_call(cand, q_pieces, k_pieces, w_query, key_gate_weight, heads, n_sel, n_cand):
     head_size = w_query.shape[0]
-    span = q_pieces[0].shape[0]
-    k_rows = k_pieces[0].shape[0]
-    blocks = len(k_pieces) * k_rows // BLOCK
-    rows = len(q_pieces) * heads * (span // BLOCK)
-    dims = (len(q_pieces), len(k_pieces), heads, n_sel, n_cand, blocks, head_size)
-    unroll = span // BLOCK // 2
+    stride = q_pieces[0].shape[0]
+    span_blocks = (stride - SEL_ROWS) // BLOCK
+    n_piece = len(q_pieces)
+    blocks = len(k_pieces) * k_pieces[0].shape[0] // BLOCK
+    rows = n_piece * heads * span_blocks
+    dims = (n_piece, len(k_pieces), heads, n_sel, n_cand, blocks, head_size)
+    unroll = span_blocks // 2
     slots = -(-(n_sel + 1) // 8) * 8
     smem = pl.BlockSpec(memory_space=pltpu.SMEM)
     hbm = pl.BlockSpec(memory_space=pl.ANY)
     vmem = pl.BlockSpec(memory_space=pltpu.VMEM)
     return pl.pallas_call(
         functools.partial(gate_kernel, dims),
-        out_shape=jax.ShapeDtypeStruct((rows, 1), jnp.float32),
-        in_specs=[smem] * 3 + [hbm] * (len(q_pieces) + len(k_pieces)) + [vmem] * 2,
-        out_specs=vmem,
+        out_shape=[jax.ShapeDtypeStruct((8, LANES), jnp.float32)] * n_piece,
+        in_specs=[smem] + [hbm] * (n_piece + len(k_pieces)) + [vmem] * 2,
+        out_specs=[vmem] * n_piece,
         scratch_shapes=[
-            pltpu.VMEM((len(q_pieces) * span, heads * head_size), jnp.bfloat16),
+            pltpu.VMEM((n_piece * stride, heads * head_size), jnp.bfloat16),
             pltpu.VMEM((blocks * BLOCK, head_size), jnp.bfloat16),
             pltpu.VMEM((blocks, 3 * head_size), jnp.float32),
             pltpu.VMEM((rows, head_size), jnp.float32),
@@ -161,11 +187,14 @@
             pltpu.VMEM((unroll, slots, LANES), jnp.float32),
             pltpu.VMEM((unroll, slots, LANES), jnp.float32),
             pltpu.VMEM((unroll, 2, slots, LANES), jnp.int32),
-            pltpu.SemaphoreType.DMA((len(q_pieces),)),
+            pltpu.VMEM((n_piece, SEL_ROWS, heads * LANES), jnp.int32),
+            pltpu.SMEM((n_piece, SEL_ROWS, heads * LANES), jnp.int32),
+            pltpu.SemaphoreType.DMA((n_piece,)),
             pltpu.SemaphoreType.DMA((len(k_pieces),)),
+            pltpu.SemaphoreType.DMA(()),
         ],
         compiler_params=pltpu.CompilerParams(vmem_limit_bytes=40 * 1024 * 1024),
-    )(sel, cand, dup, *q_pieces, *k_pieces, w_query, key_gate_weight)
+    )(cand, *q_pieces, *k_pieces, w_query, key_gate_weight)
 
 
 def per_device(queries, key_state_rows, wanted, selected, w_query, key_gate_weight):
@@ -207,60 +236,56 @@
     n_cand = candidates[0].shape[0]
     cand = place_of(jnp.stack(candidates)).astype(jnp.int32).reshape(-1)
 
-    def lists(sel):
-        sel = jnp.transpose(sel, (0, 2, 1, 3))
-        dup = jnp.any(sel == local_ids[None, None, :, None], axis=3).astype(jnp.int32)
-        return sel.reshape(-1), dup.reshape(-1)
-
-    if not ring:
-        gathered = lax.all_gather(key_state_rows, ("ctx", "pair"), axis=0, tiled=True)
-        outs = []
-        for g in range(kv_heads):
-            sel, dup = lists(selected[None, :, g * heads : (g + 1) * heads])
-            out = gate_call(
-                sel, cand, dup,
-                [queries[:, g * heads * head_size : (g + 1) * heads * head_size]],
-                [gathered[:, g * head_size : (g + 1) * head_size]],
-                w_query, key_gate_weight, heads, n_sel, n_cand,
-            )
-            outs.append(jnp.transpose(out.reshape(heads, span_blocks)))
-        return jnp.concatenate(outs, axis=1)
-
-    def flipped(x, p):
-        return x if p == 0 else lax.ppermute(x, "ctx", [(i, i ^ p) for i in range(n_ctx)])
-
-    def other_core(x):
-        return lax.ppermute(x, "pair", [(0, 1), (1, 0)])
-
-    keys = [
-        flipped(lax.dynamic_slice_in_dim(key_state_rows, (spot ^ p) * head_size, head_size, 1), p)
-        for p in range(plane)
-    ]
-    steps = [jnp.concatenate(keys, axis=0)]
     sel_rows = jnp.pad(
         selected.astype(jnp.bfloat16),
         ((0, SEL_ROWS - span_blocks), (0, 0), (0, head_size - n_sel)),
     ).reshape(SEL_ROWS, q_heads * head_size)
     sent = jnp.concatenate([queries, sel_rows], axis=0)
     width = heads * head_size
-    pieces = [
-        flipped(lax.dynamic_slice_in_dim(sent, (spot ^ p) * width, width, 1), p) for p in range(plane)
+
+    if not ring:
+        gathered = lax.all_gather(key_state_rows, ("ctx", "pair"), axis=0, tiled=True)
+        outs = []
+        for g in range(kv_heads):
+            (out,) = gate_call(
+                cand,
+                [sent[:, g * width : (g + 1) * width]],
+                [gathered[:, g * head_size : (g + 1) * head_size]],
+                w_query, key_gate_weight, heads, n_sel, n_cand,
+            )
+            outs.append(out[:span_blocks, :heads])
+        return jnp.concatenate(outs, axis=1)
+
+    def flipped(x, p):
+        return x if p == 0 else lax.ppermute(x, "ctx", [(i, i ^ p) for i in range(n_ctx)])
+
+    def other_core(x):
+        return lax.ppermute(x, "pair", [(0, 1), (1, 0)])
+
+    keys = [
+        flipped(lax.dynamic_slice_in_dim(key_state_rows, (spot ^ p) * head_size, head_size, 1), p)
+        for p in range(plane)
     ]
-    for _ in range(layers - 1):
+    parts = [lax.dynamic_slice_in_dim(sent, (spot ^ p) * width, width, 1) for p in range(plane)]
+    steps = [jnp.concatenate(keys, axis=0)]
+    steps[0], parts = lax.optimization_barrier((steps[0], parts))
+    pieces = [flipped(x, p) for p, x in enumerate(parts)]
+    for i in range(layers - 1):
+        if i == 2:
+            steps[2], pieces[1:3] = lax.optimization_barrier((steps[2], pieces[1:3]))
         steps.append(
             lax.ppermute(steps[-1], "ctx", [(i, (i + plane) % n_ctx) for i in range(n_ctx)])
         )
     k_pieces = steps + [other_core(x) for x in steps]
-    sel = jnp.stack([x[span : span + span_blocks] for x in pieces])
-    sel = sel.reshape(plane, span_blocks, heads, head_size)[..., :n_sel].astype(jnp.int32)
-    sel, dup = lists(sel)
-    q_pieces = [x[:span] for x in pieces]
-    out = gate_call(sel, cand, dup, q_pieces, k_pieces, w_query, key_gate_weight, heads, n_sel, n_cand)
-    out = out.reshape(plane, heads, span_blocks)
-    back = jnp.stack([flipped(out[p], p) for p in range(plane)])
-    order = jnp.arange(plane, dtype=jnp.int32) ^ spot
-    back = jnp.transpose(back[order], (2, 0, 1))
-    return back.reshape(span_blocks, q_heads)
+    outs = gate_call(cand, pieces, k_pieces, w_query, key_gate_weight, heads, n_sel, n_cand)
+    back = [flipped(x, p)[:span_blocks, :heads] for p, x in enumerate(outs)]
+    columns = []
+    for g in range(plane):
+        column = back[0]
+        for p in range(1, plane):
+            column = jnp.where(spot ^ g == p, back[p], column)
+        columns.append(column)
+    return jnp.concatenate(columns, axis=1)
 
 
 def solution(mesh):

time: 97.5 us -> 76 us (0.78)
  waiting for transfers between devices: 46.3 us -> 23.9 us
  local copies, waits for them, and re-layouts: 13.2 us -> 8.03 us
  other arithmetic: 0.67 us -> 5.66 us
  Pallas kernels: 20.8 us -> 25.4 us
  starting transfers between devices: 15.7 us -> 12.4 us
    ppermute x9, waiting for transfers between devices: 21.2 us -> 8.79 us  [flipped(): lax.ppermute(x, 'ctx', [(i, i ^ p) for i in range(n_ctx)])]
    ppermute x3, waiting for transfers between devices: 25.1 us -> 15.1 us  [per_device(): lax.ppermute(steps[-1], 'ctx', [(i, (i + plane) % n_ctx) for i in range(n...]
    slice x10 -> x0, local copies, waits for them, and re-layouts: 7.36 us -> none  [the longest x4 4.27 us: per_device(): q_pieces = [x[:span] for x in pieces]]
    pallas_call x1, Pallas kernels: 20.8 us -> 25.4 us  [gate_call(): pl.pallas_call(functools.partial(gate_kernel, dims), out_shape=[jax.Shape...]
    ppermute x9, starting transfers between devices: 13.2 us -> 10.2 us  [flipped(): lax.ppermute(x, 'ctx', [(i, i ^ p) for i in range(n_ctx)])]
    another operation x3, other arithmetic: 0.17 us -> 1.98 us  [per_device(): cand = place_of(jnp.stack(candidates)).astype(jnp.int32).reshape(-1)]
    dynamic_slice x1, local copies, waits for them, and re-layouts: 0.05 us -> 1.61 us  [per_device(): lax.dynamic_slice_in_dim(key_state_rows, (spot ^ p) * head_size, head_siz...]
    unnamed x12 -> x10, local copies, waits for them, and re-layouts: 1.76 us -> 3.2 us
  transfers between devices with their start and end apart: 16 -> 16, of which waited for: 7 -> 10; matrix products, arithmetic and copies ran while one was open for 10% -> 10% of each run, Pallas kernels for 0% -> 0%
where the time goes in v2:
time: 76 us; the launch traced here: 75.6 us
  Pallas kernels  25.4 us (33%)
  waiting for transfers between devices  23.9 us (31%)
  starting transfers between devices  12.4 us (16%)
  local copies, waits for them, and re-layouts  8.03 us (11%)
  other arithmetic  5.66 us (7%)
    pallas_call x1, Pallas kernels, gate_call(): pl.pallas_call(functools.partial(gate_kernel, dims), out_shape=[jax.Shape...  25.4 us
    ppermute x3, waiting for transfers between devices, per_device(): lax.ppermute(steps[-1], 'ctx', [(i, (i + plane) % n_ctx) for i in range(n...  15.1 us
    ppermute x9, starting transfers between devices, flipped(): lax.ppermute(x, 'ctx', [(i, i ^ p) for i in range(n_ctx)])  10.2 us
    ppermute x9, waiting for transfers between devices, flipped(): lax.ppermute(x, 'ctx', [(i, i ^ p) for i in range(n_ctx)])  8.79 us
    unnamed x10, local copies, waits for them, and re-layouts  3.2 us
    another operation x3, other arithmetic, per_device(): cand = place_of(jnp.stack(candidates)).astype(jnp.int32).reshape(-1)  1.98 us
    ppermute x3, starting transfers between devices, per_device(): lax.ppermute(steps[-1], 'ctx', [(i, (i + plane) % n_ctx) for i in range(n...  1.63 us
    dynamic_slice x1, local copies, waits for them, and re-layouts, per_device(): lax.dynamic_slice_in_dim(key_state_rows, (spot ^ p) * head_size, head_siz...  1.61 us
  transfers between devices with their start and end apart: 16, of which 10 were waited for; matrix products, arithmetic and copies ran while one was open for 10% of the time, Pallas kernels for 0%

profile of v2, /device:TPU:0, one launch (start us, length us, event | category | flops | bytes accessed | tf_op | source)
XLA Modules:
  0.0 75.6 jit_solution(8029067181281457872)
XLA Ops:
  0.0 1.6 %constant_dynamic-slice_fusion.7 = (bf16[256,128]{1,0:T(8,128)(2,1)S(1)}, bf16[256,128]{1,0:T(8,128)(2,1)}, bf16[256,128]{1,0:T(8,128)(2,1)}, bf16[256,128]{1,0:T(8,128)(2,1)}) fusion(bf16[256,512]{1,0:T(8,128)(2,1)} %param.7, s32[]{:T(128)S(6)} %select_n.172, s32[]{:T(128)S(6)} %select_n.173, s32[]{:T(128)S(6)} %select_n.175, s32[]{:T(128)S(6)} %select_n.174), kind=kLoop, calls=%fused_computation.10 | loop fusion | bytes 524304 | tf_op jit(solution)/shard_map/dynamic_slice | solution.py:266
  1.6 2.9 %collective-permute-start = (bf16[256,128]{1,0:T(8,128)(2,1)}, bf16[256,128]{1,0:T(8,128)(2,1)}, u32[]{:S(2)}, u32[]{:S(2)}) collective-permute-start(bf16[256,128]{1,0:T(8,128)(2,1)} %get-tuple-element.34), channel_id=1, source_target_pairs={{0,2},{2,0},{4,6},{6,4},{8,10},{10,8},{12,14},{14,12},{16,18},{18,... | collective-permute-start | bytes 196616 | tf_op jit(solution)/shard_map/ppermute | solution.py:260
  4.6 1.5 %collective-permute-start.1 = (bf16[256,128]{1,0:T(8,128)(2,1)}, bf16[256,128]{1,0:T(8,128)(2,1)}, u32[]{:S(2)}, u32[]{:S(2)}) collective-permute-start(bf16[256,128]{1,0:T(8,128)(2,1)} %get-tuple-element.36), channel_id=1, source_target_pairs={{0,4},{2,6},{4,0},{6,2},{8,12},{10,14},{12,8},{14,10},{16,20},{18,... | collective-permute-start | bytes 196616 | tf_op jit(solution)/shard_map/ppermute | solution.py:260
  6.1 1.6 %constant_dynamic-update-slice_fusion = bf16[272,3584]{1,0:T(8,128)(2,1)S(1)} fusion(bf16[256,3584]{1,0:T(8,128)(2,1)} %param.6), kind=kLoop, calls=%fused_computation.2 | loop fusion | bytes 3670016
  8.0 1.0 %constant_dynamic-slice_fusion = (bf16[272,896]{1,0:T(8,128)(2,1)}, bf16[272,896]{1,0:T(8,128)(2,1)S(1)}, bf16[272,896]{1,0:T(8,128)(2,1)S(1)}, bf16[272,896]{1,0:T(8,128)(2,1)S(1)}) fusion(bf16[272,3584]{1,0:T(8,128)(2,1)S(1)} %bitcast_dynamic-update-slice_fusion, s32[]{:T(128)S(6)} %select_n.179, s32[]{:T(128)S(6)} %select_n.178, s32[]{:T(128)S(6)} %select_n.177, ...), kind=kLoop, calls=%fused_computation.3 | loop fusion | bytes 3899408 | tf_op jit(solution)/shard_map/dynamic_slice | solution.py:269
  9.1 2.4 %collective-permute-done.2 = bf16[256,128]{1,0:T(8,128)(2,1)} collective-permute-done((bf16[256,128]{1,0:T(8,128)(2,1)}, bf16[256,128]{1,0:T(8,128)(2,1)}, u32[]{:S(2)}, u32[]{:S(2)}) %collective-permute-start.2) | collective-permute-done | bytes 65568 | tf_op jit(solution)/shard_map/ppermute | solution.py:260
  11.6 0.9 %pad_maximum_fusion.refs_5_ = bf16[1024,128]{1,0:T(8,128)(2,1)S(1)} fusion(bf16[256,128]{1,0:T(8,128)(2,1)} %collective-permute-done.2, bf16[256,128]{1,0:T(8,128)(2,1)} %collective-permute-done.1, bf16[256,128]{1,0:T(8,128)(2,1)} %collective-permute-done, bf16[256,128]{1,0:T(8,128)(2,1)S(1)} %get-tuple-element.33), kind=kLoop, calls=%fused_computation | loop fusion | flops 1048576 | bytes 524288 | tf_op jit(solution)/shard_map/concatenate | solution.py:270
  12.5 1.6 %collective-permute-start.3 = (bf16[1024,128]{1,0:T(8,128)(2,1)S(1)}, bf16[1024,128]{1,0:T(8,128)(2,1)S(1)}, u32[]{:S(2)}, u32[]{:S(2)}) collective-permute-start(bf16[1024,128]{1,0:T(8,128)(2,1)S(1)} %pad_maximum_fusion.refs_5_), channel_id=1, source_target_pairs={{0,8},{2,10},{4,12},{6,14},{8,16},{10,18},{12,20},{14,22},{16,24},... | collective-permute-start | bytes 786440 | tf_op jit(solution)/shard_map/ppermute | solution.py:277
  15.2 5.6 %collective-permute-done.3.refs_6_ = bf16[1024,128]{1,0:T(8,128)(2,1)S(1)} collective-permute-done((bf16[1024,128]{1,0:T(8,128)(2,1)S(1)}, bf16[1024,128]{1,0:T(8,128)(2,1)S(1)}, u32[]{:S(2)}, u32[]{:S(2)}) %collective-permute-start.3) | collective-permute-done | bytes 262176 | tf_op jit(solution)/shard_map/ppermute | solution.py:277
  20.7 0.8 %fusion.6 = (s32[31]{0:T(128)S(1)}, s32[31]{0:T(128)S(1)}, s32[31]{0:T(128)S(1)}, s32[31]{0:T(128)S(1)}) fusion(s32[32,31]{1,0:T(8,128)} %param.8, s32[]{:T(128)S(6)} %select_n.160, s32[]{:T(128)S(6)} %select_n.161, s32[]{:T(128)S(6)} %select_n.163, s32[]{:T(128)S(6)} %select_n.162), kind=kLoop, calls=%fused_computation.45 | loop fusion | bytes 1008 | tf_op jit(solution)/shard_map/jit(dynamic_index_in_dim)/squeeze | solution.py:230
  22.2 2.8 %collective-permute-done.5.refs_2_ = bf16[272,896]{1,0:T(8,128)(2,1)S(1)} collective-permute-done((bf16[272,896]{1,0:T(8,128)(2,1)S(1)}, bf16[272,896]{1,0:T(8,128)(2,1)S(1)}, u32[]{:S(2)}, u32[]{:S(2)}) %collective-permute-start.5) | collective-permute-done | bytes 487456 | tf_op jit(solution)/shard_map/ppermute | solution.py:260
  25.7 3.2 %collective-permute-done.4.refs_7_ = bf16[1024,128]{1,0:T(8,128)(2,1)S(1)} collective-permute-done((bf16[1024,128]{1,0:T(8,128)(2,1)S(1)}, bf16[1024,128]{1,0:T(8,128)(2,1)S(1)}, u32[]{:S(2)}, u32[]{:S(2)}) %collective-permute-start.4) | collective-permute-done | bytes 262176 | tf_op jit(solution)/shard_map/ppermute | solution.py:277
  28.9 1.2 %collective-permute-start.7 = (bf16[272,896]{1,0:T(8,128)(2,1)}, bf16[272,896]{1,0:T(8,128)(2,1)S(1)}, u32[]{:S(2)}, u32[]{:S(2)}) collective-permute-start(bf16[272,896]{1,0:T(8,128)(2,1)} %get-tuple-element.23), channel_id=1, source_target_pairs={{0,6},{2,4},{4,2},{6,0},{8,14},{10,12},{12,10},{14,8},{16,22},{18,... | collective-permute-start | bytes 1462280 | tf_op jit(solution)/shard_map/ppermute | solution.py:260
  30.8 6.3 %collective-permute-done.8.refs_8_ = bf16[1024,128]{1,0:T(8,128)(2,1)S(1)} collective-permute-done((bf16[1024,128]{1,0:T(8,128)(2,1)S(1)}, bf16[1024,128]{1,0:T(8,128)(2,1)S(1)}, u32[]{:S(2)}, u32[]{:S(2)}) %collective-permute-start.8) | collective-permute-done | bytes 262176 | tf_op jit(solution)/shard_map/ppermute | solution.py:277
  37.1 1.3 %pad_add_fusion = s32[4,39]{1,0:T(4,128)} fusion(s32[1,39]{1,0:T(1,128)S(1)} %get-tuple-element.48, s32[1,39]{1,0:T(1,128)S(1)} %get-tuple-element.47, s32[1,39]{1,0:T(1,128)} %get-tuple-element.46, s32[1,39]{1,0:T(1,128)} %get-tuple-element.45), kind=kLoop, calls=%fused_computation.17 | loop fusion | flops 468 | bytes 1248 | tf_op jit(solution)/shard_map/stack | solution.py:237
  38.3 1.3 %stack.22 = s32[156]{0:T(256)} reshape(s32[4,39]{1,0:T(4,128)} %pad_add_fusion) | data formatting | bytes 1248 | tf_op jit(solution)/shard_map/stack | solution.py:237
  39.7 0.7 fusion.4.refs_0_
  40.5 0.9 %copy-done = bf16[384,128]{1,0:T(8,128)(2,1)S(1)} copy-done((bf16[384,128]{1,0:T(8,128)(2,1)S(1)}, bf16[384,128]{1,0:T(8,128)(2,1)}, u32[]{:S(2)}) %copy-start) | copy-done | bytes 98328
  41.3 25.4 %shard_map.64 = (f32[8,128]{1,0:T(8,128)S(1)}, f32[8,128]{1,0:T(8,128)}, f32[8,128]{1,0:T(8,128)}, f32[8,128]{1,0:T(8,128)}) custom-call(s32[156]{0:T(256)S(1)} %fusion.4.refs_0_, bf16[272,896]{1,0:T(8,128)(2,1)S(1)} %get-tuple-element.17.refs_1_, bf16[272,896]{1,0:T(8,128)(2,1)S(1)} %collective-permute-done.5.refs_2_, ...), custom_call_target="tpu_custom_call" | custom-call | tf_op jit(solution)/shard_map/pallas_call | solution.py:176
  67.3 1.2 %collective-permute-start.13 = (f32[8,128]{1,0:T(8,128)}, f32[8,128]{1,0:T(8,128)S(1)}, u32[]{:S(2)}, u32[]{:S(2)}) collective-permute-start(f32[8,128]{1,0:T(8,128)} %get-tuple-element.25), channel_id=1, source_target_pairs={{0,6},{2,4},{4,2},{6,0},{8,14},{10,12},{12,10},{14,8},{16,22},{18,... | collective-permute-start | bytes 12296 | tf_op jit(solution)/shard_map/ppermute | solution.py:260
  68.5 1.2 %collective-permute-start.14 = (f32[8,128]{1,0:T(8,128)}, f32[8,128]{1,0:T(8,128)S(1)}, u32[]{:S(2)}, u32[]{:S(2)}) collective-permute-start(f32[8,128]{1,0:T(8,128)} %get-tuple-element.26), channel_id=1, source_target_pairs={{0,4},{2,6},{4,0},{6,2},{8,12},{10,14},{12,8},{14,10},{16,20},{18,... | collective-permute-start | bytes 12296 | tf_op jit(solution)/shard_map/ppermute | solution.py:260
  69.7 1.1 %collective-permute-start.15 = (f32[8,128]{1,0:T(8,128)}, f32[8,128]{1,0:T(8,128)S(1)}, u32[]{:S(2)}, u32[]{:S(2)}) collective-permute-start(f32[8,128]{1,0:T(8,128)} %get-tuple-element.27), channel_id=1, source_target_pairs={{0,2},{2,0},{4,6},{6,4},{8,10},{10,8},{12,14},{14,12},{16,18},{18,... | collective-permute-start | bytes 12296 | tf_op jit(solution)/shard_map/ppermute | solution.py:260
  70.8 1.2 %collective-permute-done.13 = f32[8,128]{1,0:T(8,128)S(1)} collective-permute-done((f32[8,128]{1,0:T(8,128)}, f32[8,128]{1,0:T(8,128)S(1)}, u32[]{:S(2)}, u32[]{:S(2)}) %collective-permute-start.13) | collective-permute-done | bytes 4128 | tf_op jit(solution)/shard_map/ppermute | solution.py:260
  72.3 1.2 %collective-permute-done.15 = f32[8,128]{1,0:T(8,128)S(1)} collective-permute-done((f32[8,128]{1,0:T(8,128)}, f32[8,128]{1,0:T(8,128)S(1)}, u32[]{:S(2)}, u32[]{:S(2)}) %collective-permute-start.15) | collective-permute-done | bytes 4128 | tf_op jit(solution)/shard_map/ppermute | solution.py:260
  (42 shorter events, 6.3 us)
Async XLA Ops:
  1.6 6.1 %copy-start.3 = (s32[4,28,16]{1,2,0:T(8,128)S(1)}, s32[4,28,16]{1,2,0:T(8,128)}, u32[]{:S(2)}) copy-start(s32[4,28,16]{1,2,0:T(8,128)} %param.9) | copy-start | bytes 21508
  1.6 7.3 %collective-permute-start = (bf16[256,128]{1,0:T(8,128)(2,1)}, bf16[256,128]{1,0:T(8,128)(2,1)}, u32[]{:S(2)}, u32[]{:S(2)}) collective-permute-start(bf16[256,128]{1,0:T(8,128)(2,1)} %get-tuple-element.34), channel_id=1, source_target_pairs={{0,2},{2,0},{4,6},{6,4},{8,10},{10,8},{12,14},{14,12},{16,18},{18,... | collective-permute-start | bytes 196616 | tf_op jit(solution)/shard_map/ppermute | solution.py:260
  4.6 4.6 %collective-permute-start.1 = (bf16[256,128]{1,0:T(8,128)(2,1)}, bf16[256,128]{1,0:T(8,128)(2,1)}, u32[]{:S(2)}, u32[]{:S(2)}) collective-permute-start(bf16[256,128]{1,0:T(8,128)(2,1)} %get-tuple-element.36), channel_id=1, source_target_pairs={{0,4},{2,6},{4,0},{6,2},{8,12},{10,14},{12,8},{14,10},{16,20},{18,... | collective-permute-start | bytes 196616 | tf_op jit(solution)/shard_map/ppermute | solution.py:260
  6.1 5.5 %collective-permute-start.2 = (bf16[256,128]{1,0:T(8,128)(2,1)}, bf16[256,128]{1,0:T(8,128)(2,1)}, u32[]{:S(2)}, u32[]{:S(2)}) collective-permute-start(bf16[256,128]{1,0:T(8,128)(2,1)} %get-tuple-element.35), channel_id=1, source_target_pairs={{0,6},{2,4},{4,2},{6,0},{8,14},{10,12},{12,10},{14,8},{16,22},{18,... | collective-permute-start | bytes 196616 | tf_op jit(solution)/shard_map/ppermute | solution.py:260
  8.0 32.5 %copy-start.1 = (bf16[128,128]{1,0:T(8,128)(2,1)S(1)}, bf16[128,128]{1,0:T(8,128)(2,1)}, u32[]{:S(2)}) copy-start(bf16[128,128]{1,0:T(8,128)(2,1)} %refs_13_.1) | copy-start | bytes 98308
  12.5 8.3 %collective-permute-start.3 = (bf16[1024,128]{1,0:T(8,128)(2,1)S(1)}, bf16[1024,128]{1,0:T(8,128)(2,1)S(1)}, u32[]{:S(2)}, u32[]{:S(2)}) collective-permute-start(bf16[1024,128]{1,0:T(8,128)(2,1)S(1)} %pad_maximum_fusion.refs_5_), channel_id=1, source_target_pairs={{0,8},{2,10},{4,12},{6,14},{8,16},{10,18},{12,20},{14,22},{16,24},... | collective-permute-start | bytes 786440 | tf_op jit(solution)/shard_map/ppermute | solution.py:277
  14.1 10.9 %collective-permute-start.5 = (bf16[272,896]{1,0:T(8,128)(2,1)S(1)}, bf16[272,896]{1,0:T(8,128)(2,1)S(1)}, u32[]{:S(2)}, u32[]{:S(2)}) collective-permute-start(bf16[272,896]{1,0:T(8,128)(2,1)S(1)} %get-tuple-element.19), channel_id=1, source_target_pairs={{0,2},{2,0},{4,6},{6,4},{8,10},{10,8},{12,14},{14,12},{16,18},{18,... | collective-permute-start | bytes 1462280 | tf_op jit(solution)/shard_map/ppermute | solution.py:260
  14.7 11.0 %collective-permute-start.6 = (bf16[272,896]{1,0:T(8,128)(2,1)S(1)}, bf16[272,896]{1,0:T(8,128)(2,1)S(1)}, u32[]{:S(2)}, u32[]{:S(2)}) collective-permute-start(bf16[272,896]{1,0:T(8,128)(2,1)S(1)} %get-tuple-element.20), channel_id=1, source_target_pairs={{0,4},{2,6},{4,0},{6,2},{8,12},{10,14},{12,8},{14,10},{16,20},{18,... | collective-permute-start | bytes 1462280 | tf_op jit(solution)/shard_map/ppermute | solution.py:260
  20.7 8.2 %collective-permute-start.4 = (bf16[1024,128]{1,0:T(8,128)(2,1)S(1)}, bf16[1024,128]{1,0:T(8,128)(2,1)S(1)}, u32[]{:S(2)}, u32[]{:S(2)}) collective-permute-start(bf16[1024,128]{1,0:T(8,128)(2,1)S(1)} %collective-permute-done.3.refs_6_), channel_id=1, source_target_pairs={{0,8},{2,10},{4,12},{6,14},{8,16},{10,18},{12,20},{14,22},{16,24},... | collective-permute-start | bytes 786440 | tf_op jit(solution)/shard_map/ppermute | solution.py:277
  28.9 8.2 %collective-permute-start.8 = (bf16[1024,128]{1,0:T(8,128)(2,1)S(1)}, bf16[1024,128]{1,0:T(8,128)(2,1)S(1)}, u32[]{:S(2)}, u32[]{:S(2)}) collective-permute-start(bf16[1024,128]{1,0:T(8,128)(2,1)S(1)} %collective-permute-done.4.refs_7_), channel_id=1, source_target_pairs={{0,8},{2,10},{4,12},{6,14},{8,16},{10,18},{12,20},{14,22},{16,24},... | collective-permute-start | bytes 786440 | tf_op jit(solution)/shard_map/ppermute | solution.py:277
  28.9 11.5 %collective-permute-start.7 = (bf16[272,896]{1,0:T(8,128)(2,1)}, bf16[272,896]{1,0:T(8,128)(2,1)S(1)}, u32[]{:S(2)}, u32[]{:S(2)}) collective-permute-start(bf16[272,896]{1,0:T(8,128)(2,1)} %get-tuple-element.23), channel_id=1, source_target_pairs={{0,6},{2,4},{4,2},{6,0},{8,14},{10,12},{12,10},{14,8},{16,22},{18,... | collective-permute-start | bytes 1462280 | tf_op jit(solution)/shard_map/ppermute | solution.py:260
  30.2 10.2 %collective-permute-start.9 = (bf16[1024,128]{1,0:T(8,128)(2,1)S(1)}, bf16[1024,128]{1,0:T(8,128)(2,1)S(1)}, u32[]{:S(2)}, u32[]{:S(2)}) collective-permute-start(bf16[1024,128]{1,0:T(8,128)(2,1)S(1)} %pad_maximum_fusion.refs_5_), channel_id=1, source_target_pairs={{0,1},{1,0},{2,3},{3,2},{4,5},{5,4},{6,7},{7,6},{8,9},{9,8},{10,11... | collective-permute-start | bytes 786440 | tf_op jit(solution)/shard_map/ppermute | solution.py:263
  30.2 10.2 %collective-permute-start.10 = (bf16[1024,128]{1,0:T(8,128)(2,1)S(1)}, bf16[1024,128]{1,0:T(8,128)(2,1)S(1)}, u32[]{:S(2)}, u32[]{:S(2)}) collective-permute-start(bf16[1024,128]{1,0:T(8,128)(2,1)S(1)} %collective-permute-done.3.refs_6_), channel_id=1, source_target_pairs={{0,1},{1,0},{2,3},{3,2},{4,5},{5,4},{6,7},{7,6},{8,9},{9,8},{10,11... | collective-permute-start | bytes 786440 | tf_op jit(solution)/shard_map/ppermute | solution.py:263
  30.7 9.7 %collective-permute-start.11 = (bf16[1024,128]{1,0:T(8,128)(2,1)S(1)}, bf16[1024,128]{1,0:T(8,128)(2,1)}, u32[]{:S(2)}, u32[]{:S(2)}) collective-permute-start(bf16[1024,128]{1,0:T(8,128)(2,1)S(1)} %collective-permute-done.4.refs_7_), channel_id=1, source_target_pairs={{0,1},{1,0},{2,3},{3,2},{4,5},{5,4},{6,7},{7,6},{8,9},{9,8},{10,11... | collective-permute-start | bytes 786440 | tf_op jit(solution)/shard_map/ppermute | solution.py:263
  37.1 3.3 %collective-permute-start.12 = (bf16[1024,128]{1,0:T(8,128)(2,1)S(1)}, bf16[1024,128]{1,0:T(8,128)(2,1)}, u32[]{:S(2)}, u32[]{:S(2)}) collective-permute-start(bf16[1024,128]{1,0:T(8,128)(2,1)S(1)} %collective-permute-done.8.refs_8_), channel_id=1, source_target_pairs={{0,1},{1,0},{2,3},{3,2},{4,5},{5,4},{6,7},{7,6},{8,9},{9,8},{10,11... | collective-permute-start | bytes 786440 | tf_op jit(solution)/shard_map/ppermute | solution.py:263
  40.4 0.9 %copy-start = (bf16[384,128]{1,0:T(8,128)(2,1)S(1)}, bf16[384,128]{1,0:T(8,128)(2,1)}, u32[]{:S(2)}) copy-start(bf16[384,128]{1,0:T(8,128)(2,1)} %refs_14_.1) | copy-start | bytes 294916
  66.7 0.6 copy-start.2
  67.3 4.7 %collective-permute-start.13 = (f32[8,128]{1,0:T(8,128)}, f32[8,128]{1,0:T(8,128)S(1)}, u32[]{:S(2)}, u32[]{:S(2)}) collective-permute-start(f32[8,128]{1,0:T(8,128)} %get-tuple-element.25), channel_id=1, source_target_pairs={{0,6},{2,4},{4,2},{6,0},{8,14},{10,12},{12,10},{14,8},{16,22},{18,... | collective-permute-start | bytes 12296 | tf_op jit(solution)/shard_map/ppermute | solution.py:260
  68.5 3.8 %collective-permute-start.14 = (f32[8,128]{1,0:T(8,128)}, f32[8,128]{1,0:T(8,128)S(1)}, u32[]{:S(2)}, u32[]{:S(2)}) collective-permute-start(f32[8,128]{1,0:T(8,128)} %get-tuple-element.26), channel_id=1, source_target_pairs={{0,4},{2,6},{4,0},{6,2},{8,12},{10,14},{12,8},{14,10},{16,20},{18,... | collective-permute-start | bytes 12296 | tf_op jit(solution)/shard_map/ppermute | solution.py:260
  69.7 3.8 %collective-permute-start.15 = (f32[8,128]{1,0:T(8,128)}, f32[8,128]{1,0:T(8,128)S(1)}, u32[]{:S(2)}, u32[]{:S(2)}) collective-permute-start(f32[8,128]{1,0:T(8,128)} %get-tuple-element.27), channel_id=1, source_target_pairs={{0,2},{2,0},{4,6},{6,4},{8,10},{10,8},{12,14},{14,12},{16,18},{18,... | collective-permute-start | bytes 12296 | tf_op jit(solution)/shard_map/ppermute | solution.py:260

commit v3 on v2

--- a/solution.py
+++ b/solution.py
@@ -11,6 +11,7 @@
 BLOCK = 64
 LANES = 128
 SEL_ROWS = 16
+SPLIT = 1
 NEG = -1e37
 
 
@@ -20,9 +21,9 @@
     q_in = refs[1 : 1 + n_piece]
     k_in = refs[1 + n_piece : 1 + n_piece + n_key]
     refs = refs[1 + n_piece + n_key :]
-    wq_ref, wk_ref = refs[:2]
+    wq_in, wk_in = refs[:2]
     out_refs = refs[2 : 2 + n_piece]
-    qbuf, kbuf, pool, qpool, teach, ms, ss, lv, sel_v, sel_s, sem_q, sem_k, sem_s = refs[2 + n_piece :]
+    qbuf, kbuf, pool, qpool, teach, ms, ss, lv, sel_v, sel_s, wq_ref, wk_ref, sem_q, sem_k, sem_s, sem_w = refs[2 + n_piece :]
     stride = q_in[0].shape[0]
     span = stride - SEL_ROWS
     span_blocks = span // BLOCK
@@ -37,23 +38,28 @@
     k_copies = [
         pltpu.make_async_copy(k_in[i], kbuf.at[pl.ds(i * k_rows, k_rows)], sem_k.at[i]) for i in range(n_key)
     ]
-    for copy in q_copies + k_copies:
+    w_copies = [
+        pltpu.make_async_copy(wq_in, wq_ref, sem_w.at[0]),
+        pltpu.make_async_copy(wk_in, wk_ref, sem_w.at[1]),
+    ]
+    for copy in q_copies + k_copies + w_copies:
         copy.start()
-    ms[...] = jnp.full(ms.shape, NEG, jnp.float32)
-    ss[...] = jnp.zeros(ss.shape, jnp.float32)
-    lv[...] = jnp.full(lv.shape, -1, jnp.int32)
     for copy in q_copies:
         copy.wait()
 
     lane = lax.broadcasted_iota(jnp.int32, (1, LANES), 1)
-    sub = lax.broadcasted_iota(jnp.int32, (SEL_ROWS, 1), 0)
+    sub = lax.broadcasted_iota(jnp.int32, (8, 1), 0)
+    listed = lane < heads * n_sel
+    group = lax.broadcasted_iota(jnp.int32, (LANES, 1), 0) // n_sel + heads * n_sel == lane
     for i in range(n_piece):
-        for h in range(heads):
-            at = slice(h * head_size, h * head_size + LANES)
-            mine = qbuf[i * stride + span : (i + 1) * stride, at].astype(jnp.int32)
-            own = jnp.where((mine == sub) & (lane < n_sel), 1, 0)
-            own = jnp.max(own, axis=1, keepdims=True)
-            sel_v[i, :, h * LANES : (h + 1) * LANES] = jnp.where(lane == n_sel, own, mine)
+        mine = qbuf[i * stride + span : (i + 1) * stride, :LANES].astype(jnp.float32)[:8].astype(jnp.int32)
+        own = ((mine == sub) & listed).astype(jnp.float32).astype(jnp.bfloat16)
+        own = jnp.dot(own, group.astype(jnp.float32).astype(jnp.bfloat16), preferred_element_type=jnp.float32)
+        at = own.astype(jnp.int32)
+        for m in range(n_cand):
+            at = jnp.where((mine == m) & listed, cand_s[i * n_cand + m], at)
+        sel_v[i] = at
+        lv[i] = jnp.transpose(jnp.broadcast_to(at.astype(jnp.float32)[None], (LANES // 8, 8, LANES)).reshape(LANES, LANES)).astype(jnp.int32)
     sel_copy = pltpu.make_async_copy(sel_v, sel_s, sem_s)
     sel_copy.start()
     for copy in k_copies:
@@ -73,66 +79,88 @@
 
     low = lane < BLOCK
     zeros = jnp.zeros((BLOCK, head_size), jnp.bfloat16)
-
-    def pair_step(ph, t, u):
+    pairs = span_blocks // 2
+
+    def places(ph, t):
+        piece = ph // heads
+        head = ph - piece * heads
+        at = [
+            [sel_s[piece, 2 * t + half, head * n_sel + slot] for half in range(2)] for slot in range(n_sel)
+        ]
+        return at + [[cand_s[piece * n_cand + 2 * t + half] for half in range(2)]]
+
+    def pair_step(ph, t):
         piece = ph // heads
         head = ph - piece * heads
         q_at = pl.ds(pl.multiple_of(piece * stride + t * 2 * BLOCK, SEL_ROWS), 2 * BLOCK)
         q = qbuf[q_at, pl.ds(pl.multiple_of(head * head_size, head_size), head_size)]
         q0, q1 = q[:BLOCK], q[BLOCK:]
         row = ph * span_blocks + 2 * t
-        means = [jnp.sum(x.astype(jnp.float32), axis=0, keepdims=True) * (1.0 / BLOCK) for x in (q0, q1)]
-        qpool[pl.ds(row, 1), :] = means[0]
-        qpool[pl.ds(row + 1, 1), :] = means[1]
+        for half, x in enumerate((q0, q1)):
+            qpool[pl.ds(row + half, 1), :] = jnp.sum(x.astype(jnp.float32), axis=0, keepdims=True) * (1.0 / BLOCK)
         rhs = jnp.concatenate(
             [jnp.concatenate([q0, zeros], axis=1), jnp.concatenate([zeros, q1], axis=1)], axis=0
         )
-        tiles = []
-        for slot in range(n_slot):
-            halves = []
-            for half in range(2):
-                if slot < n_sel:
-                    place = sel_s[piece, 2 * t + half, head * LANES + slot]
-                else:
-                    place = 2 * t + half
-                at = cand_s[piece * n_cand + place]
-                lv[u, half, slot : slot + 1, :] = jnp.full((1, LANES), at, jnp.int32)
-                halves.append(kbuf[pl.ds(pl.multiple_of(at * BLOCK, BLOCK), BLOCK), :])
-            tiles.append(jnp.concatenate(halves, axis=1))
-        scores = lax.dot_general(
-            jnp.concatenate(tiles, axis=0),
-            rhs,
-            (((1,), (1,)), ((), ())),
-            preferred_element_type=jnp.float32,
+        lhs = jnp.concatenate(
+            [
+                jnp.concatenate(
+                    [kbuf[pl.ds(pl.multiple_of(at * BLOCK, BLOCK), BLOCK), :] for at in both], axis=1
+                )
+                for both in places(ph, t)
+            ],
+            axis=0,
         )
+        scores = lax.dot_general(lhs, rhs, (((1,), (1,)), ((), ())), preferred_element_type=jnp.float32)
+        at = ph * pairs + t
         for slot in range(n_slot):
             part = scores[slot * BLOCK : (slot + 1) * BLOCK]
             top = jnp.max(part, axis=0, keepdims=True)
-            total = jnp.sum(jnp.exp2((part - top) * exp_scale), axis=0, keepdims=True)
-            if slot == n_sel:
-                drop = [sel_s[piece, 2 * t + half, head * LANES + n_sel] for half in range(2)]
-                total = total * (1 - jnp.where(low, drop[0], drop[1])).astype(jnp.float32)
-            ms[u, slot : slot + 1, :] = top
-            ss[u, slot : slot + 1, :] = total
-        tops = ms[u]
-        weight = jnp.exp2((tops - jnp.max(tops, axis=0, keepdims=True)) * exp_scale) * ss[u]
+            ms[at, slot : slot + 1, :] = top
+            ss[at, slot : slot + 1, :] = jnp.sum(jnp.exp2((part - top) * exp_scale), axis=0, keepdims=True)
+
+    def head_step(ph, carry):
+        for t in range(pairs):
+            pair_step(ph, t)
+        return carry
+
+
+    slots = ms.shape[1]
+    slot_row = lax.broadcasted_iota(jnp.int32, (slots, 1), 0)
+
+    def combine(ph, t):
+        piece = ph // heads
+        head = ph - piece * heads
+        row = ph * span_blocks + 2 * t
+        at = ph * pairs + t
+        drop = [sel_s[piece, 2 * t + half, heads * n_sel + head] for half in range(2)]
+        keep = slot_row < jnp.where(low, n_slot - drop[0], n_slot - drop[1])
+        tops = jnp.where(keep, ms[at], NEG)
+        most = jnp.max(tops, axis=0, keepdims=True)
+        weight = jnp.where(keep, jnp.exp2((tops - most) * exp_scale) * ss[at], 0.0)
         share = weight / jnp.sum(weight, axis=0, keepdims=True)
         for half in range(2):
             mine = low if half == 0 else jnp.logical_not(low)
             mean = jnp.sum(jnp.where(mine, share, 0.0), axis=1, keepdims=True) * (1.0 / BLOCK)
+            column = lv[piece, pl.ds(pl.multiple_of(head * n_sel, n_sel), n_sel), 2 * t + half : 2 * t + half + 1]
+            own = jnp.full((slots - n_sel, 1), cand_s[piece * n_cand + 2 * t + half], jnp.int32)
+            column = jnp.concatenate([column, own], axis=0)
             for c in range(blocks // LANES):
-                hit = lv[u, half] == lane + c * LANES
+                hit = column == lane + c * LANES
                 teach[c, pl.ds(row + half, 1), :] = jnp.sum(
                     jnp.where(hit, mean, 0.0), axis=0, keepdims=True
                 )
 
-    def head_step(ph, carry):
-        for t in range(span_blocks // 2):
-            pair_step(ph, t, t)
+    def combine_step(ph, carry):
+        for t in range(pairs):
+            combine(ph, t)
+        head_step(jnp.minimum(ph + 1, n_piece * heads - 1), 0)
         return carry
 
-    lax.fori_loop(0, n_piece * heads, head_step, 0)
-
+    head_step(0, 0)
+    lax.fori_loop(0, n_piece * heads, combine_step, 0, unroll=4)
+
+    for copy in w_copies:
+        copy.wait()
     k_gate = jnp.dot(
         pool[...].astype(jnp.bfloat16), wk_ref[...], preferred_element_type=jnp.float32
     ).astype(jnp.bfloat16)
@@ -149,7 +177,7 @@
     safe = jnp.where(positive, teacher, 1.0)
     kl = jnp.sum(jnp.where(positive, teacher * (jnp.log(safe) - log_gate), 0.0), axis=1, keepdims=True)
     r = lax.broadcasted_iota(jnp.int32, (rows, 1), 0)
-    spread = jnp.where(r // span_blocks % heads == lane, kl, 0.0)
+    spread = jnp.where(r // span_blocks % heads + cand_s[n_piece * n_cand] == lane, kl, 0.0)
     r = lax.broadcasted_iota(jnp.int32, (1, rows), 1)
     b = lax.broadcasted_iota(jnp.int32, (8, 1), 0)
     for i in range(n_piece):
@@ -168,7 +196,6 @@
     blocks = len(k_pieces) * k_pieces[0].shape[0] // BLOCK
     rows = n_piece * heads * span_blocks
     dims = (n_piece, len(k_pieces), heads, n_sel, n_cand, blocks, head_size)
-    unroll = span_blocks // 2
     slots = -(-(n_sel + 1) // 8) * 8
     smem = pl.BlockSpec(memory_space=pltpu.SMEM)
     hbm = pl.BlockSpec(memory_space=pl.ANY)
@@ -176,7 +203,7 @@
     return pl.pallas_call(
         functools.partial(gate_kernel, dims),
         out_shape=[jax.ShapeDtypeStruct((8, LANES), jnp.float32)] * n_piece,
-        in_specs=[smem] + [hbm] * (n_piece + len(k_pieces)) + [vmem] * 2,
+        in_specs=[smem] + [hbm] * (n_piece + len(k_pieces) + 2),
         out_specs=[vmem] * n_piece,
         scratch_shapes=[
             pltpu.VMEM((n_piece * stride, heads * head_size), jnp.bfloat16),
@@ -184,14 +211,17 @@
             pltpu.VMEM((blocks, 3 * head_size), jnp.float32),
             pltpu.VMEM((rows, head_size), jnp.float32),
             pltpu.VMEM((blocks // LANES, rows, LANES), jnp.float32),
-            pltpu.VMEM((unroll, slots, LANES), jnp.float32),
-            pltpu.VMEM((unroll, slots, LANES), jnp.float32),
-            pltpu.VMEM((unroll, 2, slots, LANES), jnp.int32),
-            pltpu.VMEM((n_piece, SEL_ROWS, heads * LANES), jnp.int32),
-            pltpu.SMEM((n_piece, SEL_ROWS, heads * LANES), jnp.int32),
+            pltpu.VMEM((rows // 2, slots, LANES), jnp.float32),
+            pltpu.VMEM((rows // 2, slots, LANES), jnp.float32),
+            pltpu.VMEM((n_piece, LANES, LANES), jnp.int32),
+            pltpu.VMEM((n_piece, 8, LANES), jnp.int32),
+            pltpu.SMEM((n_piece, 8, LANES), jnp.int32),
+            pltpu.VMEM(w_query.shape, w_query.dtype),
+            pltpu.VMEM(key_gate_weight.shape, key_gate_weight.dtype),
             pltpu.SemaphoreType.DMA((n_piece,)),
             pltpu.SemaphoreType.DMA((len(k_pieces),)),
             pltpu.SemaphoreType.DMA(()),
+            pltpu.SemaphoreType.DMA((2,)),
         ],
         compiler_params=pltpu.CompilerParams(vmem_limit_bytes=40 * 1024 * 1024),
     )(cand, *q_pieces, *k_pieces, w_query, key_gate_weight)
@@ -234,14 +264,17 @@
             )
         )
     n_cand = candidates[0].shape[0]
-    cand = place_of(jnp.stack(candidates)).astype(jnp.int32).reshape(-1)
-
+    first_lane = spot * heads if ring else 0
+    cand = jnp.concatenate(
+        [place_of(jnp.concatenate(candidates)).astype(jnp.int32), jnp.full((1,), first_lane, jnp.int32)]
+    )
+
+    width = heads * head_size
     sel_rows = jnp.pad(
-        selected.astype(jnp.bfloat16),
-        ((0, SEL_ROWS - span_blocks), (0, 0), (0, head_size - n_sel)),
+        selected.astype(jnp.bfloat16).reshape(span_blocks, kv_heads, heads * n_sel),
+        ((0, SEL_ROWS - span_blocks), (0, 0), (0, width - heads * n_sel)),
     ).reshape(SEL_ROWS, q_heads * head_size)
     sent = jnp.concatenate([queries, sel_rows], axis=0)
-    width = heads * head_size
 
     if not ring:
         gathered = lax.all_gather(key_state_rows, ("ctx", "pair"), axis=0, tiled=True)
@@ -267,25 +300,24 @@
         for p in range(plane)
     ]
     parts = [lax.dynamic_slice_in_dim(sent, (spot ^ p) * width, width, 1) for p in range(plane)]
-    steps = [jnp.concatenate(keys, axis=0)]
-    steps[0], parts = lax.optimization_barrier((steps[0], parts))
+    per = plane // SPLIT
+    streams = [[jnp.concatenate(keys[i * per : (i + 1) * per], axis=0)] for i in range(SPLIT)]
+    heads_of, parts = lax.optimization_barrier(([x[0] for x in streams], parts))
+    streams = [[x] for x in heads_of]
     pieces = [flipped(x, p) for p, x in enumerate(parts)]
     for i in range(layers - 1):
         if i == 2:
-            steps[2], pieces[1:3] = lax.optimization_barrier((steps[2], pieces[1:3]))
-        steps.append(
-            lax.ppermute(steps[-1], "ctx", [(i, (i + plane) % n_ctx) for i in range(n_ctx)])
-        )
-    k_pieces = steps + [other_core(x) for x in steps]
+            tied = ([x[i] for x in streams], pieces[1:3], cand)
+            heads_of, pieces[1:3], cand = lax.optimization_barrier(tied)
+            for x, y in zip(streams, heads_of):
+                x[i] = y
+        for x in streams:
+            x.append(lax.ppermute(x[i], "ctx", [(j, (j + plane) % n_ctx) for j in range(n_ctx)]))
+    mine = [x[i] for i in range(layers) for x in streams]
+    k_pieces = mine + [other_core(x) for x in mine]
     outs = gate_call(cand, pieces, k_pieces, w_query, key_gate_weight, heads, n_sel, n_cand)
-    back = [flipped(x, p)[:span_blocks, :heads] for p, x in enumerate(outs)]
-    columns = []
-    for g in range(plane):
-        column = back[0]
-        for p in range(1, plane):
-            column = jnp.where(spot ^ g == p, back[p], column)
-        columns.append(column)
-    return jnp.concatenate(columns, axis=1)
+    back = [flipped(x, p) for p, x in enumerate(outs)]
+    return functools.reduce(jnp.add, back)[:span_blocks, :q_heads]
 
 
 def solution(mesh):

time: 76 us -> 63 us (0.83)
  Pallas kernels: 25.4 us -> 15.7 us
  other arithmetic: 5.66 us -> 1.07 us
  starting transfers between devices: 12.4 us -> 14.6 us
  local copies, waits for them, and re-layouts: 8.03 us -> 6.01 us
  waiting for transfers between devices: 23.9 us -> 25.2 us
    pallas_call x1, Pallas kernels: 25.4 us -> 15.7 us  [gate_call(): pl.pallas_call(functools.partial(gate_kernel, dims), out_shape=[jax.Shape...]
    ppermute x9, waiting for transfers between devices: 8.79 us -> 12.4 us  [flipped(): lax.ppermute(x, 'ctx', [(i, i ^ p) for i in range(n_ctx)])]
    ppermute x3, waiting for transfers between devices: 15.1 us -> 12.7 us  [per_device(): lax.ppermute(x[i], 'ctx', [(j, (j + plane) % n_ctx) for j in range(n_ctx)])]
    ppermute x9, starting transfers between devices: 10.2 us -> 12.5 us  [flipped(): lax.ppermute(x, 'ctx', [(i, i ^ p) for i in range(n_ctx)])]
    another operation x3 -> x0, other arithmetic: 1.98 us -> none  [per_device(): cand = place_of(jnp.stack(candidates)).astype(jnp.int32).reshape(-1)]
    unnamed x10, local copies, waits for them, and re-layouts: 3.2 us -> 1.65 us
    select_n x2 -> x0, other arithmetic: 1.36 us -> none  [per_device(): column = jnp.where(spot ^ g == p, back[p], column)]
    another operation x1 -> x0, local copies, waits for them, and re-layouts: 1.34 us -> none  [per_device(): cand = place_of(jnp.stack(candidates)).astype(jnp.int32).reshape(-1)]
  transfers between devices with their start and end apart: 16 -> 16, of which waited for: 10 -> 11; matrix products, arithmetic and copies ran while one was open for 10% -> 6% of each run, Pallas kernels for 0% -> 0%
where the time goes in v3:
time: 63 us; the launch traced here: 62.8 us
  waiting for transfers between devices  25.2 us (40%)
  Pallas kernels  15.7 us (25%)
  starting transfers between devices  14.6 us (23%)
  local copies, waits for them, and re-layouts  6.01 us (10%)
  other arithmetic  1.07 us (2%)
    pallas_call x1, Pallas kernels, gate_call(): pl.pallas_call(functools.partial(gate_kernel, dims), out_shape=[jax.Shape...  15.7 us
    ppermute x3, waiting for transfers between devices, per_device(): lax.ppermute(x[i], 'ctx', [(j, (j + plane) % n_ctx) for j in range(n_ctx)])  12.7 us
    ppermute x9, starting transfers between devices, flipped(): lax.ppermute(x, 'ctx', [(i, i ^ p) for i in range(n_ctx)])  12.5 us
    ppermute x9, waiting for transfers between devices, flipped(): lax.ppermute(x, 'ctx', [(i, i ^ p) for i in range(n_ctx)])  12.4 us
    unnamed x10, local copies, waits for them, and re-layouts  1.65 us
    ppermute x3, starting transfers between devices, per_device(): lax.ppermute(x[i], 'ctx', [(j, (j + plane) % n_ctx) for j in range(n_ctx)])  1.63 us
    dynamic_slice x1, local copies, waits for them, and re-layouts, per_device(): lax.dynamic_slice_in_dim(key_state_rows, (spot ^ p) * head_size, head_siz...  1.63 us
  transfers between devices with their start and end apart: 16, of which 11 were waited for; matrix products, arithmetic and copies ran while one was open for 6% of the time, Pallas kernels for 0%

profile of v3, /device:TPU:0, one launch (start us, length us, event | category | flops | bytes accessed | tf_op | source)
XLA Modules:
  0.0 62.8 jit_solution(9440253141515113250)
XLA Ops:
  0.0 1.6 %constant_dynamic-slice_fusion.11 = (bf16[256,128]{1,0:T(8,128)(2,1)}, bf16[256,128]{1,0:T(8,128)(2,1)}, bf16[256,128]{1,0:T(8,128)(2,1)}, bf16[256,128]{1,0:T(8,128)(2,1)}) fusion(bf16[256,512]{1,0:T(8,128)(2,1)} %param.7, s32[]{:T(128)S(6)} %select_n.78, s32[]{:T(128)S(6)} %select_n.79, s32[]{:T(128)S(6)} %select_n.81, s32[]{:T(128)S(6)} %select_n.80), kind=kLoop, calls=%fused_computation.15 | loop fusion | bytes 524304 | tf_op jit(solution)/shard_map/dynamic_slice | solution.py:299
  1.6 3.9 %collective-permute-start.2 = (bf16[256,128]{1,0:T(8,128)(2,1)}, bf16[256,128]{1,0:T(8,128)(2,1)}, u32[]{:S(2)}, u32[]{:S(2)}) collective-permute-start(bf16[256,128]{1,0:T(8,128)(2,1)} %get-tuple-element.37), channel_id=1, source_target_pairs={{0,6},{2,4},{4,2},{6,0},{8,14},{10,12},{12,10},{14,8},{16,22},{18,... | collective-permute-start | bytes 196616 | tf_op jit(solution)/shard_map/ppermute | solution.py:293
  6.2 1.6 %constant_dynamic-update-slice_fusion.1 = bf16[272,3584]{1,0:T(8,128)(2,1)S(1)} fusion(bf16[256,3584]{1,0:T(8,128)(2,1)} %param.6), kind=kLoop, calls=%fused_computation.2 | loop fusion | bytes 3670016
  8.2 1.0 %constant_dynamic-slice_fusion.4 = (bf16[272,896]{1,0:T(8,128)(2,1)S(1)}, bf16[272,896]{1,0:T(8,128)(2,1)S(1)}, bf16[272,896]{1,0:T(8,128)(2,1)}, bf16[272,896]{1,0:T(8,128)(2,1)S(1)}) fusion(bf16[272,3584]{1,0:T(8,128)(2,1)S(1)} %constant_dynamic-update-slice_fusion, s32[]{:T(128)S(6)} %select_n.85, s32[]{:T(128)S(6)} %select_n.84, s32[]{:T(128)S(6)} %select_n.83, ...), kind=kLoop, calls=%fused_computation.8 | loop fusion | bytes 3899408 | tf_op jit(solution)/shard_map/dynamic_slice | solution.py:302
  9.2 1.0 %collective-permute-done.1 = bf16[256,128]{1,0:T(8,128)(2,1)} collective-permute-done((bf16[256,128]{1,0:T(8,128)(2,1)}, bf16[256,128]{1,0:T(8,128)(2,1)}, u32[]{:S(2)}, u32[]{:S(2)}) %collective-permute-start.1) | collective-permute-done | bytes 65568 | tf_op jit(solution)/shard_map/ppermute | solution.py:293
  10.6 0.9 %pad_maximum_fusion.refs_5_ = bf16[1024,128]{1,0:T(8,128)(2,1)S(1)} fusion(bf16[256,128]{1,0:T(8,128)(2,1)} %collective-permute-done.2, bf16[256,128]{1,0:T(8,128)(2,1)} %collective-permute-done.1, bf16[256,128]{1,0:T(8,128)(2,1)} %collective-permute-done, bf16[256,128]{1,0:T(8,128)(2,1)S(1)} %copy-done.2), kind=kLoop, calls=%fused_computation | loop fusion | flops 1048576 | bytes 524288 | tf_op jit(solution)/shard_map/concatenate | solution.py:304
  11.5 1.6 %collective-permute-start.3 = (bf16[1024,128]{1,0:T(8,128)(2,1)S(1)}, bf16[1024,128]{1,0:T(8,128)(2,1)S(1)}, u32[]{:S(2)}, u32[]{:S(2)}) collective-permute-start(bf16[1024,128]{1,0:T(8,128)(2,1)S(1)} %pad_maximum_fusion.refs_5_), channel_id=1, source_target_pairs={{0,8},{2,10},{4,12},{6,14},{8,16},{10,18},{12,20},{14,22},{16,24},... | collective-permute-start | bytes 786440 | tf_op jit(solution)/shard_map/ppermute | solution.py:315
  13.2 0.5 collective-permute-start.5
  13.7 1.5 %collective-permute-start.6 = (bf16[272,896]{1,0:T(8,128)(2,1)S(1)}, bf16[272,896]{1,0:T(8,128)(2,1)S(1)}, u32[]{:S(2)}, u32[]{:S(2)}) collective-permute-start(bf16[272,896]{1,0:T(8,128)(2,1)S(1)} %get-tuple-element.20), channel_id=1, source_target_pairs={{0,4},{2,6},{4,0},{6,2},{8,12},{10,14},{12,8},{14,10},{16,20},{18,... | collective-permute-start | bytes 1462280 | tf_op jit(solution)/shard_map/ppermute | solution.py:293
  15.2 0.8 %fusion.9 = (s32[31]{0:T(128)S(1)}, s32[31]{0:T(128)S(1)}, s32[31]{0:T(128)S(1)}, s32[31]{0:T(128)S(1)}) fusion(s32[32,31]{1,0:T(8,128)} %param.8, s32[]{:T(128)S(6)} %select_n.89, s32[]{:T(128)S(6)} %select_n.87, s32[]{:T(128)S(6)} %select_n.86, s32[]{:T(128)S(6)} %select_n.88), kind=kLoop, calls=%fused_computation.44 | loop fusion | bytes 1008 | tf_op jit(solution)/shard_map/jit(dynamic_index_in_dim)/squeeze | solution.py:260
  16.2 4.0 %collective-permute-done.3.refs_6_ = bf16[1024,128]{1,0:T(8,128)(2,1)S(1)} collective-permute-done((bf16[1024,128]{1,0:T(8,128)(2,1)S(1)}, bf16[1024,128]{1,0:T(8,128)(2,1)S(1)}, u32[]{:S(2)}, u32[]{:S(2)}) %collective-permute-start.3) | collective-permute-done | bytes 262176 | tf_op jit(solution)/shard_map/ppermute | solution.py:315
  20.3 4.4 %collective-permute-done.5.refs_2_ = bf16[272,896]{1,0:T(8,128)(2,1)S(1)} collective-permute-done((bf16[272,896]{1,0:T(8,128)(2,1)}, bf16[272,896]{1,0:T(8,128)(2,1)S(1)}, u32[]{:S(2)}, u32[]{:S(2)}) %collective-permute-start.5) | collective-permute-done | bytes 487456 | tf_op jit(solution)/shard_map/ppermute | solution.py:293
  24.7 0.7 %collective-permute-done.6.refs_3_ = bf16[272,896]{1,0:T(8,128)(2,1)S(1)} collective-permute-done((bf16[272,896]{1,0:T(8,128)(2,1)S(1)}, bf16[272,896]{1,0:T(8,128)(2,1)S(1)}, u32[]{:S(2)}, u32[]{:S(2)}) %collective-permute-start.6) | collective-permute-done | bytes 487456 | tf_op jit(solution)/shard_map/ppermute | solution.py:293
  25.4 3.0 %collective-permute-done.4.refs_7_ = bf16[1024,128]{1,0:T(8,128)(2,1)S(1)} collective-permute-done((bf16[1024,128]{1,0:T(8,128)(2,1)S(1)}, bf16[1024,128]{1,0:T(8,128)(2,1)S(1)}, u32[]{:S(2)}, u32[]{:S(2)}) %collective-permute-start.4) | collective-permute-done | bytes 262176 | tf_op jit(solution)/shard_map/ppermute | solution.py:315
  28.4 1.9 %collective-permute-start.7 = (bf16[272,896]{1,0:T(8,128)(2,1)S(1)}, bf16[272,896]{1,0:T(8,128)(2,1)S(1)}, u32[]{:S(2)}, u32[]{:S(2)}) collective-permute-start(bf16[272,896]{1,0:T(8,128)(2,1)S(1)} %get-tuple-element.25), channel_id=1, source_target_pairs={{0,6},{2,4},{4,2},{6,0},{8,14},{10,12},{12,10},{14,8},{16,22},{18,... | collective-permute-start | bytes 1462280 | tf_op jit(solution)/shard_map/ppermute | solution.py:293
  30.8 5.8 %collective-permute-done.8.refs_8_ = bf16[1024,128]{1,0:T(8,128)(2,1)S(1)} collective-permute-done((bf16[1024,128]{1,0:T(8,128)(2,1)S(1)}, bf16[1024,128]{1,0:T(8,128)(2,1)S(1)}, u32[]{:S(2)}, u32[]{:S(2)}) %collective-permute-start.8) | collective-permute-done | bytes 262176 | tf_op jit(solution)/shard_map/ppermute | solution.py:315
  36.5 2.3 %collective-permute-done.7.refs_4_ = bf16[272,896]{1,0:T(8,128)(2,1)S(1)} collective-permute-done((bf16[272,896]{1,0:T(8,128)(2,1)S(1)}, bf16[272,896]{1,0:T(8,128)(2,1)S(1)}, u32[]{:S(2)}, u32[]{:S(2)}) %collective-permute-start.7) | collective-permute-done | bytes 487456 | tf_op jit(solution)/shard_map/ppermute | solution.py:293
  38.9 15.7 %shard_map.64 = (f32[8,128]{1,0:T(8,128)S(1)}, f32[8,128]{1,0:T(8,128)S(1)}, f32[8,128]{1,0:T(8,128)S(1)}, f32[8,128]{1,0:T(8,128)S(1)}) custom-call(s32[157]{0:T(256)S(1)} %pad_add_fusion.refs_0_, bf16[272,896]{1,0:T(8,128)(2,1)S(1)} %get-tuple-element.22.refs_1_, bf16[272,896]{1,0:T(8,128)(2,1)S(1)} %collective-permute-done.5.refs_2_, ...), custom_call_target="tpu_custom_call" | custom-call | tf_op jit(solution)/shard_map/pallas_call | solution.py:203
  54.6 2.4 %collective-permute-start.15 = (f32[8,128]{1,0:T(8,128)S(1)}, f32[8,128]{1,0:T(8,128)S(1)}, u32[]{:S(2)}, u32[]{:S(2)}) collective-permute-start(f32[8,128]{1,0:T(8,128)S(1)} %get-tuple-element.30), channel_id=1, source_target_pairs={{0,6},{2,4},{4,2},{6,0},{8,14},{10,12},{12,10},{14,8},{16,22},{18,... | collective-permute-start | bytes 12296 | tf_op jit(solution)/shard_map/ppermute | solution.py:293
  56.9 1.6 %collective-permute-start.14 = (f32[8,128]{1,0:T(8,128)S(1)}, f32[8,128]{1,0:T(8,128)S(1)}, u32[]{:S(2)}, u32[]{:S(2)}) collective-permute-start(f32[8,128]{1,0:T(8,128)S(1)} %get-tuple-element.29), channel_id=1, source_target_pairs={{0,4},{2,6},{4,0},{6,2},{8,12},{10,14},{12,8},{14,10},{16,20},{18,... | collective-permute-start | bytes 12296 | tf_op jit(solution)/shard_map/ppermute | solution.py:293
  58.6 0.6 collective-permute-done.15
  59.1 1.4 %collective-permute-done.14 = f32[8,128]{1,0:T(8,128)S(1)} collective-permute-done((f32[8,128]{1,0:T(8,128)S(1)}, f32[8,128]{1,0:T(8,128)S(1)}, u32[]{:S(2)}, u32[]{:S(2)}) %collective-permute-start.14) | collective-permute-done | bytes 4128 | tf_op jit(solution)/shard_map/ppermute | solution.py:293
  60.5 1.6 %collective-permute-done.13 = f32[8,128]{1,0:T(8,128)S(1)} collective-permute-done((f32[8,128]{1,0:T(8,128)S(1)}, f32[8,128]{1,0:T(8,128)S(1)}, u32[]{:S(2)}, u32[]{:S(2)}) %collective-permute-start.13) | collective-permute-done | bytes 4128 | tf_op jit(solution)/shard_map/ppermute | solution.py:293
  62.2 0.6 slice.3
  (37 shorter events, 2.2 us)
Async XLA Ops:
  1.6 6.1 %copy-start.3 = (s32[4,28,16]{1,2,0:T(8,128)S(1)}, s32[4,28,16]{1,2,0:T(8,128)}, u32[]{:S(2)}) copy-start(s32[4,28,16]{1,2,0:T(8,128)} %param.9) | copy-start | bytes 21508
  1.6 7.5 %collective-permute-start.2 = (bf16[256,128]{1,0:T(8,128)(2,1)}, bf16[256,128]{1,0:T(8,128)(2,1)}, u32[]{:S(2)}, u32[]{:S(2)}) collective-permute-start(bf16[256,128]{1,0:T(8,128)(2,1)} %get-tuple-element.37), channel_id=1, source_target_pairs={{0,6},{2,4},{4,2},{6,0},{8,14},{10,12},{12,10},{14,8},{16,22},{18,... | collective-permute-start | bytes 196616 | tf_op jit(solution)/shard_map/ppermute | solution.py:293
  5.5 4.6 %collective-permute-start.1 = (bf16[256,128]{1,0:T(8,128)(2,1)}, bf16[256,128]{1,0:T(8,128)(2,1)}, u32[]{:S(2)}, u32[]{:S(2)}) collective-permute-start(bf16[256,128]{1,0:T(8,128)(2,1)} %get-tuple-element.38), channel_id=1, source_target_pairs={{0,4},{2,6},{4,0},{6,2},{8,12},{10,14},{12,8},{14,10},{16,20},{18,... | collective-permute-start | bytes 196616 | tf_op jit(solution)/shard_map/ppermute | solution.py:293
  6.0 4.6 %collective-permute-start = (bf16[256,128]{1,0:T(8,128)(2,1)}, bf16[256,128]{1,0:T(8,128)(2,1)}, u32[]{:S(2)}, u32[]{:S(2)}) collective-permute-start(bf16[256,128]{1,0:T(8,128)(2,1)} %get-tuple-element.36), channel_id=1, source_target_pairs={{0,2},{2,0},{4,6},{6,4},{8,10},{10,8},{12,14},{14,12},{16,18},{18,... | collective-permute-start | bytes 196616 | tf_op jit(solution)/shard_map/ppermute | solution.py:293
  8.2 2.5 %copy-start.2 = (bf16[256,128]{1,0:T(8,128)(2,1)S(1)}, bf16[256,128]{1,0:T(8,128)(2,1)}, u32[]{:S(2)}) copy-start(bf16[256,128]{1,0:T(8,128)(2,1)} %get-tuple-element.35) | copy-start | bytes 196612
  8.2 30.7 %copy-start = (bf16[384,128]{1,0:T(8,128)(2,1)S(1)}, bf16[384,128]{1,0:T(8,128)(2,1)}, u32[]{:S(2)}) copy-start(bf16[384,128]{1,0:T(8,128)(2,1)} %refs_14_.1) | copy-start | bytes 294916
  8.2 30.7 %copy-start.1 = (bf16[128,128]{1,0:T(8,128)(2,1)S(1)}, bf16[128,128]{1,0:T(8,128)(2,1)}, u32[]{:S(2)}) copy-start(bf16[128,128]{1,0:T(8,128)(2,1)} %refs_13_.1) | copy-start | bytes 98308
  11.5 8.7 %collective-permute-start.3 = (bf16[1024,128]{1,0:T(8,128)(2,1)S(1)}, bf16[1024,128]{1,0:T(8,128)(2,1)S(1)}, u32[]{:S(2)}, u32[]{:S(2)}) collective-permute-start(bf16[1024,128]{1,0:T(8,128)(2,1)S(1)} %pad_maximum_fusion.refs_5_), channel_id=1, source_target_pairs={{0,8},{2,10},{4,12},{6,14},{8,16},{10,18},{12,20},{14,22},{16,24},... | collective-permute-start | bytes 786440 | tf_op jit(solution)/shard_map/ppermute | solution.py:315
  13.2 11.5 %collective-permute-start.5 = (bf16[272,896]{1,0:T(8,128)(2,1)}, bf16[272,896]{1,0:T(8,128)(2,1)S(1)}, u32[]{:S(2)}, u32[]{:S(2)}) collective-permute-start(bf16[272,896]{1,0:T(8,128)(2,1)} %get-tuple-element.19), channel_id=1, source_target_pairs={{0,2},{2,0},{4,6},{6,4},{8,10},{10,8},{12,14},{14,12},{16,18},{18,... | collective-permute-start | bytes 1462280 | tf_op jit(solution)/shard_map/ppermute | solution.py:293
  13.7 11.7 %collective-permute-start.6 = (bf16[272,896]{1,0:T(8,128)(2,1)S(1)}, bf16[272,896]{1,0:T(8,128)(2,1)S(1)}, u32[]{:S(2)}, u32[]{:S(2)}) collective-permute-start(bf16[272,896]{1,0:T(8,128)(2,1)S(1)} %get-tuple-element.20), channel_id=1, source_target_pairs={{0,4},{2,6},{4,0},{6,2},{8,12},{10,14},{12,8},{14,10},{16,20},{18,... | collective-permute-start | bytes 1462280 | tf_op jit(solution)/shard_map/ppermute | solution.py:293
  20.2 8.2 %collective-permute-start.4 = (bf16[1024,128]{1,0:T(8,128)(2,1)S(1)}, bf16[1024,128]{1,0:T(8,128)(2,1)S(1)}, u32[]{:S(2)}, u32[]{:S(2)}) collective-permute-start(bf16[1024,128]{1,0:T(8,128)(2,1)S(1)} %collective-permute-done.3.refs_6_), channel_id=1, source_target_pairs={{0,8},{2,10},{4,12},{6,14},{8,16},{10,18},{12,20},{14,22},{16,24},... | collective-permute-start | bytes 786440 | tf_op jit(solution)/shard_map/ppermute | solution.py:315
  28.4 8.2 %collective-permute-start.8 = (bf16[1024,128]{1,0:T(8,128)(2,1)S(1)}, bf16[1024,128]{1,0:T(8,128)(2,1)S(1)}, u32[]{:S(2)}, u32[]{:S(2)}) collective-permute-start(bf16[1024,128]{1,0:T(8,128)(2,1)S(1)} %collective-permute-done.4.refs_7_), channel_id=1, source_target_pairs={{0,8},{2,10},{4,12},{6,14},{8,16},{10,18},{12,20},{14,22},{16,24},... | collective-permute-start | bytes 786440 | tf_op jit(solution)/shard_map/ppermute | solution.py:315
  28.4 10.5 %collective-permute-start.7 = (bf16[272,896]{1,0:T(8,128)(2,1)S(1)}, bf16[272,896]{1,0:T(8,128)(2,1)S(1)}, u32[]{:S(2)}, u32[]{:S(2)}) collective-permute-start(bf16[272,896]{1,0:T(8,128)(2,1)S(1)} %get-tuple-element.25), channel_id=1, source_target_pairs={{0,6},{2,4},{4,2},{6,0},{8,14},{10,12},{12,10},{14,8},{16,22},{18,... | collective-permute-start | bytes 1462280 | tf_op jit(solution)/shard_map/ppermute | solution.py:293
  30.3 6.3 %collective-permute-start.9 = (bf16[1024,128]{1,0:T(8,128)(2,1)S(1)}, bf16[1024,128]{1,0:T(8,128)(2,1)S(1)}, u32[]{:S(2)}, u32[]{:S(2)}) collective-permute-start(bf16[1024,128]{1,0:T(8,128)(2,1)S(1)} %pad_maximum_fusion.refs_5_), channel_id=1, source_target_pairs={{0,1},{1,0},{2,3},{3,2},{4,5},{5,4},{6,7},{7,6},{8,9},{9,8},{10,11... | collective-permute-start | bytes 786440 | tf_op jit(solution)/shard_map/ppermute | solution.py:296
  30.3 8.6 %collective-permute-start.10 = (bf16[1024,128]{1,0:T(8,128)(2,1)S(1)}, bf16[1024,128]{1,0:T(8,128)(2,1)S(1)}, u32[]{:S(2)}, u32[]{:S(2)}) collective-permute-start(bf16[1024,128]{1,0:T(8,128)(2,1)S(1)} %collective-permute-done.3.refs_6_), channel_id=1, source_target_pairs={{0,1},{1,0},{2,3},{3,2},{4,5},{5,4},{6,7},{7,6},{8,9},{9,8},{10,11... | collective-permute-start | bytes 786440 | tf_op jit(solution)/shard_map/ppermute | solution.py:296
  30.8 8.0 %collective-permute-start.11 = (bf16[1024,128]{1,0:T(8,128)(2,1)S(1)}, bf16[1024,128]{1,0:T(8,128)(2,1)S(1)}, u32[]{:S(2)}, u32[]{:S(2)}) collective-permute-start(bf16[1024,128]{1,0:T(8,128)(2,1)S(1)} %collective-permute-done.4.refs_7_), channel_id=1, source_target_pairs={{0,1},{1,0},{2,3},{3,2},{4,5},{5,4},{6,7},{7,6},{8,9},{9,8},{10,11... | collective-permute-start | bytes 786440 | tf_op jit(solution)/shard_map/ppermute | solution.py:296
  36.5 2.3 %collective-permute-start.12 = (bf16[1024,128]{1,0:T(8,128)(2,1)S(1)}, bf16[1024,128]{1,0:T(8,128)(2,1)S(1)}, u32[]{:S(2)}, u32[]{:S(2)}) collective-permute-start(bf16[1024,128]{1,0:T(8,128)(2,1)S(1)} %collective-permute-done.8.refs_8_), channel_id=1, source_target_pairs={{0,1},{1,0},{2,3},{3,2},{4,5},{5,4},{6,7},{7,6},{8,9},{9,8},{10,11... | collective-permute-start | bytes 786440 | tf_op jit(solution)/shard_map/ppermute | solution.py:296
  54.6 4.6 %collective-permute-start.15 = (f32[8,128]{1,0:T(8,128)S(1)}, f32[8,128]{1,0:T(8,128)S(1)}, u32[]{:S(2)}, u32[]{:S(2)}) collective-permute-start(f32[8,128]{1,0:T(8,128)S(1)} %get-tuple-element.30), channel_id=1, source_target_pairs={{0,6},{2,4},{4,2},{6,0},{8,14},{10,12},{12,10},{14,8},{16,22},{18,... | collective-permute-start | bytes 12296 | tf_op jit(solution)/shard_map/ppermute | solution.py:293
  56.9 3.6 %collective-permute-start.14 = (f32[8,128]{1,0:T(8,128)S(1)}, f32[8,128]{1,0:T(8,128)S(1)}, u32[]{:S(2)}, u32[]{:S(2)}) collective-permute-start(f32[8,128]{1,0:T(8,128)S(1)} %get-tuple-element.29), channel_id=1, source_target_pairs={{0,4},{2,6},{4,0},{6,2},{8,12},{10,14},{12,8},{14,10},{16,20},{18,... | collective-permute-start | bytes 12296 | tf_op jit(solution)/shard_map/ppermute | solution.py:293
  58.6 3.6 %collective-permute-start.13 = (f32[8,128]{1,0:T(8,128)S(1)}, f32[8,128]{1,0:T(8,128)S(1)}, u32[]{:S(2)}, u32[]{:S(2)}) collective-permute-start(f32[8,128]{1,0:T(8,128)S(1)} %get-tuple-element.28), channel_id=1, source_target_pairs={{0,2},{2,0},{4,6},{6,4},{8,10},{10,8},{12,14},{14,12},{16,18},{18,... | collective-permute-start | bytes 12296 | tf_op jit(solution)/shard_map/ppermute | solution.py:293

commit v4 on v3

--- a/solution.py
+++ b/solution.py
@@ -11,20 +11,18 @@
 BLOCK = 64
 LANES = 128
 SEL_ROWS = 16
-SPLIT = 1
 NEG = -1e37
 
 
 def gate_kernel(dims, *refs):
-    n_piece, n_key, heads, n_sel, n_cand, blocks, head_size = dims
+    q_plan, n_piece, n_q, n_key, heads, n_sel, n_cand, blocks, head_size, stride = dims
     cand_s = refs[0]
-    q_in = refs[1 : 1 + n_piece]
-    k_in = refs[1 + n_piece : 1 + n_piece + n_key]
-    refs = refs[1 + n_piece + n_key :]
+    q_in = refs[1 : 1 + n_q]
+    k_in = refs[1 + n_q : 1 + n_q + n_key]
+    refs = refs[1 + n_q + n_key :]
     wq_in, wk_in = refs[:2]
     out_refs = refs[2 : 2 + n_piece]
     qbuf, kbuf, pool, qpool, teach, ms, ss, lv, sel_v, sel_s, wq_ref, wk_ref, sem_q, sem_k, sem_s, sem_w = refs[2 + n_piece :]
-    stride = q_in[0].shape[0]
     span = stride - SEL_ROWS
     span_blocks = span // BLOCK
     n_slot = n_sel + 1
@@ -32,12 +30,13 @@
     exp_scale = math.log2(math.e) / math.sqrt(head_size)
 
     q_copies = [
-        pltpu.make_async_copy(q_in[i], qbuf.at[pl.ds(i * stride, stride)], sem_q.at[i]) for i in range(n_piece)
+        pltpu.make_async_copy(q_in[src].at[pl.ds(row, count)], qbuf.at[pl.ds(to, count)], sem_q.at[i])
+        for i, (src, row, count, to) in enumerate(q_plan)
     ]
-    k_rows = k_in[0].shape[0]
-    k_copies = [
-        pltpu.make_async_copy(k_in[i], kbuf.at[pl.ds(i * k_rows, k_rows)], sem_k.at[i]) for i in range(n_key)
-    ]
+    k_copies, to = [], 0
+    for i, k in enumerate(k_in):
+        k_copies.append(pltpu.make_async_copy(k, kbuf.at[pl.ds(to, k.shape[0])], sem_k.at[i]))
+        to += k.shape[0]
     w_copies = [
         pltpu.make_async_copy(wq_in, wq_ref, sem_w.at[0]),
         pltpu.make_async_copy(wk_in, wk_ref, sem_w.at[1]),
@@ -157,7 +156,7 @@
         return carry
 
     head_step(0, 0)
-    lax.fori_loop(0, n_piece * heads, combine_step, 0, unroll=4)
+    lax.fori_loop(0, n_piece * heads, combine_step, 0, unroll=7)
 
     for copy in w_copies:
         copy.wait()
@@ -179,23 +178,24 @@
     r = lax.broadcasted_iota(jnp.int32, (rows, 1), 0)
     spread = jnp.where(r // span_blocks % heads + cand_s[n_piece * n_cand] == lane, kl, 0.0)
     r = lax.broadcasted_iota(jnp.int32, (1, rows), 1)
-    b = lax.broadcasted_iota(jnp.int32, (8, 1), 0)
+    b = lax.broadcasted_iota(jnp.int32, (8 * n_piece, 1), 0)
+    pick = (r % span_blocks == b % 8) & (r // (span_blocks * heads) == b // 8)
+    tiles = jnp.dot(
+        pick.astype(jnp.float32), spread, preferred_element_type=jnp.float32, precision=lax.Precision.HIGHEST
+    )
     for i in range(n_piece):
-        pick = (r % span_blocks == b) & (r // (span_blocks * heads) == i) & (b < span_blocks)
-        tile = jnp.dot(
-            pick.astype(jnp.float32), spread, preferred_element_type=jnp.float32, precision=lax.Precision.HIGHEST
-        )
-        out_refs[i][...] = tile
-
-
-def gate_call(cand, q_pieces, k_pieces, w_query, key_gate_weight, heads, n_sel, n_cand):
+        out_refs[i][...] = tiles[8 * i : 8 * i + 8]
+
+
+def gate_call(cand, q_plan, q_pieces, k_pieces, w_query, key_gate_weight, stride, heads, n_sel, n_cand):
     head_size = w_query.shape[0]
-    stride = q_pieces[0].shape[0]
     span_blocks = (stride - SEL_ROWS) // BLOCK
-    n_piece = len(q_pieces)
-    blocks = len(k_pieces) * k_pieces[0].shape[0] // BLOCK
+    n_piece = sum(count for _, _, count, _ in q_plan) // stride
+    blocks = sum(x.shape[0] for x in k_pieces) // BLOCK
     rows = n_piece * heads * span_blocks
-    dims = (n_piece, len(k_pieces), heads, n_sel, n_cand, blocks, head_size)
+    dims = (
+        tuple(q_plan), n_piece, len(q_pieces), len(k_pieces), heads, n_sel, n_cand, blocks, head_size, stride,
+    )
     slots = -(-(n_sel + 1) // 8) * 8
     smem = pl.BlockSpec(memory_space=pltpu.SMEM)
     hbm = pl.BlockSpec(memory_space=pl.ANY)
@@ -203,7 +203,7 @@
     return pl.pallas_call(
         functools.partial(gate_kernel, dims),
         out_shape=[jax.ShapeDtypeStruct((8, LANES), jnp.float32)] * n_piece,
-        in_specs=[smem] + [hbm] * (n_piece + len(k_pieces) + 2),
+        in_specs=[smem] + [hbm] * (len(q_pieces) + len(k_pieces) + 2),
         out_specs=[vmem] * n_piece,
         scratch_shapes=[
             pltpu.VMEM((n_piece * stride, heads * head_size), jnp.bfloat16),
@@ -218,7 +218,7 @@
             pltpu.SMEM((n_piece, 8, LANES), jnp.int32),
             pltpu.VMEM(w_query.shape, w_query.dtype),
             pltpu.VMEM(key_gate_weight.shape, key_gate_weight.dtype),
-            pltpu.SemaphoreType.DMA((n_piece,)),
+            pltpu.SemaphoreType.DMA((len(q_plan),)),
             pltpu.SemaphoreType.DMA((len(k_pieces),)),
             pltpu.SemaphoreType.DMA(()),
             pltpu.SemaphoreType.DMA((2,)),
@@ -251,7 +251,9 @@
         step = (layer - other_ctx // plane) % layers
         which = (other_ctx % plane) ^ spot
         side = (span_id % n_pair) ^ core
-        return ((side * layers + step) * plane + which) * span_blocks + block % span_blocks
+        last = layers - 1
+        at = jnp.where(step == last, last * n_pair + side, side * last + step)
+        return (at * plane + which) * span_blocks + block % span_blocks
 
     local_ids = jnp.arange(span_blocks, dtype=jnp.int32)
     candidates = []
@@ -270,21 +272,22 @@
     )
 
     width = heads * head_size
+    stride = span + SEL_ROWS
     sel_rows = jnp.pad(
         selected.astype(jnp.bfloat16).reshape(span_blocks, kv_heads, heads * n_sel),
         ((0, SEL_ROWS - span_blocks), (0, 0), (0, width - heads * n_sel)),
     ).reshape(SEL_ROWS, q_heads * head_size)
     sent = jnp.concatenate([queries, sel_rows], axis=0)
-
     if not ring:
         gathered = lax.all_gather(key_state_rows, ("ctx", "pair"), axis=0, tiled=True)
         outs = []
         for g in range(kv_heads):
             (out,) = gate_call(
                 cand,
+                [(0, 0, stride, 0)],
                 [sent[:, g * width : (g + 1) * width]],
                 [gathered[:, g * head_size : (g + 1) * head_size]],
-                w_query, key_gate_weight, heads, n_sel, n_cand,
+                w_query, key_gate_weight, stride, heads, n_sel, n_cand,
             )
             outs.append(out[:span_blocks, :heads])
         return jnp.concatenate(outs, axis=1)
@@ -300,22 +303,24 @@
         for p in range(plane)
     ]
     parts = [lax.dynamic_slice_in_dim(sent, (spot ^ p) * width, width, 1) for p in range(plane)]
-    per = plane // SPLIT
-    streams = [[jnp.concatenate(keys[i * per : (i + 1) * per], axis=0)] for i in range(SPLIT)]
-    heads_of, parts = lax.optimization_barrier(([x[0] for x in streams], parts))
-    streams = [[x] for x in heads_of]
+    steps = [jnp.concatenate(keys, axis=0)]
+    other = []
+    steps[0], parts = lax.optimization_barrier((steps[0], parts))
     pieces = [flipped(x, p) for p, x in enumerate(parts)]
     for i in range(layers - 1):
         if i == 2:
-            tied = ([x[i] for x in streams], pieces[1:3], cand)
-            heads_of, pieces[1:3], cand = lax.optimization_barrier(tied)
-            for x, y in zip(streams, heads_of):
-                x[i] = y
-        for x in streams:
-            x.append(lax.ppermute(x[i], "ctx", [(j, (j + plane) % n_ctx) for j in range(n_ctx)]))
-    mine = [x[i] for i in range(layers) for x in streams]
-    k_pieces = mine + [other_core(x) for x in mine]
-    outs = gate_call(cand, pieces, k_pieces, w_query, key_gate_weight, heads, n_sel, n_cand)
+            steps[2], pieces[1:3], cand = lax.optimization_barrier((steps[2], pieces[1:3], cand))
+        steps.append(lax.ppermute(steps[i], "ctx", [(j, (j + plane) % n_ctx) for j in range(n_ctx)]))
+    other += [other_core(x) for x in steps[len(other) :]]
+    k_pieces = [jnp.concatenate(steps[:-1] + other[:-1], axis=0), steps[-1], other[-1]]
+    q_pieces = pieces
+    q_plan, to = [], 0
+    for i, x in enumerate(q_pieces):
+        q_plan.append((i, 0, x.shape[0], to))
+        to += x.shape[0]
+    outs = gate_call(
+        cand, q_plan, q_pieces, k_pieces, w_query, key_gate_weight, stride, heads, n_sel, n_cand
+    )
     back = [flipped(x, p) for p, x in enumerate(outs)]
     return functools.reduce(jnp.add, back)[:span_blocks, :q_heads]
 

time: 63 us -> 61.3 us (0.973)
  waiting for transfers between devices: 25.2 us -> 24.4 us
  Pallas kernels: 15.7 us -> 14.9 us
    ppermute x9, waiting for transfers between devices: 12.4 us -> 11.5 us  [flipped(): lax.ppermute(x, 'ctx', [(i, i ^ p) for i in range(n_ctx)])]
    pallas_call x1, Pallas kernels: 15.7 us -> 14.9 us  [gate_call(): pl.pallas_call(functools.partial(gate_kernel, dims), out_shape=[jax.Shape...]
    unnamed x10 -> x13, local copies, waits for them, and re-layouts: 1.65 us -> 1.81 us
  transfers between devices with their start and end apart: 16 -> 16, of which waited for: 11 -> 11; matrix products, arithmetic and copies ran while one was open for 6% -> 7% of each run, Pallas kernels for 0% -> 0%
where the time goes in v4:
time: 61.3 us; the launch traced here: 61.1 us
  waiting for transfers between devices  24.4 us (40%)
  Pallas kernels  14.9 us (24%)
  starting transfers between devices  14.4 us (23%)
  local copies, waits for them, and re-layouts  6.2 us (10%)
  other arithmetic  1.07 us (2%)
    pallas_call x1, Pallas kernels, gate_call(): pl.pallas_call(functools.partial(gate_kernel, dims), out_shape=[jax.Shape...  14.9 us
    ppermute x3, waiting for transfers between devices, per_device(): lax.ppermute(steps[i], 'ctx', [(j, (j + plane) % n_ctx) for j in range(n_...  12.8 us
    ppermute x9, starting transfers between devices, flipped(): lax.ppermute(x, 'ctx', [(i, i ^ p) for i in range(n_ctx)])  12.1 us
    ppermute x9, waiting for transfers between devices, flipped(): lax.ppermute(x, 'ctx', [(i, i ^ p) for i in range(n_ctx)])  11.5 us
    unnamed x13, local copies, waits for them, and re-layouts  1.81 us
    ppermute x3, starting transfers between devices, per_device(): lax.ppermute(steps[i], 'ctx', [(j, (j + plane) % n_ctx) for j in range(n_...  1.63 us
    dynamic_slice x1, local copies, waits for them, and re-layouts, per_device(): lax.dynamic_slice_in_dim(key_state_rows, (spot ^ p) * head_size, head_siz...  1.62 us
  transfers between devices with their start and end apart: 16, of which 11 were waited for; matrix products, arithmetic and copies ran while one was open for 7% of the time, Pallas kernels for 0%

profile of v4, /device:TPU:0, one launch (start us, length us, event | category | flops | bytes accessed | tf_op | source)
XLA Modules:
  0.0 61.1 jit_solution(5016865028982343092)
XLA Ops:
  0.0 1.6 %constant_dynamic-slice_fusion.11 = (bf16[256,128]{1,0:T(8,128)(2,1)S(1)}, bf16[256,128]{1,0:T(8,128)(2,1)S(1)}, bf16[256,128]{1,0:T(8,128)(2,1)}, bf16[256,128]{1,0:T(8,128)(2,1)}) fusion(bf16[256,512]{1,0:T(8,128)(2,1)} %param.7, s32[]{:T(128)S(6)} %select_n.81, s32[]{:T(128)S(6)} %select_n.82, s32[]{:T(128)S(6)} %select_n.84, s32[]{:T(128)S(6)} %select_n.83), kind=kLoop, calls=%fused_computation.21 | loop fusion | bytes 524304 | tf_op jit(solution)/shard_map/dynamic_slice | solution.py:302
  1.6 3.9 %collective-permute-start.2 = (bf16[256,128]{1,0:T(8,128)(2,1)}, bf16[256,128]{1,0:T(8,128)(2,1)}, u32[]{:S(2)}, u32[]{:S(2)}) collective-permute-start(bf16[256,128]{1,0:T(8,128)(2,1)} %get-tuple-element.37), channel_id=1, source_target_pairs={{0,6},{2,4},{4,2},{6,0},{8,14},{10,12},{12,10},{14,8},{16,22},{18,... | collective-permute-start | bytes 196616 | tf_op jit(solution)/shard_map/ppermute | solution.py:296
  6.1 1.6 %constant_dynamic-update-slice_fusion.1 = bf16[272,3584]{1,0:T(8,128)(2,1)S(1)} fusion(bf16[256,3584]{1,0:T(8,128)(2,1)} %param.6), kind=kLoop, calls=%fused_computation.2 | loop fusion | bytes 3670016
  8.1 1.0 %constant_dynamic-slice_fusion.4 = (bf16[272,896]{1,0:T(8,128)(2,1)S(1)}, bf16[272,896]{1,0:T(8,128)(2,1)S(1)}, bf16[272,896]{1,0:T(8,128)(2,1)}, bf16[272,896]{1,0:T(8,128)(2,1)S(1)}) fusion(bf16[272,3584]{1,0:T(8,128)(2,1)S(1)} %constant_dynamic-update-slice_fusion, s32[]{:T(128)S(6)} %select_n.88, s32[]{:T(128)S(6)} %select_n.87, s32[]{:T(128)S(6)} %select_n.86, ...), kind=kLoop, calls=%fused_computation.14 | loop fusion | bytes 3899408 | tf_op jit(solution)/shard_map/dynamic_slice | solution.py:305
  9.1 1.0 %collective-permute-done.1 = bf16[256,128]{1,0:T(8,128)(2,1)} collective-permute-done((bf16[256,128]{1,0:T(8,128)(2,1)}, bf16[256,128]{1,0:T(8,128)(2,1)}, u32[]{:S(2)}, u32[]{:S(2)}) %collective-permute-start.1) | collective-permute-done | bytes 65568 | tf_op jit(solution)/shard_map/ppermute | solution.py:296
  10.4 0.9 %pad_maximum_fusion = bf16[1024,128]{1,0:T(8,128)(2,1)S(1)} fusion(bf16[256,128]{1,0:T(8,128)(2,1)} %collective-permute-done.2, bf16[256,128]{1,0:T(8,128)(2,1)} %collective-permute-done.1, bf16[256,128]{1,0:T(8,128)(2,1)} %collective-permute-done, bf16[256,128]{1,0:T(8,128)(2,1)S(1)} %get-tuple-element.35), kind=kLoop, calls=%fused_computation | loop fusion | flops 1048576 | bytes 524288 | tf_op jit(solution)/shard_map/concatenate | solution.py:306
  11.3 1.6 %collective-permute-start.3 = (bf16[1024,128]{1,0:T(8,128)(2,1)S(1)}, bf16[1024,128]{1,0:T(8,128)(2,1)S(1)}, u32[]{:S(2)}, u32[]{:S(2)}) collective-permute-start(bf16[1024,128]{1,0:T(8,128)(2,1)S(1)} %pad_maximum_fusion), channel_id=1, source_target_pairs={{0,8},{2,10},{4,12},{6,14},{8,16},{10,18},{12,20},{14,22},{16,24},... | collective-permute-start | bytes 786440 | tf_op jit(solution)/shard_map/ppermute | solution.py:313
  12.9 0.7 %collective-permute-start.5 = (bf16[272,896]{1,0:T(8,128)(2,1)}, bf16[272,896]{1,0:T(8,128)(2,1)S(1)}, u32[]{:S(2)}, u32[]{:S(2)}) collective-permute-start(bf16[272,896]{1,0:T(8,128)(2,1)} %get-tuple-element.19), channel_id=1, source_target_pairs={{0,2},{2,0},{4,6},{6,4},{8,10},{10,8},{12,14},{14,12},{16,18},{18,... | collective-permute-start | bytes 1462280 | tf_op jit(solution)/shard_map/ppermute | solution.py:296
  13.6 1.5 %collective-permute-start.6 = (bf16[272,896]{1,0:T(8,128)(2,1)S(1)}, bf16[272,896]{1,0:T(8,128)(2,1)S(1)}, u32[]{:S(2)}, u32[]{:S(2)}) collective-permute-start(bf16[272,896]{1,0:T(8,128)(2,1)S(1)} %get-tuple-element.20), channel_id=1, source_target_pairs={{0,4},{2,6},{4,0},{6,2},{8,12},{10,14},{12,8},{14,10},{16,20},{18,... | collective-permute-start | bytes 1462280 | tf_op jit(solution)/shard_map/ppermute | solution.py:296
  15.1 0.8 %fusion.10 = (s32[31]{0:T(128)S(1)}, s32[31]{0:T(128)S(1)}, s32[31]{0:T(128)S(1)}, s32[31]{0:T(128)S(1)}) fusion(s32[32,31]{1,0:T(8,128)} %param.8, s32[]{:T(128)S(6)} %select_n.93, s32[]{:T(128)S(6)} %select_n.91, s32[]{:T(128)S(6)} %select_n.90, s32[]{:T(128)S(6)} %select_n.92), kind=kLoop, calls=%fused_computation.52 | loop fusion | bytes 1008 | tf_op jit(solution)/shard_map/jit(dynamic_index_in_dim)/squeeze | solution.py:262
  16.0 4.1 %collective-permute-done.3 = bf16[1024,128]{1,0:T(8,128)(2,1)S(1)} collective-permute-done((bf16[1024,128]{1,0:T(8,128)(2,1)S(1)}, bf16[1024,128]{1,0:T(8,128)(2,1)S(1)}, u32[]{:S(2)}, u32[]{:S(2)}) %collective-permute-start.3) | collective-permute-done | bytes 262176 | tf_op jit(solution)/shard_map/ppermute | solution.py:313
  20.3 4.3 %collective-permute-done.5.refs_2_ = bf16[272,896]{1,0:T(8,128)(2,1)S(1)} collective-permute-done((bf16[272,896]{1,0:T(8,128)(2,1)}, bf16[272,896]{1,0:T(8,128)(2,1)S(1)}, u32[]{:S(2)}, u32[]{:S(2)}) %collective-permute-start.5) | collective-permute-done | bytes 487456 | tf_op jit(solution)/shard_map/ppermute | solution.py:296
  25.2 3.2 %collective-permute-done.4 = bf16[1024,128]{1,0:T(8,128)(2,1)S(1)} collective-permute-done((bf16[1024,128]{1,0:T(8,128)(2,1)S(1)}, bf16[1024,128]{1,0:T(8,128)(2,1)S(1)}, u32[]{:S(2)}, u32[]{:S(2)}) %collective-permute-start.4) | collective-permute-done | bytes 262176 | tf_op jit(solution)/shard_map/ppermute | solution.py:313
  28.4 1.9 %collective-permute-start.7 = (bf16[272,896]{1,0:T(8,128)(2,1)S(1)}, bf16[272,896]{1,0:T(8,128)(2,1)S(1)}, u32[]{:S(2)}, u32[]{:S(2)}) collective-permute-start(bf16[272,896]{1,0:T(8,128)(2,1)S(1)} %get-tuple-element.25), channel_id=1, source_target_pairs={{0,6},{2,4},{4,2},{6,0},{8,14},{10,12},{12,10},{14,8},{16,22},{18,... | collective-permute-start | bytes 1462280 | tf_op jit(solution)/shard_map/ppermute | solution.py:296
  31.0 5.6 %collective-permute-done.11.refs_6_ = bf16[1024,128]{1,0:T(8,128)(2,1)S(1)} collective-permute-done((bf16[1024,128]{1,0:T(8,128)(2,1)S(1)}, bf16[1024,128]{1,0:T(8,128)(2,1)S(1)}, u32[]{:S(2)}, u32[]{:S(2)}) %collective-permute-start.11) | collective-permute-done | bytes 262176 | tf_op jit(solution)/shard_map/ppermute | solution.py:313
  36.7 2.4 %collective-permute-done.7.refs_4_ = bf16[272,896]{1,0:T(8,128)(2,1)S(1)} collective-permute-done((bf16[272,896]{1,0:T(8,128)(2,1)S(1)}, bf16[272,896]{1,0:T(8,128)(2,1)S(1)}, u32[]{:S(2)}, u32[]{:S(2)}) %collective-permute-start.7) | collective-permute-done | bytes 487456 | tf_op jit(solution)/shard_map/ppermute | solution.py:296
  39.1 14.9 %shard_map.64 = (f32[8,128]{1,0:T(8,128)S(1)}, f32[8,128]{1,0:T(8,128)S(1)}, f32[8,128]{1,0:T(8,128)S(1)}, f32[8,128]{1,0:T(8,128)S(1)}) custom-call(s32[157]{0:T(256)S(1)} %pad_add_fusion.refs_0_, bf16[272,896]{1,0:T(8,128)(2,1)S(1)} %get-tuple-element.22.refs_1_, bf16[272,896]{1,0:T(8,128)(2,1)S(1)} %collective-permute-done.5.refs_2_, ...), custom_call_target="tpu_custom_call" | custom-call | tf_op jit(solution)/shard_map/pallas_call | solution.py:203
  54.0 2.2 %collective-permute-start.15 = (f32[8,128]{1,0:T(8,128)S(1)}, f32[8,128]{1,0:T(8,128)S(1)}, u32[]{:S(2)}, u32[]{:S(2)}) collective-permute-start(f32[8,128]{1,0:T(8,128)S(1)} %get-tuple-element.30), channel_id=1, source_target_pairs={{0,6},{2,4},{4,2},{6,0},{8,14},{10,12},{12,10},{14,8},{16,22},{18,... | collective-permute-start | bytes 12296 | tf_op jit(solution)/shard_map/ppermute | solution.py:296
  56.2 0.7 %collective-permute-start.14 = (f32[8,128]{1,0:T(8,128)S(1)}, f32[8,128]{1,0:T(8,128)S(1)}, u32[]{:S(2)}, u32[]{:S(2)}) collective-permute-start(f32[8,128]{1,0:T(8,128)S(1)} %get-tuple-element.29), channel_id=1, source_target_pairs={{0,4},{2,6},{4,0},{6,2},{8,12},{10,14},{12,8},{14,10},{16,20},{18,... | collective-permute-start | bytes 12296 | tf_op jit(solution)/shard_map/ppermute | solution.py:296
  56.9 0.7 %collective-permute-start.13 = (f32[8,128]{1,0:T(8,128)S(1)}, f32[8,128]{1,0:T(8,128)S(1)}, u32[]{:S(2)}, u32[]{:S(2)}) collective-permute-start(f32[8,128]{1,0:T(8,128)S(1)} %get-tuple-element.28), channel_id=1, source_target_pairs={{0,2},{2,0},{4,6},{6,4},{8,10},{10,8},{12,14},{14,12},{16,18},{18,... | collective-permute-start | bytes 12296 | tf_op jit(solution)/shard_map/ppermute | solution.py:296
  57.5 1.0 %collective-permute-done.15 = f32[8,128]{1,0:T(8,128)S(1)} collective-permute-done((f32[8,128]{1,0:T(8,128)S(1)}, f32[8,128]{1,0:T(8,128)S(1)}, u32[]{:S(2)}, u32[]{:S(2)}) %collective-permute-start.15) | collective-permute-done | bytes 4128 | tf_op jit(solution)/shard_map/ppermute | solution.py:296
  58.6 1.2 %collective-permute-done.14 = f32[8,128]{1,0:T(8,128)S(1)} collective-permute-done((f32[8,128]{1,0:T(8,128)S(1)}, f32[8,128]{1,0:T(8,128)S(1)}, u32[]{:S(2)}, u32[]{:S(2)}) %collective-permute-start.14) | collective-permute-done | bytes 4128 | tf_op jit(solution)/shard_map/ppermute | solution.py:296
  59.8 0.7 %collective-permute-done.13 = f32[8,128]{1,0:T(8,128)S(1)} collective-permute-done((f32[8,128]{1,0:T(8,128)S(1)}, f32[8,128]{1,0:T(8,128)S(1)}, u32[]{:S(2)}, u32[]{:S(2)}) %collective-permute-start.13) | collective-permute-done | bytes 4128 | tf_op jit(solution)/shard_map/ppermute | solution.py:296
  60.5 0.6 slice.3
  (41 shorter events, 2.7 us)
Async XLA Ops:
  1.6 7.4 %collective-permute-start.2 = (bf16[256,128]{1,0:T(8,128)(2,1)}, bf16[256,128]{1,0:T(8,128)(2,1)}, u32[]{:S(2)}, u32[]{:S(2)}) collective-permute-start(bf16[256,128]{1,0:T(8,128)(2,1)} %get-tuple-element.37), channel_id=1, source_target_pairs={{0,6},{2,4},{4,2},{6,0},{8,14},{10,12},{12,10},{14,8},{16,22},{18,... | collective-permute-start | bytes 196616 | tf_op jit(solution)/shard_map/ppermute | solution.py:296
  5.5 4.6 %collective-permute-start.1 = (bf16[256,128]{1,0:T(8,128)(2,1)}, bf16[256,128]{1,0:T(8,128)(2,1)}, u32[]{:S(2)}, u32[]{:S(2)}) collective-permute-start(bf16[256,128]{1,0:T(8,128)(2,1)} %get-tuple-element.38), channel_id=1, source_target_pairs={{0,4},{2,6},{4,0},{6,2},{8,12},{10,14},{12,8},{14,10},{16,20},{18,... | collective-permute-start | bytes 196616 | tf_op jit(solution)/shard_map/ppermute | solution.py:296
  6.0 4.4 %collective-permute-start = (bf16[256,128]{1,0:T(8,128)(2,1)S(1)}, bf16[256,128]{1,0:T(8,128)(2,1)}, u32[]{:S(2)}, u32[]{:S(2)}) collective-permute-start(bf16[256,128]{1,0:T(8,128)(2,1)S(1)} %get-tuple-element.36), channel_id=1, source_target_pairs={{0,2},{2,0},{4,6},{6,4},{8,10},{10,8},{12,14},{14,12},{16,18},{18,... | collective-permute-start | bytes 196616 | tf_op jit(solution)/shard_map/ppermute | solution.py:296
  6.1 1.6 %copy-start.2 = (s32[4,28,16]{1,2,0:T(8,128)S(1)}, s32[4,28,16]{1,2,0:T(8,128)}, u32[]{:S(2)}) copy-start(s32[4,28,16]{1,2,0:T(8,128)} %param.9) | copy-start | bytes 21508
  11.3 8.9 %collective-permute-start.3 = (bf16[1024,128]{1,0:T(8,128)(2,1)S(1)}, bf16[1024,128]{1,0:T(8,128)(2,1)S(1)}, u32[]{:S(2)}, u32[]{:S(2)}) collective-permute-start(bf16[1024,128]{1,0:T(8,128)(2,1)S(1)} %pad_maximum_fusion), channel_id=1, source_target_pairs={{0,8},{2,10},{4,12},{6,14},{8,16},{10,18},{12,20},{14,22},{16,24},... | collective-permute-start | bytes 786440 | tf_op jit(solution)/shard_map/ppermute | solution.py:313
  12.9 11.7 %collective-permute-start.5 = (bf16[272,896]{1,0:T(8,128)(2,1)}, bf16[272,896]{1,0:T(8,128)(2,1)S(1)}, u32[]{:S(2)}, u32[]{:S(2)}) collective-permute-start(bf16[272,896]{1,0:T(8,128)(2,1)} %get-tuple-element.19), channel_id=1, source_target_pairs={{0,2},{2,0},{4,6},{6,4},{8,10},{10,8},{12,14},{14,12},{16,18},{18,... | collective-permute-start | bytes 1462280 | tf_op jit(solution)/shard_map/ppermute | solution.py:296
  13.6 11.6 %collective-permute-start.6 = (bf16[272,896]{1,0:T(8,128)(2,1)S(1)}, bf16[272,896]{1,0:T(8,128)(2,1)S(1)}, u32[]{:S(2)}, u32[]{:S(2)}) collective-permute-start(bf16[272,896]{1,0:T(8,128)(2,1)S(1)} %get-tuple-element.20), channel_id=1, source_target_pairs={{0,4},{2,6},{4,0},{6,2},{8,12},{10,14},{12,8},{14,10},{16,20},{18,... | collective-permute-start | bytes 1462280 | tf_op jit(solution)/shard_map/ppermute | solution.py:296
  20.2 8.2 %collective-permute-start.4 = (bf16[1024,128]{1,0:T(8,128)(2,1)S(1)}, bf16[1024,128]{1,0:T(8,128)(2,1)S(1)}, u32[]{:S(2)}, u32[]{:S(2)}) collective-permute-start(bf16[1024,128]{1,0:T(8,128)(2,1)S(1)} %collective-permute-done.3), channel_id=1, source_target_pairs={{0,8},{2,10},{4,12},{6,14},{8,16},{10,18},{12,20},{14,22},{16,24},... | collective-permute-start | bytes 786440 | tf_op jit(solution)/shard_map/ppermute | solution.py:313
  20.3 18.8 %copy-start = (bf16[384,128]{1,0:T(8,128)(2,1)S(1)}, bf16[384,128]{1,0:T(8,128)(2,1)}, u32[]{:S(2)}) copy-start(bf16[384,128]{1,0:T(8,128)(2,1)} %refs_9_.1) | copy-start | bytes 294916
  20.3 18.8 %copy-start.1 = (bf16[128,128]{1,0:T(8,128)(2,1)S(1)}, bf16[128,128]{1,0:T(8,128)(2,1)}, u32[]{:S(2)}) copy-start(bf16[128,128]{1,0:T(8,128)(2,1)} %refs_8_.1) | copy-start | bytes 98308
  20.3 16.2 %collective-permute-start.8 = (bf16[1024,128]{1,0:T(8,128)(2,1)S(1)}, bf16[1024,128]{1,0:T(8,128)(2,1)S(1)}, u32[]{:S(2)}, u32[]{:S(2)}) collective-permute-start(bf16[1024,128]{1,0:T(8,128)(2,1)S(1)} %pad_maximum_fusion), channel_id=1, source_target_pairs={{0,1},{1,0},{2,3},{3,2},{4,5},{5,4},{6,7},{7,6},{8,9},{9,8},{10,11... | collective-permute-start | bytes 786440 | tf_op jit(solution)/shard_map/ppermute | solution.py:299
  28.3 8.2 %collective-permute-start.11 = (bf16[1024,128]{1,0:T(8,128)(2,1)S(1)}, bf16[1024,128]{1,0:T(8,128)(2,1)S(1)}, u32[]{:S(2)}, u32[]{:S(2)}) collective-permute-start(bf16[1024,128]{1,0:T(8,128)(2,1)S(1)} %collective-permute-done.4), channel_id=1, source_target_pairs={{0,8},{2,10},{4,12},{6,14},{8,16},{10,18},{12,20},{14,22},{16,24},... | collective-permute-start | bytes 786440 | tf_op jit(solution)/shard_map/ppermute | solution.py:313
  28.4 10.7 %collective-permute-start.7 = (bf16[272,896]{1,0:T(8,128)(2,1)S(1)}, bf16[272,896]{1,0:T(8,128)(2,1)S(1)}, u32[]{:S(2)}, u32[]{:S(2)}) collective-permute-start(bf16[272,896]{1,0:T(8,128)(2,1)S(1)} %get-tuple-element.25), channel_id=1, source_target_pairs={{0,6},{2,4},{4,2},{6,0},{8,14},{10,12},{12,10},{14,8},{16,22},{18,... | collective-permute-start | bytes 1462280 | tf_op jit(solution)/shard_map/ppermute | solution.py:296
  30.3 6.3 %collective-permute-start.9 = (bf16[1024,128]{1,0:T(8,128)(2,1)S(1)}, bf16[1024,128]{1,0:T(8,128)(2,1)S(1)}, u32[]{:S(2)}, u32[]{:S(2)}) collective-permute-start(bf16[1024,128]{1,0:T(8,128)(2,1)S(1)} %collective-permute-done.3), channel_id=1, source_target_pairs={{0,1},{1,0},{2,3},{3,2},{4,5},{5,4},{6,7},{7,6},{8,9},{9,8},{10,11... | collective-permute-start | bytes 786440 | tf_op jit(solution)/shard_map/ppermute | solution.py:299
  30.3 6.3 %collective-permute-start.10 = (bf16[1024,128]{1,0:T(8,128)(2,1)S(1)}, bf16[1024,128]{1,0:T(8,128)(2,1)S(1)}, u32[]{:S(2)}, u32[]{:S(2)}) collective-permute-start(bf16[1024,128]{1,0:T(8,128)(2,1)S(1)} %collective-permute-done.4), channel_id=1, source_target_pairs={{0,1},{1,0},{2,3},{3,2},{4,5},{5,4},{6,7},{7,6},{8,9},{9,8},{10,11... | collective-permute-start | bytes 786440 | tf_op jit(solution)/shard_map/ppermute | solution.py:299
  36.5 2.6 %collective-permute-start.12 = (bf16[1024,128]{1,0:T(8,128)(2,1)S(1)}, bf16[1024,128]{1,0:T(8,128)(2,1)S(1)}, u32[]{:S(2)}, u32[]{:S(2)}) collective-permute-start(bf16[1024,128]{1,0:T(8,128)(2,1)S(1)} %collective-permute-done.11.refs_6_), channel_id=1, source_target_pairs={{0,1},{1,0},{2,3},{3,2},{4,5},{5,4},{6,7},{7,6},{8,9},{9,8},{10,11... | collective-permute-start | bytes 786440 | tf_op jit(solution)/shard_map/ppermute | solution.py:299
  54.0 4.6 %collective-permute-start.15 = (f32[8,128]{1,0:T(8,128)S(1)}, f32[8,128]{1,0:T(8,128)S(1)}, u32[]{:S(2)}, u32[]{:S(2)}) collective-permute-start(f32[8,128]{1,0:T(8,128)S(1)} %get-tuple-element.30), channel_id=1, source_target_pairs={{0,6},{2,4},{4,2},{6,0},{8,14},{10,12},{12,10},{14,8},{16,22},{18,... | collective-permute-start | bytes 12296 | tf_op jit(solution)/shard_map/ppermute | solution.py:296
  56.2 3.6 %collective-permute-start.14 = (f32[8,128]{1,0:T(8,128)S(1)}, f32[8,128]{1,0:T(8,128)S(1)}, u32[]{:S(2)}, u32[]{:S(2)}) collective-permute-start(f32[8,128]{1,0:T(8,128)S(1)} %get-tuple-element.29), channel_id=1, source_target_pairs={{0,4},{2,6},{4,0},{6,2},{8,12},{10,14},{12,8},{14,10},{16,20},{18,... | collective-permute-start | bytes 12296 | tf_op jit(solution)/shard_map/ppermute | solution.py:296
  56.9 3.6 %collective-permute-start.13 = (f32[8,128]{1,0:T(8,128)S(1)}, f32[8,128]{1,0:T(8,128)S(1)}, u32[]{:S(2)}, u32[]{:S(2)}) collective-permute-start(f32[8,128]{1,0:T(8,128)S(1)} %get-tuple-element.28), channel_id=1, source_target_pairs={{0,2},{2,0},{4,6},{6,4},{8,10},{10,8},{12,14},{14,12},{16,18},{18,... | collective-permute-start | bytes 12296 | tf_op jit(solution)/shard_map/ppermute | solution.py:296

commit v5 on v4

--- a/solution.py
+++ b/solution.py
@@ -156,7 +156,7 @@
         return carry
 
     head_step(0, 0)
-    lax.fori_loop(0, n_piece * heads, combine_step, 0, unroll=7)
+    lax.fori_loop(0, n_piece * heads, combine_step, 0, unroll=14)
 
     for copy in w_copies:
         copy.wait()
@@ -322,7 +322,7 @@
         cand, q_plan, q_pieces, k_pieces, w_query, key_gate_weight, stride, heads, n_sel, n_cand
     )
     back = [flipped(x, p) for p, x in enumerate(outs)]
-    return functools.reduce(jnp.add, back)[:span_blocks, :q_heads]
+    return functools.reduce(jnp.add, [x[:span_blocks, :q_heads] for x in back])
 
 
 def solution(mesh):

time: 61.3 us -> 61 us (level)
  no operation moved by 1% of the time
where the time goes in v5:
time: 61 us; the launch traced here: 60.8 us
  waiting for transfers between devices  24.4 us (40%)
  Pallas kernels  14.6 us (24%)
  starting transfers between devices  14.4 us (24%)
  local copies, waits for them, and re-layouts  5.61 us (9%)
  other arithmetic  1.64 us (3%)
    pallas_call x1, Pallas kernels, gate_call(): pl.pallas_call(functools.partial(gate_kernel, dims), out_shape=[jax.Shape...  14.6 us
    ppermute x3, waiting for transfers between devices, per_device(): lax.ppermute(steps[i], 'ctx', [(j, (j + plane) % n_ctx) for j in range(n_...  12.8 us
    ppermute x9, starting transfers between devices, flipped(): lax.ppermute(x, 'ctx', [(i, i ^ p) for i in range(n_ctx)])  12.1 us
    ppermute x9, waiting for transfers between devices, flipped(): lax.ppermute(x, 'ctx', [(i, i ^ p) for i in range(n_ctx)])  11.5 us
    unnamed x13, local copies, waits for them, and re-layouts  1.81 us
    ppermute x3, starting transfers between devices, per_device(): lax.ppermute(steps[i], 'ctx', [(j, (j + plane) % n_ctx) for j in range(n_...  1.63 us
    dynamic_slice x1, local copies, waits for them, and re-layouts, per_device(): lax.dynamic_slice_in_dim(key_state_rows, (spot ^ p) * head_size, head_siz...  1.62 us
  transfers between devices with their start and end apart: 16, of which 11 were waited for; matrix products, arithmetic and copies ran while one was open for 7% of the time, Pallas kernels for 0%

profile of v5, /device:TPU:0, one launch (start us, length us, event | category | flops | bytes accessed | tf_op | source)
XLA Modules:
  0.0 60.8 jit_solution(2786825115334080585)
XLA Ops:
  0.0 1.6 %constant_dynamic-slice_fusion.11 = (bf16[256,128]{1,0:T(8,128)(2,1)S(1)}, bf16[256,128]{1,0:T(8,128)(2,1)S(1)}, bf16[256,128]{1,0:T(8,128)(2,1)}, bf16[256,128]{1,0:T(8,128)(2,1)}) fusion(bf16[256,512]{1,0:T(8,128)(2,1)} %param.7, s32[]{:T(128)S(6)} %select_n.81, s32[]{:T(128)S(6)} %select_n.82, s32[]{:T(128)S(6)} %select_n.84, s32[]{:T(128)S(6)} %select_n.83), kind=kLoop, calls=%fused_computation.20 | loop fusion | bytes 524304 | tf_op jit(solution)/shard_map/dynamic_slice | solution.py:302
  1.6 3.9 %collective-permute-start.2 = (bf16[256,128]{1,0:T(8,128)(2,1)}, bf16[256,128]{1,0:T(8,128)(2,1)}, u32[]{:S(2)}, u32[]{:S(2)}) collective-permute-start(bf16[256,128]{1,0:T(8,128)(2,1)} %get-tuple-element.37), channel_id=1, source_target_pairs={{0,6},{2,4},{4,2},{6,0},{8,14},{10,12},{12,10},{14,8},{16,22},{18,... | collective-permute-start | bytes 196616 | tf_op jit(solution)/shard_map/ppermute | solution.py:296
  6.1 1.6 %constant_dynamic-update-slice_fusion.1 = bf16[272,3584]{1,0:T(8,128)(2,1)S(1)} fusion(bf16[256,3584]{1,0:T(8,128)(2,1)} %param.6), kind=kLoop, calls=%fused_computation.2 | loop fusion | bytes 3670016
  8.1 1.0 %constant_dynamic-slice_fusion.4 = (bf16[272,896]{1,0:T(8,128)(2,1)S(1)}, bf16[272,896]{1,0:T(8,128)(2,1)S(1)}, bf16[272,896]{1,0:T(8,128)(2,1)}, bf16[272,896]{1,0:T(8,128)(2,1)S(1)}) fusion(bf16[272,3584]{1,0:T(8,128)(2,1)S(1)} %constant_dynamic-update-slice_fusion, s32[]{:T(128)S(6)} %select_n.88, s32[]{:T(128)S(6)} %select_n.87, s32[]{:T(128)S(6)} %select_n.86, ...), kind=kLoop, calls=%fused_computation.13 | loop fusion | bytes 3899408 | tf_op jit(solution)/shard_map/dynamic_slice | solution.py:305
  9.1 1.0 %collective-permute-done.1 = bf16[256,128]{1,0:T(8,128)(2,1)} collective-permute-done((bf16[256,128]{1,0:T(8,128)(2,1)}, bf16[256,128]{1,0:T(8,128)(2,1)}, u32[]{:S(2)}, u32[]{:S(2)}) %collective-permute-start.1) | collective-permute-done | bytes 65568 | tf_op jit(solution)/shard_map/ppermute | solution.py:296
  10.4 0.9 %pad_maximum_fusion = bf16[1024,128]{1,0:T(8,128)(2,1)S(1)} fusion(bf16[256,128]{1,0:T(8,128)(2,1)} %collective-permute-done.2, bf16[256,128]{1,0:T(8,128)(2,1)} %collective-permute-done.1, bf16[256,128]{1,0:T(8,128)(2,1)} %collective-permute-done, bf16[256,128]{1,0:T(8,128)(2,1)S(1)} %get-tuple-element.35), kind=kLoop, calls=%fused_computation | loop fusion | flops 1048576 | bytes 524288 | tf_op jit(solution)/shard_map/concatenate | solution.py:306
  11.3 1.6 %collective-permute-start.3 = (bf16[1024,128]{1,0:T(8,128)(2,1)S(1)}, bf16[1024,128]{1,0:T(8,128)(2,1)S(1)}, u32[]{:S(2)}, u32[]{:S(2)}) collective-permute-start(bf16[1024,128]{1,0:T(8,128)(2,1)S(1)} %pad_maximum_fusion), channel_id=1, source_target_pairs={{0,8},{2,10},{4,12},{6,14},{8,16},{10,18},{12,20},{14,22},{16,24},... | collective-permute-start | bytes 786440 | tf_op jit(solution)/shard_map/ppermute | solution.py:313
  12.9 0.7 %collective-permute-start.5 = (bf16[272,896]{1,0:T(8,128)(2,1)}, bf16[272,896]{1,0:T(8,128)(2,1)S(1)}, u32[]{:S(2)}, u32[]{:S(2)}) collective-permute-start(bf16[272,896]{1,0:T(8,128)(2,1)} %get-tuple-element.19), channel_id=1, source_target_pairs={{0,2},{2,0},{4,6},{6,4},{8,10},{10,8},{12,14},{14,12},{16,18},{18,... | collective-permute-start | bytes 1462280 | tf_op jit(solution)/shard_map/ppermute | solution.py:296
  13.6 1.5 %collective-permute-start.6 = (bf16[272,896]{1,0:T(8,128)(2,1)S(1)}, bf16[272,896]{1,0:T(8,128)(2,1)S(1)}, u32[]{:S(2)}, u32[]{:S(2)}) collective-permute-start(bf16[272,896]{1,0:T(8,128)(2,1)S(1)} %get-tuple-element.20), channel_id=1, source_target_pairs={{0,4},{2,6},{4,0},{6,2},{8,12},{10,14},{12,8},{14,10},{16,20},{18,... | collective-permute-start | bytes 1462280 | tf_op jit(solution)/shard_map/ppermute | solution.py:296
  15.1 0.8 %fusion.10 = (s32[31]{0:T(128)S(1)}, s32[31]{0:T(128)S(1)}, s32[31]{0:T(128)S(1)}, s32[31]{0:T(128)S(1)}) fusion(s32[32,31]{1,0:T(8,128)} %param.8, s32[]{:T(128)S(6)} %select_n.93, s32[]{:T(128)S(6)} %select_n.91, s32[]{:T(128)S(6)} %select_n.90, s32[]{:T(128)S(6)} %select_n.92), kind=kLoop, calls=%fused_computation.52 | loop fusion | bytes 1008 | tf_op jit(solution)/shard_map/jit(dynamic_index_in_dim)/squeeze | solution.py:262
  16.0 4.1 %collective-permute-done.3 = bf16[1024,128]{1,0:T(8,128)(2,1)S(1)} collective-permute-done((bf16[1024,128]{1,0:T(8,128)(2,1)S(1)}, bf16[1024,128]{1,0:T(8,128)(2,1)S(1)}, u32[]{:S(2)}, u32[]{:S(2)}) %collective-permute-start.3) | collective-permute-done | bytes 262176 | tf_op jit(solution)/shard_map/ppermute | solution.py:313
  20.3 4.3 %collective-permute-done.5.refs_2_ = bf16[272,896]{1,0:T(8,128)(2,1)S(1)} collective-permute-done((bf16[272,896]{1,0:T(8,128)(2,1)}, bf16[272,896]{1,0:T(8,128)(2,1)S(1)}, u32[]{:S(2)}, u32[]{:S(2)}) %collective-permute-start.5) | collective-permute-done | bytes 487456 | tf_op jit(solution)/shard_map/ppermute | solution.py:296
  25.2 3.2 %collective-permute-done.4 = bf16[1024,128]{1,0:T(8,128)(2,1)S(1)} collective-permute-done((bf16[1024,128]{1,0:T(8,128)(2,1)S(1)}, bf16[1024,128]{1,0:T(8,128)(2,1)S(1)}, u32[]{:S(2)}, u32[]{:S(2)}) %collective-permute-start.4) | collective-permute-done | bytes 262176 | tf_op jit(solution)/shard_map/ppermute | solution.py:313
  28.4 1.9 %collective-permute-start.7 = (bf16[272,896]{1,0:T(8,128)(2,1)S(1)}, bf16[272,896]{1,0:T(8,128)(2,1)S(1)}, u32[]{:S(2)}, u32[]{:S(2)}) collective-permute-start(bf16[272,896]{1,0:T(8,128)(2,1)S(1)} %get-tuple-element.25), channel_id=1, source_target_pairs={{0,6},{2,4},{4,2},{6,0},{8,14},{10,12},{12,10},{14,8},{16,22},{18,... | collective-permute-start | bytes 1462280 | tf_op jit(solution)/shard_map/ppermute | solution.py:296
  31.0 5.6 %collective-permute-done.11.refs_6_ = bf16[1024,128]{1,0:T(8,128)(2,1)S(1)} collective-permute-done((bf16[1024,128]{1,0:T(8,128)(2,1)S(1)}, bf16[1024,128]{1,0:T(8,128)(2,1)S(1)}, u32[]{:S(2)}, u32[]{:S(2)}) %collective-permute-start.11) | collective-permute-done | bytes 262176 | tf_op jit(solution)/shard_map/ppermute | solution.py:313
  36.7 2.4 %collective-permute-done.7.refs_4_ = bf16[272,896]{1,0:T(8,128)(2,1)S(1)} collective-permute-done((bf16[272,896]{1,0:T(8,128)(2,1)S(1)}, bf16[272,896]{1,0:T(8,128)(2,1)S(1)}, u32[]{:S(2)}, u32[]{:S(2)}) %collective-permute-start.7) | collective-permute-done | bytes 487456 | tf_op jit(solution)/shard_map/ppermute | solution.py:296
  39.1 14.6 %shard_map.64 = (f32[8,128]{1,0:T(8,128)S(1)}, f32[8,128]{1,0:T(8,128)S(1)}, f32[8,128]{1,0:T(8,128)S(1)}, f32[8,128]{1,0:T(8,128)S(1)}) custom-call(s32[157]{0:T(256)S(1)} %pad_add_fusion.refs_0_, bf16[272,896]{1,0:T(8,128)(2,1)S(1)} %get-tuple-element.22.refs_1_, bf16[272,896]{1,0:T(8,128)(2,1)S(1)} %collective-permute-done.5.refs_2_, ...), custom_call_target="tpu_custom_call" | custom-call | tf_op jit(solution)/shard_map/pallas_call | solution.py:203
  53.7 2.2 %collective-permute-start.15 = (f32[8,128]{1,0:T(8,128)S(1)}, f32[8,128]{1,0:T(8,128)S(1)}, u32[]{:S(2)}, u32[]{:S(2)}) collective-permute-start(f32[8,128]{1,0:T(8,128)S(1)} %get-tuple-element.30), channel_id=1, source_target_pairs={{0,6},{2,4},{4,2},{6,0},{8,14},{10,12},{12,10},{14,8},{16,22},{18,... | collective-permute-start | bytes 12296 | tf_op jit(solution)/shard_map/ppermute | solution.py:296
  55.9 0.7 %collective-permute-start.14 = (f32[8,128]{1,0:T(8,128)S(1)}, f32[8,128]{1,0:T(8,128)S(1)}, u32[]{:S(2)}, u32[]{:S(2)}) collective-permute-start(f32[8,128]{1,0:T(8,128)S(1)} %get-tuple-element.29), channel_id=1, source_target_pairs={{0,4},{2,6},{4,0},{6,2},{8,12},{10,14},{12,8},{14,10},{16,20},{18,... | collective-permute-start | bytes 12296 | tf_op jit(solution)/shard_map/ppermute | solution.py:296
  56.6 0.7 %collective-permute-start.13 = (f32[8,128]{1,0:T(8,128)S(1)}, f32[8,128]{1,0:T(8,128)S(1)}, u32[]{:S(2)}, u32[]{:S(2)}) collective-permute-start(f32[8,128]{1,0:T(8,128)S(1)} %get-tuple-element.28), channel_id=1, source_target_pairs={{0,2},{2,0},{4,6},{6,4},{8,10},{10,8},{12,14},{14,12},{16,18},{18,... | collective-permute-start | bytes 12296 | tf_op jit(solution)/shard_map/ppermute | solution.py:296
  57.3 1.0 %collective-permute-done.15 = f32[8,128]{1,0:T(8,128)S(1)} collective-permute-done((f32[8,128]{1,0:T(8,128)S(1)}, f32[8,128]{1,0:T(8,128)S(1)}, u32[]{:S(2)}, u32[]{:S(2)}) %collective-permute-start.15) | collective-permute-done | bytes 4128 | tf_op jit(solution)/shard_map/ppermute | solution.py:296
  58.3 1.2 %collective-permute-done.14 = f32[8,128]{1,0:T(8,128)S(1)} collective-permute-done((f32[8,128]{1,0:T(8,128)S(1)}, f32[8,128]{1,0:T(8,128)S(1)}, u32[]{:S(2)}, u32[]{:S(2)}) %collective-permute-start.14) | collective-permute-done | bytes 4128 | tf_op jit(solution)/shard_map/ppermute | solution.py:296
  59.5 0.7 %collective-permute-done.13 = f32[8,128]{1,0:T(8,128)S(1)} collective-permute-done((f32[8,128]{1,0:T(8,128)S(1)}, f32[8,128]{1,0:T(8,128)S(1)}, u32[]{:S(2)}, u32[]{:S(2)}) %collective-permute-start.13) | collective-permute-done | bytes 4128 | tf_op jit(solution)/shard_map/ppermute | solution.py:296
  60.2 0.6 slice_add_fusion
  (40 shorter events, 2.7 us)
Async XLA Ops:
  1.6 7.4 %collective-permute-start.2 = (bf16[256,128]{1,0:T(8,128)(2,1)}, bf16[256,128]{1,0:T(8,128)(2,1)}, u32[]{:S(2)}, u32[]{:S(2)}) collective-permute-start(bf16[256,128]{1,0:T(8,128)(2,1)} %get-tuple-element.37), channel_id=1, source_target_pairs={{0,6},{2,4},{4,2},{6,0},{8,14},{10,12},{12,10},{14,8},{16,22},{18,... | collective-permute-start | bytes 196616 | tf_op jit(solution)/shard_map/ppermute | solution.py:296
  5.5 4.6 %collective-permute-start.1 = (bf16[256,128]{1,0:T(8,128)(2,1)}, bf16[256,128]{1,0:T(8,128)(2,1)}, u32[]{:S(2)}, u32[]{:S(2)}) collective-permute-start(bf16[256,128]{1,0:T(8,128)(2,1)} %get-tuple-element.38), channel_id=1, source_target_pairs={{0,4},{2,6},{4,0},{6,2},{8,12},{10,14},{12,8},{14,10},{16,20},{18,... | collective-permute-start | bytes 196616 | tf_op jit(solution)/shard_map/ppermute | solution.py:296
  6.0 4.4 %collective-permute-start = (bf16[256,128]{1,0:T(8,128)(2,1)S(1)}, bf16[256,128]{1,0:T(8,128)(2,1)}, u32[]{:S(2)}, u32[]{:S(2)}) collective-permute-start(bf16[256,128]{1,0:T(8,128)(2,1)S(1)} %get-tuple-element.36), channel_id=1, source_target_pairs={{0,2},{2,0},{4,6},{6,4},{8,10},{10,8},{12,14},{14,12},{16,18},{18,... | collective-permute-start | bytes 196616 | tf_op jit(solution)/shard_map/ppermute | solution.py:296
  6.1 1.6 %copy-start.2 = (s32[4,28,16]{1,2,0:T(8,128)S(1)}, s32[4,28,16]{1,2,0:T(8,128)}, u32[]{:S(2)}) copy-start(s32[4,28,16]{1,2,0:T(8,128)} %param.9) | copy-start | bytes 21508
  11.3 8.9 %collective-permute-start.3 = (bf16[1024,128]{1,0:T(8,128)(2,1)S(1)}, bf16[1024,128]{1,0:T(8,128)(2,1)S(1)}, u32[]{:S(2)}, u32[]{:S(2)}) collective-permute-start(bf16[1024,128]{1,0:T(8,128)(2,1)S(1)} %pad_maximum_fusion), channel_id=1, source_target_pairs={{0,8},{2,10},{4,12},{6,14},{8,16},{10,18},{12,20},{14,22},{16,24},... | collective-permute-start | bytes 786440 | tf_op jit(solution)/shard_map/ppermute | solution.py:313
  12.9 11.7 %collective-permute-start.5 = (bf16[272,896]{1,0:T(8,128)(2,1)}, bf16[272,896]{1,0:T(8,128)(2,1)S(1)}, u32[]{:S(2)}, u32[]{:S(2)}) collective-permute-start(bf16[272,896]{1,0:T(8,128)(2,1)} %get-tuple-element.19), channel_id=1, source_target_pairs={{0,2},{2,0},{4,6},{6,4},{8,10},{10,8},{12,14},{14,12},{16,18},{18,... | collective-permute-start | bytes 1462280 | tf_op jit(solution)/shard_map/ppermute | solution.py:296
  13.6 11.6 %collective-permute-start.6 = (bf16[272,896]{1,0:T(8,128)(2,1)S(1)}, bf16[272,896]{1,0:T(8,128)(2,1)S(1)}, u32[]{:S(2)}, u32[]{:S(2)}) collective-permute-start(bf16[272,896]{1,0:T(8,128)(2,1)S(1)} %get-tuple-element.20), channel_id=1, source_target_pairs={{0,4},{2,6},{4,0},{6,2},{8,12},{10,14},{12,8},{14,10},{16,20},{18,... | collective-permute-start | bytes 1462280 | tf_op jit(solution)/shard_map/ppermute | solution.py:296
  20.2 8.2 %collective-permute-start.4 = (bf16[1024,128]{1,0:T(8,128)(2,1)S(1)}, bf16[1024,128]{1,0:T(8,128)(2,1)S(1)}, u32[]{:S(2)}, u32[]{:S(2)}) collective-permute-start(bf16[1024,128]{1,0:T(8,128)(2,1)S(1)} %collective-permute-done.3), channel_id=1, source_target_pairs={{0,8},{2,10},{4,12},{6,14},{8,16},{10,18},{12,20},{14,22},{16,24},... | collective-permute-start | bytes 786440 | tf_op jit(solution)/shard_map/ppermute | solution.py:313
  20.3 18.8 %copy-start = (bf16[384,128]{1,0:T(8,128)(2,1)S(1)}, bf16[384,128]{1,0:T(8,128)(2,1)}, u32[]{:S(2)}) copy-start(bf16[384,128]{1,0:T(8,128)(2,1)} %refs_9_.1) | copy-start | bytes 294916
  20.3 18.8 %copy-start.1 = (bf16[128,128]{1,0:T(8,128)(2,1)S(1)}, bf16[128,128]{1,0:T(8,128)(2,1)}, u32[]{:S(2)}) copy-start(bf16[128,128]{1,0:T(8,128)(2,1)} %refs_8_.1) | copy-start | bytes 98308
  20.3 16.2 %collective-permute-start.8 = (bf16[1024,128]{1,0:T(8,128)(2,1)S(1)}, bf16[1024,128]{1,0:T(8,128)(2,1)S(1)}, u32[]{:S(2)}, u32[]{:S(2)}) collective-permute-start(bf16[1024,128]{1,0:T(8,128)(2,1)S(1)} %pad_maximum_fusion), channel_id=1, source_target_pairs={{0,1},{1,0},{2,3},{3,2},{4,5},{5,4},{6,7},{7,6},{8,9},{9,8},{10,11... | collective-permute-start | bytes 786440 | tf_op jit(solution)/shard_map/ppermute | solution.py:299
  28.3 8.2 %collective-permute-start.11 = (bf16[1024,128]{1,0:T(8,128)(2,1)S(1)}, bf16[1024,128]{1,0:T(8,128)(2,1)S(1)}, u32[]{:S(2)}, u32[]{:S(2)}) collective-permute-start(bf16[1024,128]{1,0:T(8,128)(2,1)S(1)} %collective-permute-done.4), channel_id=1, source_target_pairs={{0,8},{2,10},{4,12},{6,14},{8,16},{10,18},{12,20},{14,22},{16,24},... | collective-permute-start | bytes 786440 | tf_op jit(solution)/shard_map/ppermute | solution.py:313
  28.4 10.7 %collective-permute-start.7 = (bf16[272,896]{1,0:T(8,128)(2,1)S(1)}, bf16[272,896]{1,0:T(8,128)(2,1)S(1)}, u32[]{:S(2)}, u32[]{:S(2)}) collective-permute-start(bf16[272,896]{1,0:T(8,128)(2,1)S(1)} %get-tuple-element.25), channel_id=1, source_target_pairs={{0,6},{2,4},{4,2},{6,0},{8,14},{10,12},{12,10},{14,8},{16,22},{18,... | collective-permute-start | bytes 1462280 | tf_op jit(solution)/shard_map/ppermute | solution.py:296
  30.3 6.3 %collective-permute-start.9 = (bf16[1024,128]{1,0:T(8,128)(2,1)S(1)}, bf16[1024,128]{1,0:T(8,128)(2,1)S(1)}, u32[]{:S(2)}, u32[]{:S(2)}) collective-permute-start(bf16[1024,128]{1,0:T(8,128)(2,1)S(1)} %collective-permute-done.3), channel_id=1, source_target_pairs={{0,1},{1,0},{2,3},{3,2},{4,5},{5,4},{6,7},{7,6},{8,9},{9,8},{10,11... | collective-permute-start | bytes 786440 | tf_op jit(solution)/shard_map/ppermute | solution.py:299
  30.3 6.3 %collective-permute-start.10 = (bf16[1024,128]{1,0:T(8,128)(2,1)S(1)}, bf16[1024,128]{1,0:T(8,128)(2,1)S(1)}, u32[]{:S(2)}, u32[]{:S(2)}) collective-permute-start(bf16[1024,128]{1,0:T(8,128)(2,1)S(1)} %collective-permute-done.4), channel_id=1, source_target_pairs={{0,1},{1,0},{2,3},{3,2},{4,5},{5,4},{6,7},{7,6},{8,9},{9,8},{10,11... | collective-permute-start | bytes 786440 | tf_op jit(solution)/shard_map/ppermute | solution.py:299
  36.5 2.6 %collective-permute-start.12 = (bf16[1024,128]{1,0:T(8,128)(2,1)S(1)}, bf16[1024,128]{1,0:T(8,128)(2,1)S(1)}, u32[]{:S(2)}, u32[]{:S(2)}) collective-permute-start(bf16[1024,128]{1,0:T(8,128)(2,1)S(1)} %collective-permute-done.11.refs_6_), channel_id=1, source_target_pairs={{0,1},{1,0},{2,3},{3,2},{4,5},{5,4},{6,7},{7,6},{8,9},{9,8},{10,11... | collective-permute-start | bytes 786440 | tf_op jit(solution)/shard_map/ppermute | solution.py:299
  53.7 4.6 %collective-permute-start.15 = (f32[8,128]{1,0:T(8,128)S(1)}, f32[8,128]{1,0:T(8,128)S(1)}, u32[]{:S(2)}, u32[]{:S(2)}) collective-permute-start(f32[8,128]{1,0:T(8,128)S(1)} %get-tuple-element.30), channel_id=1, source_target_pairs={{0,6},{2,4},{4,2},{6,0},{8,14},{10,12},{12,10},{14,8},{16,22},{18,... | collective-permute-start | bytes 12296 | tf_op jit(solution)/shard_map/ppermute | solution.py:296
  55.9 3.6 %collective-permute-start.14 = (f32[8,128]{1,0:T(8,128)S(1)}, f32[8,128]{1,0:T(8,128)S(1)}, u32[]{:S(2)}, u32[]{:S(2)}) collective-permute-start(f32[8,128]{1,0:T(8,128)S(1)} %get-tuple-element.29), channel_id=1, source_target_pairs={{0,4},{2,6},{4,0},{6,2},{8,12},{10,14},{12,8},{14,10},{16,20},{18,... | collective-permute-start | bytes 12296 | tf_op jit(solution)/shard_map/ppermute | solution.py:296
  56.6 3.6 %collective-permute-start.13 = (f32[8,128]{1,0:T(8,128)S(1)}, f32[8,128]{1,0:T(8,128)S(1)}, u32[]{:S(2)}, u32[]{:S(2)}) collective-permute-start(f32[8,128]{1,0:T(8,128)S(1)} %get-tuple-element.28), channel_id=1, source_target_pairs={{0,2},{2,0},{4,6},{6,4},{8,10},{10,8},{12,14},{14,12},{16,18},{18,... | collective-permute-start | bytes 12296 | tf_op jit(solution)/shard_map/ppermute | solution.py:296

commit v6 on v5

--- a/solution.py
+++ b/solution.py
@@ -302,14 +302,16 @@
         flipped(lax.dynamic_slice_in_dim(key_state_rows, (spot ^ p) * head_size, head_size, 1), p)
         for p in range(plane)
     ]
-    parts = [lax.dynamic_slice_in_dim(sent, (spot ^ p) * width, width, 1) for p in range(plane)]
+    parts = [lax.dynamic_slice_in_dim(sent, (spot ^ p) * width, width, 1) for p in range(plane - 1)]
+    for first, count in ((0, 64), (64, stride - 64)):
+        parts.append(lax.dynamic_slice(sent, (first, (spot ^ (plane - 1)) * width), (count, width)))
     steps = [jnp.concatenate(keys, axis=0)]
     other = []
     steps[0], parts = lax.optimization_barrier((steps[0], parts))
-    pieces = [flipped(x, p) for p, x in enumerate(parts)]
+    pieces = [flipped(x, min(p, plane - 1)) for p, x in enumerate(parts)]
     for i in range(layers - 1):
         if i == 2:
-            steps[2], pieces[1:3], cand = lax.optimization_barrier((steps[2], pieces[1:3], cand))
+            steps[2], pieces[1:4], cand = lax.optimization_barrier((steps[2], pieces[1:4], cand))
         steps.append(lax.ppermute(steps[i], "ctx", [(j, (j + plane) % n_ctx) for j in range(n_ctx)]))
     other += [other_core(x) for x in steps[len(other) :]]
     k_pieces = [jnp.concatenate(steps[:-1] + other[:-1], axis=0), steps[-1], other[-1]]

time: 61 us -> 60.6 us (level)
  waiting for transfers between devices: 24.4 us -> 21 us
  starting transfers between devices: 14.4 us -> 16.7 us
    ppermute x3, waiting for transfers between devices: 12.8 us -> 7.59 us  [per_device(): lax.ppermute(steps[i], 'ctx', [(j, (j + plane) % n_ctx) for j in range(n_...]
    ppermute x9 -> x10, waiting for transfers between devices: 11.5 us -> 13.4 us  [flipped(): lax.ppermute(x, 'ctx', [(i, i ^ p) for i in range(n_ctx)])]
    dynamic_slice x0 -> x2, local copies, waits for them, and re-layouts: none -> 1.44 us  [per_device(): lax.dynamic_slice(sent, (first, (spot ^ plane - 1) * width), (count, width))]
    ppermute x3, starting transfers between devices: 1.63 us -> 2.97 us  [per_device(): lax.ppermute(steps[i], 'ctx', [(j, (j + plane) % n_ctx) for j in range(n_...]
    ppermute x9 -> x10, starting transfers between devices: 12.1 us -> 13.1 us  [flipped(): lax.ppermute(x, 'ctx', [(i, i ^ p) for i in range(n_ctx)])]
    dynamic_slice x1, local copies, waits for them, and re-layouts: 0.97 us -> 0.12 us  [per_device(): lax.dynamic_slice_in_dim(sent, (spot ^ p) * width, width, 1)]
  transfers between devices with their start and end apart: 16 -> 17, of which waited for: 11 -> 11; matrix products, arithmetic and copies ran while one was open for 7% -> 8% of each run, Pallas kernels for 0% -> 0%
where the time goes in v6:
time: 60.6 us; the launch traced here: 60.3 us
  waiting for transfers between devices  21 us (35%)
  starting transfers between devices  16.7 us (28%)
  Pallas kernels  14.6 us (24%)
  local copies, waits for them, and re-layouts  6.19 us (10%)
  other arithmetic  1.64 us (3%)
    pallas_call x1, Pallas kernels, gate_call(): pl.pallas_call(functools.partial(gate_kernel, dims), out_shape=[jax.Shape...  14.6 us
    ppermute x10, waiting for transfers between devices, flipped(): lax.ppermute(x, 'ctx', [(i, i ^ p) for i in range(n_ctx)])  13.4 us
    ppermute x10, starting transfers between devices, flipped(): lax.ppermute(x, 'ctx', [(i, i ^ p) for i in range(n_ctx)])  13.1 us
    ppermute x3, waiting for transfers between devices, per_device(): lax.ppermute(steps[i], 'ctx', [(j, (j + plane) % n_ctx) for j in range(n_...  7.59 us
    ppermute x3, starting transfers between devices, per_device(): lax.ppermute(steps[i], 'ctx', [(j, (j + plane) % n_ctx) for j in range(n_...  2.97 us
    unnamed x13, local copies, waits for them, and re-layouts  1.81 us
    dynamic_slice x1, local copies, waits for them, and re-layouts, per_device(): lax.dynamic_slice_in_dim(key_state_rows, (spot ^ p) * head_size, head_siz...  1.61 us
    dynamic_slice x2, local copies, waits for them, and re-layouts, per_device(): lax.dynamic_slice(sent, (first, (spot ^ plane - 1) * width), (count, width))  1.44 us
  transfers between devices with their start and end apart: 17, of which 11 were waited for; matrix products, arithmetic and copies ran while one was open for 8% of the time, Pallas kernels for 0%

profile of v6, /device:TPU:0, one launch (start us, length us, event | category | flops | bytes accessed | tf_op | source)
XLA Modules:
  0.0 60.3 jit_solution(15841506567549217225)
XLA Ops:
  0.0 1.6 %constant_dynamic-slice_fusion.11 = (bf16[256,128]{1,0:T(8,128)(2,1)S(1)}, bf16[256,128]{1,0:T(8,128)(2,1)S(1)}, bf16[256,128]{1,0:T(8,128)(2,1)}, bf16[256,128]{1,0:T(8,128)(2,1)}) fusion(bf16[256,512]{1,0:T(8,128)(2,1)} %param.7, s32[]{:T(128)S(6)} %select_n.82, s32[]{:T(128)S(6)} %select_n.83, s32[]{:T(128)S(6)} %select_n.85, s32[]{:T(128)S(6)} %select_n.84), kind=kLoop, calls=%fused_computation.20 | loop fusion | bytes 524304 | tf_op jit(solution)/shard_map/dynamic_slice | solution.py:302
  1.6 3.9 %collective-permute-start.2 = (bf16[256,128]{1,0:T(8,128)(2,1)}, bf16[256,128]{1,0:T(8,128)(2,1)}, u32[]{:S(2)}, u32[]{:S(2)}) collective-permute-start(bf16[256,128]{1,0:T(8,128)(2,1)} %get-tuple-element.40), channel_id=1, source_target_pairs={{0,6},{2,4},{4,2},{6,0},{8,14},{10,12},{12,10},{14,8},{16,22},{18,... | collective-permute-start | bytes 196616 | tf_op jit(solution)/shard_map/ppermute | solution.py:296
  6.1 1.6 %constant_dynamic-update-slice_fusion.1 = bf16[272,3584]{1,0:T(8,128)(2,1)S(1)} fusion(bf16[256,3584]{1,0:T(8,128)(2,1)} %param.6), kind=kLoop, calls=%fused_computation.2 | loop fusion | bytes 3670016
  8.0 0.7 %constant_dynamic-slice_fusion.4 = bf16[64,896]{1,0:T(8,128)(2,1)} fusion(bf16[272,3584]{1,0:T(8,128)(2,1)S(1)} %constant_dynamic-update-slice_fusion, s32[]{:T(128)S(6)} %select_n.89), kind=kLoop, calls=%fused_computation.13 | loop fusion | bytes 229380 | tf_op jit(solution)/shard_map/dynamic_slice | solution.py:307
  8.7 0.8 %constant_dynamic-slice_fusion.12 = bf16[208,896]{1,0:T(8,128)(2,1)} fusion(bf16[272,3584]{1,0:T(8,128)(2,1)S(1)} %constant_dynamic-update-slice_fusion, s32[]{:T(128)S(6)} %select_n.89), kind=kLoop, calls=%fused_computation.61 | loop fusion | bytes 745476 | tf_op jit(solution)/shard_map/dynamic_slice | solution.py:307
  10.4 0.9 %pad_maximum_fusion = bf16[1024,128]{1,0:T(8,128)(2,1)S(1)} fusion(bf16[256,128]{1,0:T(8,128)(2,1)} %collective-permute-done.2, bf16[256,128]{1,0:T(8,128)(2,1)} %collective-permute-done.1, bf16[256,128]{1,0:T(8,128)(2,1)} %collective-permute-done, bf16[256,128]{1,0:T(8,128)(2,1)S(1)} %get-tuple-element.38), kind=kLoop, calls=%fused_computation | loop fusion | flops 1048576 | bytes 524288 | tf_op jit(solution)/shard_map/concatenate | solution.py:308
  11.3 1.6 %collective-permute-start.3 = (bf16[1024,128]{1,0:T(8,128)(2,1)S(1)}, bf16[1024,128]{1,0:T(8,128)(2,1)S(1)}, u32[]{:S(2)}, u32[]{:S(2)}) collective-permute-start(bf16[1024,128]{1,0:T(8,128)(2,1)S(1)} %pad_maximum_fusion), channel_id=1, source_target_pairs={{0,8},{2,10},{4,12},{6,14},{8,16},{10,18},{12,20},{14,22},{16,24},... | collective-permute-start | bytes 786440 | tf_op jit(solution)/shard_map/ppermute | solution.py:315
  12.9 1.2 %collective-permute-start.5 = (bf16[272,896]{1,0:T(8,128)(2,1)S(1)}, bf16[272,896]{1,0:T(8,128)(2,1)S(1)}, u32[]{:S(2)}, u32[]{:S(2)}) collective-permute-start(bf16[272,896]{1,0:T(8,128)(2,1)S(1)} %get-tuple-element.21), channel_id=1, source_target_pairs={{0,2},{2,0},{4,6},{6,4},{8,10},{10,8},{12,14},{14,12},{16,18},{18,... | collective-permute-start | bytes 1462280 | tf_op jit(solution)/shard_map/ppermute | solution.py:296
  14.2 1.5 %collective-permute-start.6 = (bf16[272,896]{1,0:T(8,128)(2,1)S(1)}, bf16[272,896]{1,0:T(8,128)(2,1)S(1)}, u32[]{:S(2)}, u32[]{:S(2)}) collective-permute-start(bf16[272,896]{1,0:T(8,128)(2,1)S(1)} %get-tuple-element.22), channel_id=1, source_target_pairs={{0,4},{2,6},{4,0},{6,2},{8,12},{10,14},{12,8},{14,10},{16,20},{18,... | collective-permute-start | bytes 1462280 | tf_op jit(solution)/shard_map/ppermute | solution.py:296
  15.7 0.8 %fusion.10 = (s32[31]{0:T(128)S(1)}, s32[31]{0:T(128)S(1)}, s32[31]{0:T(128)S(1)}, s32[31]{0:T(128)S(1)}) fusion(s32[32,31]{1,0:T(8,128)} %param.8, s32[]{:T(128)S(6)} %select_n.94, s32[]{:T(128)S(6)} %select_n.92, s32[]{:T(128)S(6)} %select_n.91, s32[]{:T(128)S(6)} %select_n.93), kind=kLoop, calls=%fused_computation.52 | loop fusion | bytes 1008 | tf_op jit(solution)/shard_map/jit(dynamic_index_in_dim)/squeeze | solution.py:262
  16.6 0.8 %collective-permute-start.7 = (bf16[64,896]{1,0:T(8,128)(2,1)}, bf16[64,896]{1,0:T(8,128)(2,1)S(1)}, u32[]{:S(2)}, u32[]{:S(2)}) collective-permute-start(bf16[64,896]{1,0:T(8,128)(2,1)} %constant_dynamic-slice_fusion.4), channel_id=1, source_target_pairs={{0,6},{2,4},{4,2},{6,0},{8,14},{10,12},{12,10},{14,8},{16,22},{18,... | collective-permute-start | bytes 344072 | tf_op jit(solution)/shard_map/ppermute | solution.py:296
  17.4 2.7 %collective-permute-done.3 = bf16[1024,128]{1,0:T(8,128)(2,1)S(1)} collective-permute-done((bf16[1024,128]{1,0:T(8,128)(2,1)S(1)}, bf16[1024,128]{1,0:T(8,128)(2,1)S(1)}, u32[]{:S(2)}, u32[]{:S(2)}) %collective-permute-start.3) | collective-permute-done | bytes 262176 | tf_op jit(solution)/shard_map/ppermute | solution.py:315
  20.3 7.6 %collective-permute-done.7.refs_4_ = bf16[64,896]{1,0:T(8,128)(2,1)S(1)} collective-permute-done((bf16[64,896]{1,0:T(8,128)(2,1)}, bf16[64,896]{1,0:T(8,128)(2,1)S(1)}, u32[]{:S(2)}, u32[]{:S(2)}) %collective-permute-start.7) | collective-permute-done | bytes 114720 | tf_op jit(solution)/shard_map/ppermute | solution.py:296
  28.3 1.3 %collective-permute-start.12 = (bf16[1024,128]{1,0:T(8,128)(2,1)S(1)}, bf16[1024,128]{1,0:T(8,128)(2,1)S(1)}, u32[]{:S(2)}, u32[]{:S(2)}) collective-permute-start(bf16[1024,128]{1,0:T(8,128)(2,1)S(1)} %collective-permute-done.4), channel_id=1, source_target_pairs={{0,8},{2,10},{4,12},{6,14},{8,16},{10,18},{12,20},{14,22},{16,24},... | collective-permute-start | bytes 786440 | tf_op jit(solution)/shard_map/ppermute | solution.py:315
  29.7 1.6 %collective-permute-start.8 = (bf16[208,896]{1,0:T(8,128)(2,1)}, bf16[208,896]{1,0:T(8,128)(2,1)S(1)}, u32[]{:S(2)}, u32[]{:S(2)}) collective-permute-start(bf16[208,896]{1,0:T(8,128)(2,1)} %constant_dynamic-slice_fusion.12), channel_id=1, source_target_pairs={{0,6},{2,4},{4,2},{6,0},{8,14},{10,12},{12,10},{14,8},{16,22},{18,... | collective-permute-start | bytes 1118216 | tf_op jit(solution)/shard_map/ppermute | solution.py:296
  31.9 4.6 %collective-permute-done.12.refs_7_ = bf16[1024,128]{1,0:T(8,128)(2,1)S(1)} collective-permute-done((bf16[1024,128]{1,0:T(8,128)(2,1)S(1)}, bf16[1024,128]{1,0:T(8,128)(2,1)S(1)}, u32[]{:S(2)}, u32[]{:S(2)}) %collective-permute-start.12) | collective-permute-done | bytes 262176 | tf_op jit(solution)/shard_map/ppermute | solution.py:315
  36.7 1.8 %collective-permute-done.8.refs_5_ = bf16[208,896]{1,0:T(8,128)(2,1)S(1)} collective-permute-done((bf16[208,896]{1,0:T(8,128)(2,1)}, bf16[208,896]{1,0:T(8,128)(2,1)S(1)}, u32[]{:S(2)}, u32[]{:S(2)}) %collective-permute-start.8) | collective-permute-done | bytes 372768 | tf_op jit(solution)/shard_map/ppermute | solution.py:296
  38.4 14.6 %shard_map.64 = (f32[8,128]{1,0:T(8,128)S(1)}, f32[8,128]{1,0:T(8,128)S(1)}, f32[8,128]{1,0:T(8,128)S(1)}, f32[8,128]{1,0:T(8,128)S(1)}) custom-call(s32[157]{0:T(256)S(1)} %pad_add_fusion.refs_0_, bf16[272,896]{1,0:T(8,128)(2,1)S(1)} %get-tuple-element.25.refs_1_, bf16[272,896]{1,0:T(8,128)(2,1)S(1)} %collective-permute-done.5.refs_2_, ...), custom_call_target="tpu_custom_call" | custom-call | tf_op jit(solution)/shard_map/pallas_call | solution.py:203
  53.0 2.1 %collective-permute-start.16 = (f32[8,128]{1,0:T(8,128)S(1)}, f32[8,128]{1,0:T(8,128)S(1)}, u32[]{:S(2)}, u32[]{:S(2)}) collective-permute-start(f32[8,128]{1,0:T(8,128)S(1)} %get-tuple-element.34), channel_id=1, source_target_pairs={{0,6},{2,4},{4,2},{6,0},{8,14},{10,12},{12,10},{14,8},{16,22},{18,... | collective-permute-start | bytes 12296 | tf_op jit(solution)/shard_map/ppermute | solution.py:296
  55.2 0.9 %collective-permute-start.15 = (f32[8,128]{1,0:T(8,128)S(1)}, f32[8,128]{1,0:T(8,128)S(1)}, u32[]{:S(2)}, u32[]{:S(2)}) collective-permute-start(f32[8,128]{1,0:T(8,128)S(1)} %get-tuple-element.33), channel_id=1, source_target_pairs={{0,4},{2,6},{4,0},{6,2},{8,12},{10,14},{12,8},{14,10},{16,20},{18,... | collective-permute-start | bytes 12296 | tf_op jit(solution)/shard_map/ppermute | solution.py:296
  56.6 1.0 %collective-permute-done.16 = f32[8,128]{1,0:T(8,128)S(1)} collective-permute-done((f32[8,128]{1,0:T(8,128)S(1)}, f32[8,128]{1,0:T(8,128)S(1)}, u32[]{:S(2)}, u32[]{:S(2)}) %collective-permute-start.16) | collective-permute-done | bytes 4128 | tf_op jit(solution)/shard_map/ppermute | solution.py:296
  57.6 1.2 %collective-permute-done.15 = f32[8,128]{1,0:T(8,128)S(1)} collective-permute-done((f32[8,128]{1,0:T(8,128)S(1)}, f32[8,128]{1,0:T(8,128)S(1)}, u32[]{:S(2)}, u32[]{:S(2)}) %collective-permute-start.15) | collective-permute-done | bytes 4128 | tf_op jit(solution)/shard_map/ppermute | solution.py:296
  58.8 0.9 %collective-permute-done.14 = f32[8,128]{1,0:T(8,128)S(1)} collective-permute-done((f32[8,128]{1,0:T(8,128)S(1)}, f32[8,128]{1,0:T(8,128)S(1)}, u32[]{:S(2)}, u32[]{:S(2)}) %collective-permute-start.14) | collective-permute-done | bytes 4128 | tf_op jit(solution)/shard_map/ppermute | solution.py:296
  59.7 0.6 slice_add_fusion
  (44 shorter events, 3.7 us)
Async XLA Ops:
  1.6 8.0 %collective-permute-start.2 = (bf16[256,128]{1,0:T(8,128)(2,1)}, bf16[256,128]{1,0:T(8,128)(2,1)}, u32[]{:S(2)}, u32[]{:S(2)}) collective-permute-start(bf16[256,128]{1,0:T(8,128)(2,1)} %get-tuple-element.40), channel_id=1, source_target_pairs={{0,6},{2,4},{4,2},{6,0},{8,14},{10,12},{12,10},{14,8},{16,22},{18,... | collective-permute-start | bytes 196616 | tf_op jit(solution)/shard_map/ppermute | solution.py:296
  5.5 4.6 %collective-permute-start.1 = (bf16[256,128]{1,0:T(8,128)(2,1)}, bf16[256,128]{1,0:T(8,128)(2,1)}, u32[]{:S(2)}, u32[]{:S(2)}) collective-permute-start(bf16[256,128]{1,0:T(8,128)(2,1)} %get-tuple-element.41), channel_id=1, source_target_pairs={{0,4},{2,6},{4,0},{6,2},{8,12},{10,14},{12,8},{14,10},{16,20},{18,... | collective-permute-start | bytes 196616 | tf_op jit(solution)/shard_map/ppermute | solution.py:296
  6.0 4.4 %collective-permute-start = (bf16[256,128]{1,0:T(8,128)(2,1)S(1)}, bf16[256,128]{1,0:T(8,128)(2,1)}, u32[]{:S(2)}, u32[]{:S(2)}) collective-permute-start(bf16[256,128]{1,0:T(8,128)(2,1)S(1)} %get-tuple-element.39), channel_id=1, source_target_pairs={{0,2},{2,0},{4,6},{6,4},{8,10},{10,8},{12,14},{14,12},{16,18},{18,... | collective-permute-start | bytes 196616 | tf_op jit(solution)/shard_map/ppermute | solution.py:296
  6.1 1.6 %copy-start.2 = (s32[4,28,16]{1,2,0:T(8,128)S(1)}, s32[4,28,16]{1,2,0:T(8,128)}, u32[]{:S(2)}) copy-start(s32[4,28,16]{1,2,0:T(8,128)} %param.9) | copy-start | bytes 21508
  11.3 8.9 %collective-permute-start.3 = (bf16[1024,128]{1,0:T(8,128)(2,1)S(1)}, bf16[1024,128]{1,0:T(8,128)(2,1)S(1)}, u32[]{:S(2)}, u32[]{:S(2)}) collective-permute-start(bf16[1024,128]{1,0:T(8,128)(2,1)S(1)} %pad_maximum_fusion), channel_id=1, source_target_pairs={{0,8},{2,10},{4,12},{6,14},{8,16},{10,18},{12,20},{14,22},{16,24},... | collective-permute-start | bytes 786440 | tf_op jit(solution)/shard_map/ppermute | solution.py:315
  12.9 15.0 %collective-permute-start.5 = (bf16[272,896]{1,0:T(8,128)(2,1)S(1)}, bf16[272,896]{1,0:T(8,128)(2,1)S(1)}, u32[]{:S(2)}, u32[]{:S(2)}) collective-permute-start(bf16[272,896]{1,0:T(8,128)(2,1)S(1)} %get-tuple-element.21), channel_id=1, source_target_pairs={{0,2},{2,0},{4,6},{6,4},{8,10},{10,8},{12,14},{14,12},{16,18},{18,... | collective-permute-start | bytes 1462280 | tf_op jit(solution)/shard_map/ppermute | solution.py:296
  14.2 13.9 %collective-permute-start.6 = (bf16[272,896]{1,0:T(8,128)(2,1)S(1)}, bf16[272,896]{1,0:T(8,128)(2,1)S(1)}, u32[]{:S(2)}, u32[]{:S(2)}) collective-permute-start(bf16[272,896]{1,0:T(8,128)(2,1)S(1)} %get-tuple-element.22), channel_id=1, source_target_pairs={{0,4},{2,6},{4,0},{6,2},{8,12},{10,14},{12,8},{14,10},{16,20},{18,... | collective-permute-start | bytes 1462280 | tf_op jit(solution)/shard_map/ppermute | solution.py:296
  16.6 11.3 %collective-permute-start.7 = (bf16[64,896]{1,0:T(8,128)(2,1)}, bf16[64,896]{1,0:T(8,128)(2,1)S(1)}, u32[]{:S(2)}, u32[]{:S(2)}) collective-permute-start(bf16[64,896]{1,0:T(8,128)(2,1)} %constant_dynamic-slice_fusion.4), channel_id=1, source_target_pairs={{0,6},{2,4},{4,2},{6,0},{8,14},{10,12},{12,10},{14,8},{16,22},{18,... | collective-permute-start | bytes 344072 | tf_op jit(solution)/shard_map/ppermute | solution.py:296
  20.2 8.2 %collective-permute-start.4 = (bf16[1024,128]{1,0:T(8,128)(2,1)S(1)}, bf16[1024,128]{1,0:T(8,128)(2,1)S(1)}, u32[]{:S(2)}, u32[]{:S(2)}) collective-permute-start(bf16[1024,128]{1,0:T(8,128)(2,1)S(1)} %collective-permute-done.3), channel_id=1, source_target_pairs={{0,8},{2,10},{4,12},{6,14},{8,16},{10,18},{12,20},{14,22},{16,24},... | collective-permute-start | bytes 786440 | tf_op jit(solution)/shard_map/ppermute | solution.py:315
  20.3 18.1 %copy-start = (bf16[384,128]{1,0:T(8,128)(2,1)S(1)}, bf16[384,128]{1,0:T(8,128)(2,1)}, u32[]{:S(2)}) copy-start(bf16[384,128]{1,0:T(8,128)(2,1)} %refs_10_.1) | copy-start | bytes 294916
  20.3 18.1 %copy-start.1 = (bf16[128,128]{1,0:T(8,128)(2,1)S(1)}, bf16[128,128]{1,0:T(8,128)(2,1)}, u32[]{:S(2)}) copy-start(bf16[128,128]{1,0:T(8,128)(2,1)} %refs_9_.1) | copy-start | bytes 98308
  20.3 16.2 %collective-permute-start.9 = (bf16[1024,128]{1,0:T(8,128)(2,1)S(1)}, bf16[1024,128]{1,0:T(8,128)(2,1)S(1)}, u32[]{:S(2)}, u32[]{:S(2)}) collective-permute-start(bf16[1024,128]{1,0:T(8,128)(2,1)S(1)} %pad_maximum_fusion), channel_id=1, source_target_pairs={{0,1},{1,0},{2,3},{3,2},{4,5},{5,4},{6,7},{7,6},{8,9},{9,8},{10,11... | collective-permute-start | bytes 786440 | tf_op jit(solution)/shard_map/ppermute | solution.py:299
  28.3 8.2 %collective-permute-start.12 = (bf16[1024,128]{1,0:T(8,128)(2,1)S(1)}, bf16[1024,128]{1,0:T(8,128)(2,1)S(1)}, u32[]{:S(2)}, u32[]{:S(2)}) collective-permute-start(bf16[1024,128]{1,0:T(8,128)(2,1)S(1)} %collective-permute-done.4), channel_id=1, source_target_pairs={{0,8},{2,10},{4,12},{6,14},{8,16},{10,18},{12,20},{14,22},{16,24},... | collective-permute-start | bytes 786440 | tf_op jit(solution)/shard_map/ppermute | solution.py:315
  29.7 8.7 %collective-permute-start.8 = (bf16[208,896]{1,0:T(8,128)(2,1)}, bf16[208,896]{1,0:T(8,128)(2,1)S(1)}, u32[]{:S(2)}, u32[]{:S(2)}) collective-permute-start(bf16[208,896]{1,0:T(8,128)(2,1)} %constant_dynamic-slice_fusion.12), channel_id=1, source_target_pairs={{0,6},{2,4},{4,2},{6,0},{8,14},{10,12},{12,10},{14,8},{16,22},{18,... | collective-permute-start | bytes 1118216 | tf_op jit(solution)/shard_map/ppermute | solution.py:296
  31.3 5.3 %collective-permute-start.10 = (bf16[1024,128]{1,0:T(8,128)(2,1)S(1)}, bf16[1024,128]{1,0:T(8,128)(2,1)S(1)}, u32[]{:S(2)}, u32[]{:S(2)}) collective-permute-start(bf16[1024,128]{1,0:T(8,128)(2,1)S(1)} %collective-permute-done.3), channel_id=1, source_target_pairs={{0,1},{1,0},{2,3},{3,2},{4,5},{5,4},{6,7},{7,6},{8,9},{9,8},{10,11... | collective-permute-start | bytes 786440 | tf_op jit(solution)/shard_map/ppermute | solution.py:299
  31.3 5.3 %collective-permute-start.11 = (bf16[1024,128]{1,0:T(8,128)(2,1)S(1)}, bf16[1024,128]{1,0:T(8,128)(2,1)S(1)}, u32[]{:S(2)}, u32[]{:S(2)}) collective-permute-start(bf16[1024,128]{1,0:T(8,128)(2,1)S(1)} %collective-permute-done.4), channel_id=1, source_target_pairs={{0,1},{1,0},{2,3},{3,2},{4,5},{5,4},{6,7},{7,6},{8,9},{9,8},{10,11... | collective-permute-start | bytes 786440 | tf_op jit(solution)/shard_map/ppermute | solution.py:299
  36.5 1.9 %collective-permute-start.13 = (bf16[1024,128]{1,0:T(8,128)(2,1)S(1)}, bf16[1024,128]{1,0:T(8,128)(2,1)S(1)}, u32[]{:S(2)}, u32[]{:S(2)}) collective-permute-start(bf16[1024,128]{1,0:T(8,128)(2,1)S(1)} %collective-permute-done.12.refs_7_), channel_id=1, source_target_pairs={{0,1},{1,0},{2,3},{3,2},{4,5},{5,4},{6,7},{7,6},{8,9},{9,8},{10,11... | collective-permute-start | bytes 786440 | tf_op jit(solution)/shard_map/ppermute | solution.py:299
  53.0 4.6 %collective-permute-start.16 = (f32[8,128]{1,0:T(8,128)S(1)}, f32[8,128]{1,0:T(8,128)S(1)}, u32[]{:S(2)}, u32[]{:S(2)}) collective-permute-start(f32[8,128]{1,0:T(8,128)S(1)} %get-tuple-element.34), channel_id=1, source_target_pairs={{0,6},{2,4},{4,2},{6,0},{8,14},{10,12},{12,10},{14,8},{16,22},{18,... | collective-permute-start | bytes 12296 | tf_op jit(solution)/shard_map/ppermute | solution.py:296
  55.2 3.6 %collective-permute-start.15 = (f32[8,128]{1,0:T(8,128)S(1)}, f32[8,128]{1,0:T(8,128)S(1)}, u32[]{:S(2)}, u32[]{:S(2)}) collective-permute-start(f32[8,128]{1,0:T(8,128)S(1)} %get-tuple-element.33), channel_id=1, source_target_pairs={{0,4},{2,6},{4,0},{6,2},{8,12},{10,14},{12,8},{14,10},{16,20},{18,... | collective-permute-start | bytes 12296 | tf_op jit(solution)/shard_map/ppermute | solution.py:296
  56.1 3.6 %collective-permute-start.14 = (f32[8,128]{1,0:T(8,128)S(1)}, f32[8,128]{1,0:T(8,128)S(1)}, u32[]{:S(2)}, u32[]{:S(2)}) collective-permute-start(f32[8,128]{1,0:T(8,128)S(1)} %get-tuple-element.32), channel_id=1, source_target_pairs={{0,2},{2,0},{4,6},{6,4},{8,10},{10,8},{12,14},{14,12},{16,18},{18,... | collective-permute-start | bytes 12296 | tf_op jit(solution)/shard_map/ppermute | solution.py:296

commit v7 on v6

--- a/solution.py
+++ b/solution.py
@@ -156,7 +156,7 @@
         return carry
 
     head_step(0, 0)
-    lax.fori_loop(0, n_piece * heads, combine_step, 0, unroll=14)
+    lax.fori_loop(0, n_piece * heads, combine_step, 0, unroll=28)
 
     for copy in w_copies:
         copy.wait()

time: 60.6 us -> 59 us (0.974)
  Pallas kernels: 14.6 us -> 13 us
    pallas_call x1, Pallas kernels: 14.6 us -> 13 us  [gate_call(): pl.pallas_call(functools.partial(gate_kernel, dims), out_shape=[jax.Shape...]
where the time goes in v7:
time: 59 us; the launch traced here: 58.7 us
  waiting for transfers between devices  21 us (36%)
  starting transfers between devices  16.7 us (28%)
  Pallas kernels  13 us (22%)
  local copies, waits for them, and re-layouts  6.19 us (10%)
  other arithmetic  1.64 us (3%)
    ppermute x10, waiting for transfers between devices, flipped(): lax.ppermute(x, 'ctx', [(i, i ^ p) for i in range(n_ctx)])  13.4 us
    ppermute x10, starting transfers between devices, flipped(): lax.ppermute(x, 'ctx', [(i, i ^ p) for i in range(n_ctx)])  13.1 us
    pallas_call x1, Pallas kernels, gate_call(): pl.pallas_call(functools.partial(gate_kernel, dims), out_shape=[jax.Shape...  13 us
    ppermute x3, waiting for transfers between devices, per_device(): lax.ppermute(steps[i], 'ctx', [(j, (j + plane) % n_ctx) for j in range(n_...  7.59 us
    ppermute x3, starting transfers between devices, per_device(): lax.ppermute(steps[i], 'ctx', [(j, (j + plane) % n_ctx) for j in range(n_...  2.97 us
    unnamed x13, local copies, waits for them, and re-layouts  1.81 us
    dynamic_slice x1, local copies, waits for them, and re-layouts, per_device(): lax.dynamic_slice_in_dim(key_state_rows, (spot ^ p) * head_size, head_siz...  1.61 us
    dynamic_slice x2, local copies, waits for them, and re-layouts, per_device(): lax.dynamic_slice(sent, (first, (spot ^ plane - 1) * width), (count, width))  1.44 us
  transfers between devices with their start and end apart: 17, of which 11 were waited for; matrix products, arithmetic and copies ran while one was open for 8% of the time, Pallas kernels for 0%

profile of v7, /device:TPU:0, one launch (start us, length us, event | category | flops | bytes accessed | tf_op | source)
XLA Modules:
  0.0 58.7 jit_solution(7897702563785052055)
XLA Ops:
  0.0 1.6 %constant_dynamic-slice_fusion.11 = (bf16[256,128]{1,0:T(8,128)(2,1)S(1)}, bf16[256,128]{1,0:T(8,128)(2,1)S(1)}, bf16[256,128]{1,0:T(8,128)(2,1)}, bf16[256,128]{1,0:T(8,128)(2,1)}) fusion(bf16[256,512]{1,0:T(8,128)(2,1)} %param.7, s32[]{:T(128)S(6)} %select_n.82, s32[]{:T(128)S(6)} %select_n.83, s32[]{:T(128)S(6)} %select_n.85, s32[]{:T(128)S(6)} %select_n.84), kind=kLoop, calls=%fused_computation.20 | loop fusion | bytes 524304 | tf_op jit(solution)/shard_map/dynamic_slice | solution.py:302
  1.6 3.9 %collective-permute-start.2 = (bf16[256,128]{1,0:T(8,128)(2,1)}, bf16[256,128]{1,0:T(8,128)(2,1)}, u32[]{:S(2)}, u32[]{:S(2)}) collective-permute-start(bf16[256,128]{1,0:T(8,128)(2,1)} %get-tuple-element.40), channel_id=1, source_target_pairs={{0,6},{2,4},{4,2},{6,0},{8,14},{10,12},{12,10},{14,8},{16,22},{18,... | collective-permute-start | bytes 196616 | tf_op jit(solution)/shard_map/ppermute | solution.py:296
  6.1 1.6 %constant_dynamic-update-slice_fusion.1 = bf16[272,3584]{1,0:T(8,128)(2,1)S(1)} fusion(bf16[256,3584]{1,0:T(8,128)(2,1)} %param.6), kind=kLoop, calls=%fused_computation.2 | loop fusion | bytes 3670016
  8.0 0.7 %constant_dynamic-slice_fusion.4 = bf16[64,896]{1,0:T(8,128)(2,1)} fusion(bf16[272,3584]{1,0:T(8,128)(2,1)S(1)} %constant_dynamic-update-slice_fusion, s32[]{:T(128)S(6)} %select_n.89), kind=kLoop, calls=%fused_computation.13 | loop fusion | bytes 229380 | tf_op jit(solution)/shard_map/dynamic_slice | solution.py:307
  8.7 0.8 %constant_dynamic-slice_fusion.12 = bf16[208,896]{1,0:T(8,128)(2,1)} fusion(bf16[272,3584]{1,0:T(8,128)(2,1)S(1)} %constant_dynamic-update-slice_fusion, s32[]{:T(128)S(6)} %select_n.89), kind=kLoop, calls=%fused_computation.61 | loop fusion | bytes 745476 | tf_op jit(solution)/shard_map/dynamic_slice | solution.py:307
  10.4 0.9 %pad_maximum_fusion = bf16[1024,128]{1,0:T(8,128)(2,1)S(1)} fusion(bf16[256,128]{1,0:T(8,128)(2,1)} %collective-permute-done.2, bf16[256,128]{1,0:T(8,128)(2,1)} %collective-permute-done.1, bf16[256,128]{1,0:T(8,128)(2,1)} %collective-permute-done, bf16[256,128]{1,0:T(8,128)(2,1)S(1)} %get-tuple-element.38), kind=kLoop, calls=%fused_computation | loop fusion | flops 1048576 | bytes 524288 | tf_op jit(solution)/shard_map/concatenate | solution.py:308
  11.3 1.6 %collective-permute-start.3 = (bf16[1024,128]{1,0:T(8,128)(2,1)S(1)}, bf16[1024,128]{1,0:T(8,128)(2,1)S(1)}, u32[]{:S(2)}, u32[]{:S(2)}) collective-permute-start(bf16[1024,128]{1,0:T(8,128)(2,1)S(1)} %pad_maximum_fusion), channel_id=1, source_target_pairs={{0,8},{2,10},{4,12},{6,14},{8,16},{10,18},{12,20},{14,22},{16,24},... | collective-permute-start | bytes 786440 | tf_op jit(solution)/shard_map/ppermute | solution.py:315
  12.9 1.2 %collective-permute-start.5 = (bf16[272,896]{1,0:T(8,128)(2,1)S(1)}, bf16[272,896]{1,0:T(8,128)(2,1)S(1)}, u32[]{:S(2)}, u32[]{:S(2)}) collective-permute-start(bf16[272,896]{1,0:T(8,128)(2,1)S(1)} %get-tuple-element.21), channel_id=1, source_target_pairs={{0,2},{2,0},{4,6},{6,4},{8,10},{10,8},{12,14},{14,12},{16,18},{18,... | collective-permute-start | bytes 1462280 | tf_op jit(solution)/shard_map/ppermute | solution.py:296
  14.2 1.5 %collective-permute-start.6 = (bf16[272,896]{1,0:T(8,128)(2,1)S(1)}, bf16[272,896]{1,0:T(8,128)(2,1)S(1)}, u32[]{:S(2)}, u32[]{:S(2)}) collective-permute-start(bf16[272,896]{1,0:T(8,128)(2,1)S(1)} %get-tuple-element.22), channel_id=1, source_target_pairs={{0,4},{2,6},{4,0},{6,2},{8,12},{10,14},{12,8},{14,10},{16,20},{18,... | collective-permute-start | bytes 1462280 | tf_op jit(solution)/shard_map/ppermute | solution.py:296
  15.7 0.8 %fusion.10 = (s32[31]{0:T(128)S(1)}, s32[31]{0:T(128)S(1)}, s32[31]{0:T(128)S(1)}, s32[31]{0:T(128)S(1)}) fusion(s32[32,31]{1,0:T(8,128)} %param.8, s32[]{:T(128)S(6)} %select_n.94, s32[]{:T(128)S(6)} %select_n.92, s32[]{:T(128)S(6)} %select_n.91, s32[]{:T(128)S(6)} %select_n.93), kind=kLoop, calls=%fused_computation.52 | loop fusion | bytes 1008 | tf_op jit(solution)/shard_map/jit(dynamic_index_in_dim)/squeeze | solution.py:262
  16.6 0.8 %collective-permute-start.7 = (bf16[64,896]{1,0:T(8,128)(2,1)}, bf16[64,896]{1,0:T(8,128)(2,1)S(1)}, u32[]{:S(2)}, u32[]{:S(2)}) collective-permute-start(bf16[64,896]{1,0:T(8,128)(2,1)} %constant_dynamic-slice_fusion.4), channel_id=1, source_target_pairs={{0,6},{2,4},{4,2},{6,0},{8,14},{10,12},{12,10},{14,8},{16,22},{18,... | collective-permute-start | bytes 344072 | tf_op jit(solution)/shard_map/ppermute | solution.py:296
  17.4 2.7 %collective-permute-done.3 = bf16[1024,128]{1,0:T(8,128)(2,1)S(1)} collective-permute-done((bf16[1024,128]{1,0:T(8,128)(2,1)S(1)}, bf16[1024,128]{1,0:T(8,128)(2,1)S(1)}, u32[]{:S(2)}, u32[]{:S(2)}) %collective-permute-start.3) | collective-permute-done | bytes 262176 | tf_op jit(solution)/shard_map/ppermute | solution.py:315
  20.3 7.6 %collective-permute-done.7.refs_4_ = bf16[64,896]{1,0:T(8,128)(2,1)S(1)} collective-permute-done((bf16[64,896]{1,0:T(8,128)(2,1)}, bf16[64,896]{1,0:T(8,128)(2,1)S(1)}, u32[]{:S(2)}, u32[]{:S(2)}) %collective-permute-start.7) | collective-permute-done | bytes 114720 | tf_op jit(solution)/shard_map/ppermute | solution.py:296
  28.3 1.3 %collective-permute-start.12 = (bf16[1024,128]{1,0:T(8,128)(2,1)S(1)}, bf16[1024,128]{1,0:T(8,128)(2,1)S(1)}, u32[]{:S(2)}, u32[]{:S(2)}) collective-permute-start(bf16[1024,128]{1,0:T(8,128)(2,1)S(1)} %collective-permute-done.4), channel_id=1, source_target_pairs={{0,8},{2,10},{4,12},{6,14},{8,16},{10,18},{12,20},{14,22},{16,24},... | collective-permute-start | bytes 786440 | tf_op jit(solution)/shard_map/ppermute | solution.py:315
  29.7 1.6 %collective-permute-start.8 = (bf16[208,896]{1,0:T(8,128)(2,1)}, bf16[208,896]{1,0:T(8,128)(2,1)S(1)}, u32[]{:S(2)}, u32[]{:S(2)}) collective-permute-start(bf16[208,896]{1,0:T(8,128)(2,1)} %constant_dynamic-slice_fusion.12), channel_id=1, source_target_pairs={{0,6},{2,4},{4,2},{6,0},{8,14},{10,12},{12,10},{14,8},{16,22},{18,... | collective-permute-start | bytes 1118216 | tf_op jit(solution)/shard_map/ppermute | solution.py:296
  31.9 4.6 %collective-permute-done.12.refs_7_ = bf16[1024,128]{1,0:T(8,128)(2,1)S(1)} collective-permute-done((bf16[1024,128]{1,0:T(8,128)(2,1)S(1)}, bf16[1024,128]{1,0:T(8,128)(2,1)S(1)}, u32[]{:S(2)}, u32[]{:S(2)}) %collective-permute-start.12) | collective-permute-done | bytes 262176 | tf_op jit(solution)/shard_map/ppermute | solution.py:315
  36.7 1.8 %collective-permute-done.8.refs_5_ = bf16[208,896]{1,0:T(8,128)(2,1)S(1)} collective-permute-done((bf16[208,896]{1,0:T(8,128)(2,1)}, bf16[208,896]{1,0:T(8,128)(2,1)S(1)}, u32[]{:S(2)}, u32[]{:S(2)}) %collective-permute-start.8) | collective-permute-done | bytes 372768 | tf_op jit(solution)/shard_map/ppermute | solution.py:296
  38.4 13.0 %shard_map.64 = (f32[8,128]{1,0:T(8,128)S(1)}, f32[8,128]{1,0:T(8,128)S(1)}, f32[8,128]{1,0:T(8,128)S(1)}, f32[8,128]{1,0:T(8,128)S(1)}) custom-call(s32[157]{0:T(256)S(1)} %pad_add_fusion.refs_0_, bf16[272,896]{1,0:T(8,128)(2,1)S(1)} %get-tuple-element.25.refs_1_, bf16[272,896]{1,0:T(8,128)(2,1)S(1)} %collective-permute-done.5.refs_2_, ...), custom_call_target="tpu_custom_call" | custom-call | tf_op jit(solution)/shard_map/pallas_call | solution.py:203
  51.5 2.1 %collective-permute-start.16 = (f32[8,128]{1,0:T(8,128)S(1)}, f32[8,128]{1,0:T(8,128)S(1)}, u32[]{:S(2)}, u32[]{:S(2)}) collective-permute-start(f32[8,128]{1,0:T(8,128)S(1)} %get-tuple-element.34), channel_id=1, source_target_pairs={{0,6},{2,4},{4,2},{6,0},{8,14},{10,12},{12,10},{14,8},{16,22},{18,... | collective-permute-start | bytes 12296 | tf_op jit(solution)/shard_map/ppermute | solution.py:296
  53.6 1.0 %collective-permute-start.15 = (f32[8,128]{1,0:T(8,128)S(1)}, f32[8,128]{1,0:T(8,128)S(1)}, u32[]{:S(2)}, u32[]{:S(2)}) collective-permute-start(f32[8,128]{1,0:T(8,128)S(1)} %get-tuple-element.33), channel_id=1, source_target_pairs={{0,4},{2,6},{4,0},{6,2},{8,12},{10,14},{12,8},{14,10},{16,20},{18,... | collective-permute-start | bytes 12296 | tf_op jit(solution)/shard_map/ppermute | solution.py:296
  55.0 1.0 %collective-permute-done.16 = f32[8,128]{1,0:T(8,128)S(1)} collective-permute-done((f32[8,128]{1,0:T(8,128)S(1)}, f32[8,128]{1,0:T(8,128)S(1)}, u32[]{:S(2)}, u32[]{:S(2)}) %collective-permute-start.16) | collective-permute-done | bytes 4128 | tf_op jit(solution)/shard_map/ppermute | solution.py:296
  56.0 1.1 %collective-permute-done.15 = f32[8,128]{1,0:T(8,128)S(1)} collective-permute-done((f32[8,128]{1,0:T(8,128)S(1)}, f32[8,128]{1,0:T(8,128)S(1)}, u32[]{:S(2)}, u32[]{:S(2)}) %collective-permute-start.15) | collective-permute-done | bytes 4128 | tf_op jit(solution)/shard_map/ppermute | solution.py:296
  57.2 1.0 %collective-permute-done.14 = f32[8,128]{1,0:T(8,128)S(1)} collective-permute-done((f32[8,128]{1,0:T(8,128)S(1)}, f32[8,128]{1,0:T(8,128)S(1)}, u32[]{:S(2)}, u32[]{:S(2)}) %collective-permute-start.14) | collective-permute-done | bytes 4128 | tf_op jit(solution)/shard_map/ppermute | solution.py:296
  58.1 0.6 slice_add_fusion
  (44 shorter events, 3.7 us)
Async XLA Ops:
  1.6 8.0 %collective-permute-start.2 = (bf16[256,128]{1,0:T(8,128)(2,1)}, bf16[256,128]{1,0:T(8,128)(2,1)}, u32[]{:S(2)}, u32[]{:S(2)}) collective-permute-start(bf16[256,128]{1,0:T(8,128)(2,1)} %get-tuple-element.40), channel_id=1, source_target_pairs={{0,6},{2,4},{4,2},{6,0},{8,14},{10,12},{12,10},{14,8},{16,22},{18,... | collective-permute-start | bytes 196616 | tf_op jit(solution)/shard_map/ppermute | solution.py:296
  5.5 4.6 %collective-permute-start.1 = (bf16[256,128]{1,0:T(8,128)(2,1)}, bf16[256,128]{1,0:T(8,128)(2,1)}, u32[]{:S(2)}, u32[]{:S(2)}) collective-permute-start(bf16[256,128]{1,0:T(8,128)(2,1)} %get-tuple-element.41), channel_id=1, source_target_pairs={{0,4},{2,6},{4,0},{6,2},{8,12},{10,14},{12,8},{14,10},{16,20},{18,... | collective-permute-start | bytes 196616 | tf_op jit(solution)/shard_map/ppermute | solution.py:296
  6.0 4.4 %collective-permute-start = (bf16[256,128]{1,0:T(8,128)(2,1)S(1)}, bf16[256,128]{1,0:T(8,128)(2,1)}, u32[]{:S(2)}, u32[]{:S(2)}) collective-permute-start(bf16[256,128]{1,0:T(8,128)(2,1)S(1)} %get-tuple-element.39), channel_id=1, source_target_pairs={{0,2},{2,0},{4,6},{6,4},{8,10},{10,8},{12,14},{14,12},{16,18},{18,... | collective-permute-start | bytes 196616 | tf_op jit(solution)/shard_map/ppermute | solution.py:296
  6.1 1.6 %copy-start.2 = (s32[4,28,16]{1,2,0:T(8,128)S(1)}, s32[4,28,16]{1,2,0:T(8,128)}, u32[]{:S(2)}) copy-start(s32[4,28,16]{1,2,0:T(8,128)} %param.9) | copy-start | bytes 21508
  11.3 8.9 %collective-permute-start.3 = (bf16[1024,128]{1,0:T(8,128)(2,1)S(1)}, bf16[1024,128]{1,0:T(8,128)(2,1)S(1)}, u32[]{:S(2)}, u32[]{:S(2)}) collective-permute-start(bf16[1024,128]{1,0:T(8,128)(2,1)S(1)} %pad_maximum_fusion), channel_id=1, source_target_pairs={{0,8},{2,10},{4,12},{6,14},{8,16},{10,18},{12,20},{14,22},{16,24},... | collective-permute-start | bytes 786440 | tf_op jit(solution)/shard_map/ppermute | solution.py:315
  12.9 15.0 %collective-permute-start.5 = (bf16[272,896]{1,0:T(8,128)(2,1)S(1)}, bf16[272,896]{1,0:T(8,128)(2,1)S(1)}, u32[]{:S(2)}, u32[]{:S(2)}) collective-permute-start(bf16[272,896]{1,0:T(8,128)(2,1)S(1)} %get-tuple-element.21), channel_id=1, source_target_pairs={{0,2},{2,0},{4,6},{6,4},{8,10},{10,8},{12,14},{14,12},{16,18},{18,... | collective-permute-start | bytes 1462280 | tf_op jit(solution)/shard_map/ppermute | solution.py:296
  14.2 13.9 %collective-permute-start.6 = (bf16[272,896]{1,0:T(8,128)(2,1)S(1)}, bf16[272,896]{1,0:T(8,128)(2,1)S(1)}, u32[]{:S(2)}, u32[]{:S(2)}) collective-permute-start(bf16[272,896]{1,0:T(8,128)(2,1)S(1)} %get-tuple-element.22), channel_id=1, source_target_pairs={{0,4},{2,6},{4,0},{6,2},{8,12},{10,14},{12,8},{14,10},{16,20},{18,... | collective-permute-start | bytes 1462280 | tf_op jit(solution)/shard_map/ppermute | solution.py:296
  16.6 11.3 %collective-permute-start.7 = (bf16[64,896]{1,0:T(8,128)(2,1)}, bf16[64,896]{1,0:T(8,128)(2,1)S(1)}, u32[]{:S(2)}, u32[]{:S(2)}) collective-permute-start(bf16[64,896]{1,0:T(8,128)(2,1)} %constant_dynamic-slice_fusion.4), channel_id=1, source_target_pairs={{0,6},{2,4},{4,2},{6,0},{8,14},{10,12},{12,10},{14,8},{16,22},{18,... | collective-permute-start | bytes 344072 | tf_op jit(solution)/shard_map/ppermute | solution.py:296
  20.2 8.2 %collective-permute-start.4 = (bf16[1024,128]{1,0:T(8,128)(2,1)S(1)}, bf16[1024,128]{1,0:T(8,128)(2,1)S(1)}, u32[]{:S(2)}, u32[]{:S(2)}) collective-permute-start(bf16[1024,128]{1,0:T(8,128)(2,1)S(1)} %collective-permute-done.3), channel_id=1, source_target_pairs={{0,8},{2,10},{4,12},{6,14},{8,16},{10,18},{12,20},{14,22},{16,24},... | collective-permute-start | bytes 786440 | tf_op jit(solution)/shard_map/ppermute | solution.py:315
  20.3 18.1 %copy-start = (bf16[384,128]{1,0:T(8,128)(2,1)S(1)}, bf16[384,128]{1,0:T(8,128)(2,1)}, u32[]{:S(2)}) copy-start(bf16[384,128]{1,0:T(8,128)(2,1)} %refs_10_.1) | copy-start | bytes 294916
  20.3 18.1 %copy-start.1 = (bf16[128,128]{1,0:T(8,128)(2,1)S(1)}, bf16[128,128]{1,0:T(8,128)(2,1)}, u32[]{:S(2)}) copy-start(bf16[128,128]{1,0:T(8,128)(2,1)} %refs_9_.1) | copy-start | bytes 98308
  20.3 16.2 %collective-permute-start.9 = (bf16[1024,128]{1,0:T(8,128)(2,1)S(1)}, bf16[1024,128]{1,0:T(8,128)(2,1)S(1)}, u32[]{:S(2)}, u32[]{:S(2)}) collective-permute-start(bf16[1024,128]{1,0:T(8,128)(2,1)S(1)} %pad_maximum_fusion), channel_id=1, source_target_pairs={{0,1},{1,0},{2,3},{3,2},{4,5},{5,4},{6,7},{7,6},{8,9},{9,8},{10,11... | collective-permute-start | bytes 786440 | tf_op jit(solution)/shard_map/ppermute | solution.py:299
  28.3 8.2 %collective-permute-start.12 = (bf16[1024,128]{1,0:T(8,128)(2,1)S(1)}, bf16[1024,128]{1,0:T(8,128)(2,1)S(1)}, u32[]{:S(2)}, u32[]{:S(2)}) collective-permute-start(bf16[1024,128]{1,0:T(8,128)(2,1)S(1)} %collective-permute-done.4), channel_id=1, source_target_pairs={{0,8},{2,10},{4,12},{6,14},{8,16},{10,18},{12,20},{14,22},{16,24},... | collective-permute-start | bytes 786440 | tf_op jit(solution)/shard_map/ppermute | solution.py:315
  29.7 8.7 %collective-permute-start.8 = (bf16[208,896]{1,0:T(8,128)(2,1)}, bf16[208,896]{1,0:T(8,128)(2,1)S(1)}, u32[]{:S(2)}, u32[]{:S(2)}) collective-permute-start(bf16[208,896]{1,0:T(8,128)(2,1)} %constant_dynamic-slice_fusion.12), channel_id=1, source_target_pairs={{0,6},{2,4},{4,2},{6,0},{8,14},{10,12},{12,10},{14,8},{16,22},{18,... | collective-permute-start | bytes 1118216 | tf_op jit(solution)/shard_map/ppermute | solution.py:296
  31.3 5.3 %collective-permute-start.10 = (bf16[1024,128]{1,0:T(8,128)(2,1)S(1)}, bf16[1024,128]{1,0:T(8,128)(2,1)S(1)}, u32[]{:S(2)}, u32[]{:S(2)}) collective-permute-start(bf16[1024,128]{1,0:T(8,128)(2,1)S(1)} %collective-permute-done.3), channel_id=1, source_target_pairs={{0,1},{1,0},{2,3},{3,2},{4,5},{5,4},{6,7},{7,6},{8,9},{9,8},{10,11... | collective-permute-start | bytes 786440 | tf_op jit(solution)/shard_map/ppermute | solution.py:299
  31.3 5.3 %collective-permute-start.11 = (bf16[1024,128]{1,0:T(8,128)(2,1)S(1)}, bf16[1024,128]{1,0:T(8,128)(2,1)S(1)}, u32[]{:S(2)}, u32[]{:S(2)}) collective-permute-start(bf16[1024,128]{1,0:T(8,128)(2,1)S(1)} %collective-permute-done.4), channel_id=1, source_target_pairs={{0,1},{1,0},{2,3},{3,2},{4,5},{5,4},{6,7},{7,6},{8,9},{9,8},{10,11... | collective-permute-start | bytes 786440 | tf_op jit(solution)/shard_map/ppermute | solution.py:299
  36.5 1.9 %collective-permute-start.13 = (bf16[1024,128]{1,0:T(8,128)(2,1)S(1)}, bf16[1024,128]{1,0:T(8,128)(2,1)S(1)}, u32[]{:S(2)}, u32[]{:S(2)}) collective-permute-start(bf16[1024,128]{1,0:T(8,128)(2,1)S(1)} %collective-permute-done.12.refs_7_), channel_id=1, source_target_pairs={{0,1},{1,0},{2,3},{3,2},{4,5},{5,4},{6,7},{7,6},{8,9},{9,8},{10,11... | collective-permute-start | bytes 786440 | tf_op jit(solution)/shard_map/ppermute | solution.py:299
  51.5 4.6 %collective-permute-start.16 = (f32[8,128]{1,0:T(8,128)S(1)}, f32[8,128]{1,0:T(8,128)S(1)}, u32[]{:S(2)}, u32[]{:S(2)}) collective-permute-start(f32[8,128]{1,0:T(8,128)S(1)} %get-tuple-element.34), channel_id=1, source_target_pairs={{0,6},{2,4},{4,2},{6,0},{8,14},{10,12},{12,10},{14,8},{16,22},{18,... | collective-permute-start | bytes 12296 | tf_op jit(solution)/shard_map/ppermute | solution.py:296
  53.6 3.6 %collective-permute-start.15 = (f32[8,128]{1,0:T(8,128)S(1)}, f32[8,128]{1,0:T(8,128)S(1)}, u32[]{:S(2)}, u32[]{:S(2)}) collective-permute-start(f32[8,128]{1,0:T(8,128)S(1)} %get-tuple-element.33), channel_id=1, source_target_pairs={{0,4},{2,6},{4,0},{6,2},{8,12},{10,14},{12,8},{14,10},{16,20},{18,... | collective-permute-start | bytes 12296 | tf_op jit(solution)/shard_map/ppermute | solution.py:296
  54.5 3.6 %collective-permute-start.14 = (f32[8,128]{1,0:T(8,128)S(1)}, f32[8,128]{1,0:T(8,128)S(1)}, u32[]{:S(2)}, u32[]{:S(2)}) collective-permute-start(f32[8,128]{1,0:T(8,128)S(1)} %get-tuple-element.32), channel_id=1, source_target_pairs={{0,2},{2,0},{4,6},{6,4},{8,10},{10,8},{12,14},{14,12},{16,18},{18,... | collective-permute-start | bytes 12296 | tf_op jit(solution)/shard_map/ppermute | solution.py:296

commit v8 on v7

--- a/solution.py
+++ b/solution.py
@@ -152,11 +152,14 @@
     def combine_step(ph, carry):
         for t in range(pairs):
             combine(ph, t)
-        head_step(jnp.minimum(ph + 1, n_piece * heads - 1), 0)
+        head_step(ph + 1, 0)
         return carry
 
     head_step(0, 0)
-    lax.fori_loop(0, n_piece * heads, combine_step, 0, unroll=28)
+    last = n_piece * heads - 1
+    lax.fori_loop(0, last, combine_step, 0, unroll=last)
+    for t in range(pairs):
+        combine(last, t)
 
     for copy in w_copies:
         copy.wait()

time: 59 us -> 58.8 us (level)
  no operation moved by 1% of the time
where the time goes in v8:
time: 58.8 us; the launch traced here: 58.6 us
  waiting for transfers between devices  21 us (36%)
  starting transfers between devices  16.7 us (28%)
  Pallas kernels  12.9 us (22%)
  local copies, waits for them, and re-layouts  6.19 us (11%)
  other arithmetic  1.64 us (3%)
    ppermute x10, waiting for transfers between devices, flipped(): lax.ppermute(x, 'ctx', [(i, i ^ p) for i in range(n_ctx)])  13.4 us
    ppermute x10, starting transfers between devices, flipped(): lax.ppermute(x, 'ctx', [(i, i ^ p) for i in range(n_ctx)])  13.1 us
    pallas_call x1, Pallas kernels, gate_call(): pl.pallas_call(functools.partial(gate_kernel, dims), out_shape=[jax.Shape...  12.9 us
    ppermute x3, waiting for transfers between devices, per_device(): lax.ppermute(steps[i], 'ctx', [(j, (j + plane) % n_ctx) for j in range(n_...  7.59 us
    ppermute x3, starting transfers between devices, per_device(): lax.ppermute(steps[i], 'ctx', [(j, (j + plane) % n_ctx) for j in range(n_...  2.97 us
    unnamed x13, local copies, waits for them, and re-layouts  1.81 us
    dynamic_slice x1, local copies, waits for them, and re-layouts, per_device(): lax.dynamic_slice_in_dim(key_state_rows, (spot ^ p) * head_size, head_siz...  1.61 us
    dynamic_slice x2, local copies, waits for them, and re-layouts, per_device(): lax.dynamic_slice(sent, (first, (spot ^ plane - 1) * width), (count, width))  1.44 us
  transfers between devices with their start and end apart: 17, of which 11 were waited for; matrix products, arithmetic and copies ran while one was open for 8% of the time, Pallas kernels for 0%

profile of v8, /device:TPU:0, one launch (start us, length us, event | category | flops | bytes accessed | tf_op | source)
XLA Modules:
  0.0 58.6 jit_solution(9251176286863018281)
XLA Ops:
  0.0 1.6 %constant_dynamic-slice_fusion.11 = (bf16[256,128]{1,0:T(8,128)(2,1)S(1)}, bf16[256,128]{1,0:T(8,128)(2,1)S(1)}, bf16[256,128]{1,0:T(8,128)(2,1)}, bf16[256,128]{1,0:T(8,128)(2,1)}) fusion(bf16[256,512]{1,0:T(8,128)(2,1)} %param.7, s32[]{:T(128)S(6)} %select_n.82, s32[]{:T(128)S(6)} %select_n.83, s32[]{:T(128)S(6)} %select_n.85, s32[]{:T(128)S(6)} %select_n.84), kind=kLoop, calls=%fused_computation.20 | loop fusion | bytes 524304 | tf_op jit(solution)/shard_map/dynamic_slice | solution.py:305
  1.6 3.9 %collective-permute-start.2 = (bf16[256,128]{1,0:T(8,128)(2,1)}, bf16[256,128]{1,0:T(8,128)(2,1)}, u32[]{:S(2)}, u32[]{:S(2)}) collective-permute-start(bf16[256,128]{1,0:T(8,128)(2,1)} %get-tuple-element.40), channel_id=1, source_target_pairs={{0,6},{2,4},{4,2},{6,0},{8,14},{10,12},{12,10},{14,8},{16,22},{18,... | collective-permute-start | bytes 196616 | tf_op jit(solution)/shard_map/ppermute | solution.py:299
  6.1 1.6 %constant_dynamic-update-slice_fusion.1 = bf16[272,3584]{1,0:T(8,128)(2,1)S(1)} fusion(bf16[256,3584]{1,0:T(8,128)(2,1)} %param.6), kind=kLoop, calls=%fused_computation.2 | loop fusion | bytes 3670016
  8.0 0.7 %constant_dynamic-slice_fusion.4 = bf16[64,896]{1,0:T(8,128)(2,1)} fusion(bf16[272,3584]{1,0:T(8,128)(2,1)S(1)} %constant_dynamic-update-slice_fusion, s32[]{:T(128)S(6)} %select_n.89), kind=kLoop, calls=%fused_computation.13 | loop fusion | bytes 229380 | tf_op jit(solution)/shard_map/dynamic_slice | solution.py:310
  8.7 0.8 %constant_dynamic-slice_fusion.12 = bf16[208,896]{1,0:T(8,128)(2,1)} fusion(bf16[272,3584]{1,0:T(8,128)(2,1)S(1)} %constant_dynamic-update-slice_fusion, s32[]{:T(128)S(6)} %select_n.89), kind=kLoop, calls=%fused_computation.61 | loop fusion | bytes 745476 | tf_op jit(solution)/shard_map/dynamic_slice | solution.py:310
  10.4 0.9 %pad_maximum_fusion = bf16[1024,128]{1,0:T(8,128)(2,1)S(1)} fusion(bf16[256,128]{1,0:T(8,128)(2,1)} %collective-permute-done.2, bf16[256,128]{1,0:T(8,128)(2,1)} %collective-permute-done.1, bf16[256,128]{1,0:T(8,128)(2,1)} %collective-permute-done, bf16[256,128]{1,0:T(8,128)(2,1)S(1)} %get-tuple-element.38), kind=kLoop, calls=%fused_computation | loop fusion | flops 1048576 | bytes 524288 | tf_op jit(solution)/shard_map/concatenate | solution.py:311
  11.3 1.6 %collective-permute-start.3 = (bf16[1024,128]{1,0:T(8,128)(2,1)S(1)}, bf16[1024,128]{1,0:T(8,128)(2,1)S(1)}, u32[]{:S(2)}, u32[]{:S(2)}) collective-permute-start(bf16[1024,128]{1,0:T(8,128)(2,1)S(1)} %pad_maximum_fusion), channel_id=1, source_target_pairs={{0,8},{2,10},{4,12},{6,14},{8,16},{10,18},{12,20},{14,22},{16,24},... | collective-permute-start | bytes 786440 | tf_op jit(solution)/shard_map/ppermute | solution.py:318
  12.9 1.2 %collective-permute-start.5 = (bf16[272,896]{1,0:T(8,128)(2,1)S(1)}, bf16[272,896]{1,0:T(8,128)(2,1)S(1)}, u32[]{:S(2)}, u32[]{:S(2)}) collective-permute-start(bf16[272,896]{1,0:T(8,128)(2,1)S(1)} %get-tuple-element.21), channel_id=1, source_target_pairs={{0,2},{2,0},{4,6},{6,4},{8,10},{10,8},{12,14},{14,12},{16,18},{18,... | collective-permute-start | bytes 1462280 | tf_op jit(solution)/shard_map/ppermute | solution.py:299
  14.2 1.5 %collective-permute-start.6 = (bf16[272,896]{1,0:T(8,128)(2,1)S(1)}, bf16[272,896]{1,0:T(8,128)(2,1)S(1)}, u32[]{:S(2)}, u32[]{:S(2)}) collective-permute-start(bf16[272,896]{1,0:T(8,128)(2,1)S(1)} %get-tuple-element.22), channel_id=1, source_target_pairs={{0,4},{2,6},{4,0},{6,2},{8,12},{10,14},{12,8},{14,10},{16,20},{18,... | collective-permute-start | bytes 1462280 | tf_op jit(solution)/shard_map/ppermute | solution.py:299
  15.7 0.8 %fusion.10 = (s32[31]{0:T(128)S(1)}, s32[31]{0:T(128)S(1)}, s32[31]{0:T(128)S(1)}, s32[31]{0:T(128)S(1)}) fusion(s32[32,31]{1,0:T(8,128)} %param.8, s32[]{:T(128)S(6)} %select_n.94, s32[]{:T(128)S(6)} %select_n.92, s32[]{:T(128)S(6)} %select_n.91, s32[]{:T(128)S(6)} %select_n.93), kind=kLoop, calls=%fused_computation.52 | loop fusion | bytes 1008 | tf_op jit(solution)/shard_map/jit(dynamic_index_in_dim)/squeeze | solution.py:265
  16.6 0.8 %collective-permute-start.7 = (bf16[64,896]{1,0:T(8,128)(2,1)}, bf16[64,896]{1,0:T(8,128)(2,1)S(1)}, u32[]{:S(2)}, u32[]{:S(2)}) collective-permute-start(bf16[64,896]{1,0:T(8,128)(2,1)} %constant_dynamic-slice_fusion.4), channel_id=1, source_target_pairs={{0,6},{2,4},{4,2},{6,0},{8,14},{10,12},{12,10},{14,8},{16,22},{18,... | collective-permute-start | bytes 344072 | tf_op jit(solution)/shard_map/ppermute | solution.py:299
  17.4 2.7 %collective-permute-done.3 = bf16[1024,128]{1,0:T(8,128)(2,1)S(1)} collective-permute-done((bf16[1024,128]{1,0:T(8,128)(2,1)S(1)}, bf16[1024,128]{1,0:T(8,128)(2,1)S(1)}, u32[]{:S(2)}, u32[]{:S(2)}) %collective-permute-start.3) | collective-permute-done | bytes 262176 | tf_op jit(solution)/shard_map/ppermute | solution.py:318
  20.3 7.6 %collective-permute-done.7.refs_4_ = bf16[64,896]{1,0:T(8,128)(2,1)S(1)} collective-permute-done((bf16[64,896]{1,0:T(8,128)(2,1)}, bf16[64,896]{1,0:T(8,128)(2,1)S(1)}, u32[]{:S(2)}, u32[]{:S(2)}) %collective-permute-start.7) | collective-permute-done | bytes 114720 | tf_op jit(solution)/shard_map/ppermute | solution.py:299
  28.3 1.3 %collective-permute-start.12 = (bf16[1024,128]{1,0:T(8,128)(2,1)S(1)}, bf16[1024,128]{1,0:T(8,128)(2,1)S(1)}, u32[]{:S(2)}, u32[]{:S(2)}) collective-permute-start(bf16[1024,128]{1,0:T(8,128)(2,1)S(1)} %collective-permute-done.4), channel_id=1, source_target_pairs={{0,8},{2,10},{4,12},{6,14},{8,16},{10,18},{12,20},{14,22},{16,24},... | collective-permute-start | bytes 786440 | tf_op jit(solution)/shard_map/ppermute | solution.py:318
  29.7 1.6 %collective-permute-start.8 = (bf16[208,896]{1,0:T(8,128)(2,1)}, bf16[208,896]{1,0:T(8,128)(2,1)S(1)}, u32[]{:S(2)}, u32[]{:S(2)}) collective-permute-start(bf16[208,896]{1,0:T(8,128)(2,1)} %constant_dynamic-slice_fusion.12), channel_id=1, source_target_pairs={{0,6},{2,4},{4,2},{6,0},{8,14},{10,12},{12,10},{14,8},{16,22},{18,... | collective-permute-start | bytes 1118216 | tf_op jit(solution)/shard_map/ppermute | solution.py:299
  31.9 4.6 %collective-permute-done.12.refs_7_ = bf16[1024,128]{1,0:T(8,128)(2,1)S(1)} collective-permute-done((bf16[1024,128]{1,0:T(8,128)(2,1)S(1)}, bf16[1024,128]{1,0:T(8,128)(2,1)S(1)}, u32[]{:S(2)}, u32[]{:S(2)}) %collective-permute-start.12) | collective-permute-done | bytes 262176 | tf_op jit(solution)/shard_map/ppermute | solution.py:318
  36.7 1.8 %collective-permute-done.8.refs_5_ = bf16[208,896]{1,0:T(8,128)(2,1)S(1)} collective-permute-done((bf16[208,896]{1,0:T(8,128)(2,1)}, bf16[208,896]{1,0:T(8,128)(2,1)S(1)}, u32[]{:S(2)}, u32[]{:S(2)}) %collective-permute-start.8) | collective-permute-done | bytes 372768 | tf_op jit(solution)/shard_map/ppermute | solution.py:299
  38.4 12.9 %shard_map.64 = (f32[8,128]{1,0:T(8,128)S(1)}, f32[8,128]{1,0:T(8,128)S(1)}, f32[8,128]{1,0:T(8,128)S(1)}, f32[8,128]{1,0:T(8,128)S(1)}) custom-call(s32[157]{0:T(256)S(1)} %pad_add_fusion.refs_0_, bf16[272,896]{1,0:T(8,128)(2,1)S(1)} %get-tuple-element.25.refs_1_, bf16[272,896]{1,0:T(8,128)(2,1)S(1)} %collective-permute-done.5.refs_2_, ...), custom_call_target="tpu_custom_call" | custom-call | tf_op jit(solution)/shard_map/pallas_call | solution.py:206
  51.3 2.1 %collective-permute-start.16 = (f32[8,128]{1,0:T(8,128)S(1)}, f32[8,128]{1,0:T(8,128)S(1)}, u32[]{:S(2)}, u32[]{:S(2)}) collective-permute-start(f32[8,128]{1,0:T(8,128)S(1)} %get-tuple-element.34), channel_id=1, source_target_pairs={{0,6},{2,4},{4,2},{6,0},{8,14},{10,12},{12,10},{14,8},{16,22},{18,... | collective-permute-start | bytes 12296 | tf_op jit(solution)/shard_map/ppermute | solution.py:299
  53.4 1.0 %collective-permute-start.15 = (f32[8,128]{1,0:T(8,128)S(1)}, f32[8,128]{1,0:T(8,128)S(1)}, u32[]{:S(2)}, u32[]{:S(2)}) collective-permute-start(f32[8,128]{1,0:T(8,128)S(1)} %get-tuple-element.33), channel_id=1, source_target_pairs={{0,4},{2,6},{4,0},{6,2},{8,12},{10,14},{12,8},{14,10},{16,20},{18,... | collective-permute-start | bytes 12296 | tf_op jit(solution)/shard_map/ppermute | solution.py:299
  54.9 1.0 %collective-permute-done.16 = f32[8,128]{1,0:T(8,128)S(1)} collective-permute-done((f32[8,128]{1,0:T(8,128)S(1)}, f32[8,128]{1,0:T(8,128)S(1)}, u32[]{:S(2)}, u32[]{:S(2)}) %collective-permute-start.16) | collective-permute-done | bytes 4128 | tf_op jit(solution)/shard_map/ppermute | solution.py:299
  55.9 1.1 %collective-permute-done.15 = f32[8,128]{1,0:T(8,128)S(1)} collective-permute-done((f32[8,128]{1,0:T(8,128)S(1)}, f32[8,128]{1,0:T(8,128)S(1)}, u32[]{:S(2)}, u32[]{:S(2)}) %collective-permute-start.15) | collective-permute-done | bytes 4128 | tf_op jit(solution)/shard_map/ppermute | solution.py:299
  57.0 1.0 %collective-permute-done.14 = f32[8,128]{1,0:T(8,128)S(1)} collective-permute-done((f32[8,128]{1,0:T(8,128)S(1)}, f32[8,128]{1,0:T(8,128)S(1)}, u32[]{:S(2)}, u32[]{:S(2)}) %collective-permute-start.14) | collective-permute-done | bytes 4128 | tf_op jit(solution)/shard_map/ppermute | solution.py:299
  58.0 0.6 slice_add_fusion
  (44 shorter events, 3.7 us)
Async XLA Ops:
  1.6 8.0 %collective-permute-start.2 = (bf16[256,128]{1,0:T(8,128)(2,1)}, bf16[256,128]{1,0:T(8,128)(2,1)}, u32[]{:S(2)}, u32[]{:S(2)}) collective-permute-start(bf16[256,128]{1,0:T(8,128)(2,1)} %get-tuple-element.40), channel_id=1, source_target_pairs={{0,6},{2,4},{4,2},{6,0},{8,14},{10,12},{12,10},{14,8},{16,22},{18,... | collective-permute-start | bytes 196616 | tf_op jit(solution)/shard_map/ppermute | solution.py:299
  5.5 4.6 %collective-permute-start.1 = (bf16[256,128]{1,0:T(8,128)(2,1)}, bf16[256,128]{1,0:T(8,128)(2,1)}, u32[]{:S(2)}, u32[]{:S(2)}) collective-permute-start(bf16[256,128]{1,0:T(8,128)(2,1)} %get-tuple-element.41), channel_id=1, source_target_pairs={{0,4},{2,6},{4,0},{6,2},{8,12},{10,14},{12,8},{14,10},{16,20},{18,... | collective-permute-start | bytes 196616 | tf_op jit(solution)/shard_map/ppermute | solution.py:299
  6.0 4.4 %collective-permute-start = (bf16[256,128]{1,0:T(8,128)(2,1)S(1)}, bf16[256,128]{1,0:T(8,128)(2,1)}, u32[]{:S(2)}, u32[]{:S(2)}) collective-permute-start(bf16[256,128]{1,0:T(8,128)(2,1)S(1)} %get-tuple-element.39), channel_id=1, source_target_pairs={{0,2},{2,0},{4,6},{6,4},{8,10},{10,8},{12,14},{14,12},{16,18},{18,... | collective-permute-start | bytes 196616 | tf_op jit(solution)/shard_map/ppermute | solution.py:299
  6.1 1.6 %copy-start.2 = (s32[4,28,16]{1,2,0:T(8,128)S(1)}, s32[4,28,16]{1,2,0:T(8,128)}, u32[]{:S(2)}) copy-start(s32[4,28,16]{1,2,0:T(8,128)} %param.9) | copy-start | bytes 21508
  11.3 8.9 %collective-permute-start.3 = (bf16[1024,128]{1,0:T(8,128)(2,1)S(1)}, bf16[1024,128]{1,0:T(8,128)(2,1)S(1)}, u32[]{:S(2)}, u32[]{:S(2)}) collective-permute-start(bf16[1024,128]{1,0:T(8,128)(2,1)S(1)} %pad_maximum_fusion), channel_id=1, source_target_pairs={{0,8},{2,10},{4,12},{6,14},{8,16},{10,18},{12,20},{14,22},{16,24},... | collective-permute-start | bytes 786440 | tf_op jit(solution)/shard_map/ppermute | solution.py:318
  12.9 15.0 %collective-permute-start.5 = (bf16[272,896]{1,0:T(8,128)(2,1)S(1)}, bf16[272,896]{1,0:T(8,128)(2,1)S(1)}, u32[]{:S(2)}, u32[]{:S(2)}) collective-permute-start(bf16[272,896]{1,0:T(8,128)(2,1)S(1)} %get-tuple-element.21), channel_id=1, source_target_pairs={{0,2},{2,0},{4,6},{6,4},{8,10},{10,8},{12,14},{14,12},{16,18},{18,... | collective-permute-start | bytes 1462280 | tf_op jit(solution)/shard_map/ppermute | solution.py:299
  14.2 13.9 %collective-permute-start.6 = (bf16[272,896]{1,0:T(8,128)(2,1)S(1)}, bf16[272,896]{1,0:T(8,128)(2,1)S(1)}, u32[]{:S(2)}, u32[]{:S(2)}) collective-permute-start(bf16[272,896]{1,0:T(8,128)(2,1)S(1)} %get-tuple-element.22), channel_id=1, source_target_pairs={{0,4},{2,6},{4,0},{6,2},{8,12},{10,14},{12,8},{14,10},{16,20},{18,... | collective-permute-start | bytes 1462280 | tf_op jit(solution)/shard_map/ppermute | solution.py:299
  16.6 11.3 %collective-permute-start.7 = (bf16[64,896]{1,0:T(8,128)(2,1)}, bf16[64,896]{1,0:T(8,128)(2,1)S(1)}, u32[]{:S(2)}, u32[]{:S(2)}) collective-permute-start(bf16[64,896]{1,0:T(8,128)(2,1)} %constant_dynamic-slice_fusion.4), channel_id=1, source_target_pairs={{0,6},{2,4},{4,2},{6,0},{8,14},{10,12},{12,10},{14,8},{16,22},{18,... | collective-permute-start | bytes 344072 | tf_op jit(solution)/shard_map/ppermute | solution.py:299
  20.2 8.2 %collective-permute-start.4 = (bf16[1024,128]{1,0:T(8,128)(2,1)S(1)}, bf16[1024,128]{1,0:T(8,128)(2,1)S(1)}, u32[]{:S(2)}, u32[]{:S(2)}) collective-permute-start(bf16[1024,128]{1,0:T(8,128)(2,1)S(1)} %collective-permute-done.3), channel_id=1, source_target_pairs={{0,8},{2,10},{4,12},{6,14},{8,16},{10,18},{12,20},{14,22},{16,24},... | collective-permute-start | bytes 786440 | tf_op jit(solution)/shard_map/ppermute | solution.py:318
  20.3 18.1 %copy-start = (bf16[384,128]{1,0:T(8,128)(2,1)S(1)}, bf16[384,128]{1,0:T(8,128)(2,1)}, u32[]{:S(2)}) copy-start(bf16[384,128]{1,0:T(8,128)(2,1)} %refs_10_.1) | copy-start | bytes 294916
  20.3 18.1 %copy-start.1 = (bf16[128,128]{1,0:T(8,128)(2,1)S(1)}, bf16[128,128]{1,0:T(8,128)(2,1)}, u32[]{:S(2)}) copy-start(bf16[128,128]{1,0:T(8,128)(2,1)} %refs_9_.1) | copy-start | bytes 98308
  20.3 16.2 %collective-permute-start.9 = (bf16[1024,128]{1,0:T(8,128)(2,1)S(1)}, bf16[1024,128]{1,0:T(8,128)(2,1)S(1)}, u32[]{:S(2)}, u32[]{:S(2)}) collective-permute-start(bf16[1024,128]{1,0:T(8,128)(2,1)S(1)} %pad_maximum_fusion), channel_id=1, source_target_pairs={{0,1},{1,0},{2,3},{3,2},{4,5},{5,4},{6,7},{7,6},{8,9},{9,8},{10,11... | collective-permute-start | bytes 786440 | tf_op jit(solution)/shard_map/ppermute | solution.py:302
  28.3 8.2 %collective-permute-start.12 = (bf16[1024,128]{1,0:T(8,128)(2,1)S(1)}, bf16[1024,128]{1,0:T(8,128)(2,1)S(1)}, u32[]{:S(2)}, u32[]{:S(2)}) collective-permute-start(bf16[1024,128]{1,0:T(8,128)(2,1)S(1)} %collective-permute-done.4), channel_id=1, source_target_pairs={{0,8},{2,10},{4,12},{6,14},{8,16},{10,18},{12,20},{14,22},{16,24},... | collective-permute-start | bytes 786440 | tf_op jit(solution)/shard_map/ppermute | solution.py:318
  29.7 8.7 %collective-permute-start.8 = (bf16[208,896]{1,0:T(8,128)(2,1)}, bf16[208,896]{1,0:T(8,128)(2,1)S(1)}, u32[]{:S(2)}, u32[]{:S(2)}) collective-permute-start(bf16[208,896]{1,0:T(8,128)(2,1)} %constant_dynamic-slice_fusion.12), channel_id=1, source_target_pairs={{0,6},{2,4},{4,2},{6,0},{8,14},{10,12},{12,10},{14,8},{16,22},{18,... | collective-permute-start | bytes 1118216 | tf_op jit(solution)/shard_map/ppermute | solution.py:299
  31.3 5.3 %collective-permute-start.10 = (bf16[1024,128]{1,0:T(8,128)(2,1)S(1)}, bf16[1024,128]{1,0:T(8,128)(2,1)S(1)}, u32[]{:S(2)}, u32[]{:S(2)}) collective-permute-start(bf16[1024,128]{1,0:T(8,128)(2,1)S(1)} %collective-permute-done.3), channel_id=1, source_target_pairs={{0,1},{1,0},{2,3},{3,2},{4,5},{5,4},{6,7},{7,6},{8,9},{9,8},{10,11... | collective-permute-start | bytes 786440 | tf_op jit(solution)/shard_map/ppermute | solution.py:302
  31.3 5.3 %collective-permute-start.11 = (bf16[1024,128]{1,0:T(8,128)(2,1)S(1)}, bf16[1024,128]{1,0:T(8,128)(2,1)S(1)}, u32[]{:S(2)}, u32[]{:S(2)}) collective-permute-start(bf16[1024,128]{1,0:T(8,128)(2,1)S(1)} %collective-permute-done.4), channel_id=1, source_target_pairs={{0,1},{1,0},{2,3},{3,2},{4,5},{5,4},{6,7},{7,6},{8,9},{9,8},{10,11... | collective-permute-start | bytes 786440 | tf_op jit(solution)/shard_map/ppermute | solution.py:302
  36.5 1.9 %collective-permute-start.13 = (bf16[1024,128]{1,0:T(8,128)(2,1)S(1)}, bf16[1024,128]{1,0:T(8,128)(2,1)S(1)}, u32[]{:S(2)}, u32[]{:S(2)}) collective-permute-start(bf16[1024,128]{1,0:T(8,128)(2,1)S(1)} %collective-permute-done.12.refs_7_), channel_id=1, source_target_pairs={{0,1},{1,0},{2,3},{3,2},{4,5},{5,4},{6,7},{7,6},{8,9},{9,8},{10,11... | collective-permute-start | bytes 786440 | tf_op jit(solution)/shard_map/ppermute | solution.py:302
  51.3 4.6 %collective-permute-start.16 = (f32[8,128]{1,0:T(8,128)S(1)}, f32[8,128]{1,0:T(8,128)S(1)}, u32[]{:S(2)}, u32[]{:S(2)}) collective-permute-start(f32[8,128]{1,0:T(8,128)S(1)} %get-tuple-element.34), channel_id=1, source_target_pairs={{0,6},{2,4},{4,2},{6,0},{8,14},{10,12},{12,10},{14,8},{16,22},{18,... | collective-permute-start | bytes 12296 | tf_op jit(solution)/shard_map/ppermute | solution.py:299
  53.4 3.6 %collective-permute-start.15 = (f32[8,128]{1,0:T(8,128)S(1)}, f32[8,128]{1,0:T(8,128)S(1)}, u32[]{:S(2)}, u32[]{:S(2)}) collective-permute-start(f32[8,128]{1,0:T(8,128)S(1)} %get-tuple-element.33), channel_id=1, source_target_pairs={{0,4},{2,6},{4,0},{6,2},{8,12},{10,14},{12,8},{14,10},{16,20},{18,... | collective-permute-start | bytes 12296 | tf_op jit(solution)/shard_map/ppermute | solution.py:299
  54.4 3.6 %collective-permute-start.14 = (f32[8,128]{1,0:T(8,128)S(1)}, f32[8,128]{1,0:T(8,128)S(1)}, u32[]{:S(2)}, u32[]{:S(2)}) collective-permute-start(f32[8,128]{1,0:T(8,128)S(1)} %get-tuple-element.32), channel_id=1, source_target_pairs={{0,2},{2,0},{4,6},{6,4},{8,10},{10,8},{12,14},{14,12},{16,18},{18,... | collective-permute-start | bytes 12296 | tf_op jit(solution)/shard_map/ppermute | solution.py:299
